TPU v7x, 32 devices: a whole 2x2x4 slice. The times are simulated.
32 devices in a mesh: dp: 16 (over z, x, core), mp: 2 (over y).
Axes of the slice: x: 2, y: 2, z: 4, core: 2. Of those that a mesh axis runs over, the one named last changes fastest.
Arguments:
- hidden_in: bfloat16 [8192, 768], P('dp'), may hold values from -6 to 6
- norm1_gain: float32 [768], replicated, may hold values from 0.5 to 1.5
- w_query: bfloat16 [768, 768], P(None, 'mp'), may hold values from -0.3125 to 0.3125
- w_key: bfloat16 [768, 768], P(None, 'mp'), may hold values from -0.21875 to 0.21875
- w_value: bfloat16 [768, 768], P(None, 'mp'), may hold values from -0.21875 to 0.21875
- w_output: bfloat16 [768, 768], P('mp'), may hold values from -1.25 to 1.25
- bias_table: float32 [32, 12], P(None, 'mp'), may hold values from -4 to 4
- bucket_ids: int32 [512, 512], replicated, may hold values from 0 to 31, as said below
- norm2_gain: float32 [768], replicated, may hold values from 0.5 to 1.5
- router: float32 [768, 16], replicated, may hold values from -0.109375 to 0.109375
- w_in: bfloat16 [16, 768, 3072], P('dp', None, 'mp'), may hold values from -0.21875 to 0.21875
- w_out: bfloat16 [16, 3072, 768], P('dp', 'mp'), may hold values from -1.75 to 1.75
- expert_ids: int32 [8192], P('dp'), may hold values from 0 to 15, as said below
- slot_ids: int32 [8192], P('dp'), may hold values from 0 to 39, as said below
- out_grad: bfloat16 [8192, 768], P('dp'), may hold values from -6 to 6
Outputs:
- hidden_out: bfloat16 [8192, 768], P('dp')
- grad_hidden_in: float32 [8192, 768], P('dp')
- grad_norm1_gain: float32 [768], replicated
- grad_w_query: float32 [768, 768], P(None, 'mp')
- grad_w_key: float32 [768, 768], P(None, 'mp')
- grad_w_value: float32 [768, 768], P(None, 'mp')
- grad_w_output: float32 [768, 768], P('mp')
- grad_bias_table: float32 [32, 12], P(None, 'mp')
- grad_norm2_gain: float32 [768], replicated
- grad_router: float32 [768, 16], replicated
- grad_w_in: float32 [16, 768, 3072], P('dp', None, 'mp')
- grad_w_out: float32 [16, 3072, 768], P('dp', 'mp')
Inputs may be any that keep to these rules, and one draw needn't show every extreme that they name: `expert_ids`: among the 512 tokens of one device, no expert is named by more than 40 tokens and some expert by exactly 40; one expert is named by exactly 40 tokens of every device; every expert is named somewhere. `slot_ids`: tokens of one device that name the same expert have distinct slots. bucket_ids[i, j] depends only on j - i; keys at or before the query take the lower half of the buckets and later keys the upper half, and within each half the bucket does not fall as the distance grows.
All inputs are finite; a program needn't handle non-finite values.
Results may differ from a plain program's by a relative error of at most 0.018.
Values may be sent and summed in bfloat16 or wider, within the bound.
No kernel may reach another device: no remote copies, remote signals or barrier semaphores. Data moves between devices by JAX's collectives and lax.ppermute only.
A program may use at most 128 MiB of HBM per device.

v0:
```python
import functools

import jax
import jax.numpy as jnp
from jax import lax
from jax.experimental import pallas as pl
from jax.experimental.pallas import tpu as pltpu
from jax.sharding import PartitionSpec as P

epsilon = 1e-06
bf16 = jnp.bfloat16
f32 = jnp.float32
vmem_bytes = 62 * 1024 * 1024
gelu_scale = 0.7978845608028654
gelu_cubic = 0.044715


def dot(left, right):
    return jnp.dot(left, right, preferred_element_type=f32)


def contract_last(left, right):
    return lax.dot_general(left, right, (((1,), (1,)), ((), ())), preferred_element_type=f32)


def contract_rows(left, right, precision=None):
    return lax.dot_general(
        left, right, (((0,), (0,)), ((), ())), preferred_element_type=f32, precision=precision
    )


def whole(shape):
    return pl.BlockSpec(shape, lambda *_: (0,) * len(shape))


def scalars():
    return pl.BlockSpec(memory_space=pltpu.SMEM)


def params():
    return pltpu.CompilerParams(vmem_limit_bytes=vmem_bytes)


def cost(flops, moved):
    return pl.CostEstimate(flops=flops, bytes_accessed=moved, transcendentals=0)


def attend_kernel(
    x_ref, gain_ref, wq_ref, wk_ref, wv_ref, table_ref, first_ref, last_ref,
    o_ref, q_ref, k_ref, v_ref, p_ref, ids_ref, n_ref, bias_ref,
):
    pair = pl.program_id(0)
    length = x_ref.shape[0]
    buckets = table_ref.shape[0]
    half = o_ref.shape[1] // 2
    scale = half ** (-0.5)
    blocks = length // 128

    @pl.when(pair == 0)
    def _():
        x = x_ref[...].astype(f32)
        inverse = lax.rsqrt(jnp.mean(x * x, axis=-1, keepdims=True) + epsilon)
        n_ref[...] = (x * inverse * gain_ref[...]).astype(bf16)
        blank = jnp.zeros((8, length), jnp.int32)
        ahead = jnp.concatenate([jnp.broadcast_to(first_ref[0:1, :], (8, length)), blank], axis=1)
        behind = jnp.concatenate([jnp.broadcast_to(last_ref[7:8, :], (8, length)), blank], axis=1)
        place = lax.broadcasted_iota(jnp.int32, (8, 2 * length), 1)
        row = lax.broadcasted_iota(jnp.int32, (8, 2 * length), 0)
        line = jnp.where(place < length, behind, pltpu.roll(ahead, length - 1, 1))
        ids = line
        for r in range(1, 8):
            ids = jnp.where(row == r, pltpu.roll(line, r, 1), ids)
        ids_ref[...] = ids

    normed = n_ref[...]
    q = dot(normed, wq_ref[...]).astype(bf16)
    k = dot(normed, wk_ref[...]).astype(bf16)
    v = dot(normed, wv_ref[...]).astype(bf16)
    q_ref[...] = q
    k_ref[...] = k
    v_ref[...] = v
    ids = ids_ref[...]
    lane = lax.broadcasted_iota(jnp.int32, (length, 2 * half), 1)
    zero = jnp.zeros_like(q)
    out = None
    for h in range(2):
        head = 2 * pair + h
        mine = (lane < half) if h == 0 else (lane >= half)
        spread = jnp.zeros(ids.shape, f32)
        for b in range(buckets):
            spread = jnp.where(ids == b, table_ref[b, head], spread)
        for a in range(16):
            left = 127 - 8 * a
            bias_ref[8 * a : 8 * a + 8, :] = pltpu.roll(spread, 2 * length - left, 1)
        q_head = jnp.where(mine, q, zero)
        for i in range(blocks):
            rows = slice(128 * i, 128 * i + 128)
            start = 128 * (blocks - 1 - i)
            s = contract_last(q_head[rows], k) * scale + bias_ref[:, start : start + length]
            e = jnp.exp(s - jnp.max(s, axis=-1, keepdims=True))
            p = e / jnp.sum(e, axis=-1, keepdims=True)
            p_ref[h, rows, :] = p.astype(bf16)
        part = dot(p_ref[h], jnp.where(mine, v, zero))
        out = part if out is None else out + part
    o_ref[...] = out.astype(bf16)


def attend(x, gain, wq, wk, wv, table, bucket_ids):
    length, width = x.shape
    local = wq.shape[1]
    heads = table.shape[1]
    span = 2 * local // heads
    column = pl.BlockSpec((length, span), lambda j: (0, j))
    weight = pl.BlockSpec((width, span), lambda j: (0, j))
    thin = jax.ShapeDtypeStruct((length, local), bf16)
    return pl.pallas_call(
        attend_kernel,
        grid=(heads // 2,),
        in_specs=[
            whole((length, width)), whole((1, width)), weight, weight, weight, scalars(),
            pl.BlockSpec((8, length), lambda j: (0, 0)),
            pl.BlockSpec((8, length), lambda j: (length // 8 - 1, 0)),
        ],
        out_specs=[
            column, column, column, column,
            pl.BlockSpec((2, length, length), lambda j: (j, 0, 0)),
            whole((8, 2 * length)),
        ],
        out_shape=[
            thin, thin, thin, thin,
            jax.ShapeDtypeStruct((heads, length, length), bf16),
            jax.ShapeDtypeStruct((8, 2 * length), jnp.int32),
        ],
        scratch_shapes=[pltpu.VMEM((length, width), bf16), pltpu.VMEM((128, 2 * length), f32)],
        compiler_params=params(),
        cost_estimate=cost(9_000_000_000, 9_000_000),
        name="attend",
    )(x, gain, wq, wk, wv, table, bucket_ids, bucket_ids)


def attend_back_kernel(
    side_ref, do_ref, q_ref, k_ref, v_ref, p_ref, wq_ref, wk_ref, wv_ref,
    o_ref, da_ref, x_ref, gain_ref, ids_ref, router_ref, norm2_ref, buckets_ref,
    dn_ref, keep_a_ref, send_a_ref, keep_b_ref, send_b_ref,
    ds_ref, acc_ref, total_ref, n_ref, small_ref,
):
    pair = pl.program_id(0)
    last = pl.num_programs(0) - 1
    length = do_ref.shape[0]
    span = do_ref.shape[1]
    half = span // 2
    scale = half ** (-0.5)
    blocks = length // 128
    buckets = buckets_ref.shape[0]
    experts = router_ref.shape[0]
    local = keep_a_ref.shape[0]
    even = side_ref[0] == 0

    @pl.when(pair == 0)
    def _():
        x = x_ref[...].astype(f32)
        inverse = lax.rsqrt(jnp.mean(x * x, axis=-1, keepdims=True) + epsilon)
        n_ref[...] = (x * inverse * gain_ref[...]).astype(bf16)
        small_ref[...] = jnp.zeros_like(small_ref)
        small_ref[0:experts, :] = router_ref[...]
        small_ref[experts + 1 : experts + 2, :] = norm2_ref[...]

    do = do_ref[...]
    q = q_ref[...]
    k = k_ref[...]
    v = v_ref[...]
    ids = ids_ref[...]
    q_turned = q.T
    do_turned = do.T
    lane = lax.broadcasted_iota(jnp.int32, (length, span), 1)
    zero = jnp.zeros_like(q)
    dq = None
    dk_parts = []
    dv_parts = []
    for h in range(2):
        mine = (lane < half) if h == 0 else (lane >= half)
        do_head = jnp.where(mine, do, zero)
        acc_ref[...] = jnp.zeros_like(acc_ref)
        for i in range(blocks):
            rows = slice(128 * i, 128 * i + 128)
            start = 128 * (blocks - 1 - i)
            p = p_ref[h, rows, :].astype(f32)
            dp = contract_last(do_head[rows], v)
            ds = p * (dp - jnp.sum(p * dp, axis=-1, keepdims=True))
            acc_ref[:, start : start + length] += ds
            ds_ref[rows, :] = ds.astype(bf16)
        ds_all = ds_ref[...]
        part = dot(ds_all, jnp.where(mine, k, zero))
        dq = part if dq is None else dq + part
        dk_parts.append(dot(q_turned[h * half : (h + 1) * half], ds_all))
        dv_parts.append(dot(do_turned[h * half : (h + 1) * half], p_ref[h]))
        diag = None
        for a in range(16):
            piece = pltpu.roll(acc_ref[8 * a : 8 * a + 8, :], 127 - 8 * a, 1)
            diag = piece if diag is None else diag + piece
        lines = []
        for b in range(buckets):
            hit = jnp.where(ids == b, diag, 0.0)
            fold = hit[:, 0:128]
            for y in range(1, 2 * length // 128):
                fold = fold + hit[:, 128 * y : 128 * y + 128]
            lines.append(jnp.sum(fold, axis=0, keepdims=True))
        lines.append(jnp.zeros((128 - buckets, 128), f32))
        sums = jnp.sum(jnp.concatenate(lines, axis=0).T, axis=0, keepdims=True)
        row = lax.broadcasted_iota(jnp.int32, (small_ref.shape[0], 128), 0)
        small_ref[:, 0:128] = jnp.where(
            row == experts + 2 + 2 * pair + h, sums, small_ref[:, 0:128]
        )
    dq_low = (dq * scale).astype(bf16)
    dk_turned = (jnp.concatenate(dk_parts, axis=0) * scale).astype(bf16)
    dv_turned = jnp.concatenate(dv_parts, axis=0).astype(bf16)
    part = (
        contract_last(dq_low, wq_ref[...])
        + contract_last(dk_turned.T, wk_ref[...])
        + contract_last(dv_turned.T, wv_ref[...])
    )
    normed = n_ref[...]
    here = pl.ds(pl.multiple_of(pair * span, span), span)
    grad_k = dot(dk_turned, normed).astype(bf16)
    grad_v = dot(dv_turned, normed).astype(bf16)
    keep_a_ref[here, :] = jnp.where(even, grad_k, grad_v)
    send_a_ref[here, :] = jnp.where(even, grad_v, grad_k)
    grad_q = dot(dq_low.T, normed).astype(bf16)
    grad_o = dot(o_ref[...].T, da_ref[...]).astype(bf16)
    keep_b_ref[here, :] = jnp.where(even, grad_q, grad_o)
    send_b_ref[here, :] = jnp.where(even, grad_o, grad_q)

    @pl.when(pair == 0)
    def _():
        total_ref[...] = part

    @pl.when(pair > 0)
    def _():
        total_ref[...] += part

    @pl.when(pair == last)
    def _():
        total = total_ref[...]
        dn_ref[...] = total.astype(bf16)
        x = x_ref[...].astype(f32)
        inverse = lax.rsqrt(jnp.mean(x * x, axis=-1, keepdims=True) + epsilon)
        small_ref[experts : experts + 1, :] = jnp.sum(
            total * x * inverse, axis=0, keepdims=True
        )
        small = small_ref[...].astype(bf16)
        keep_b_ref[local:, :] = small
        send_b_ref[local:, :] = small


def small_rows(experts, heads):
    return -(-(experts + 2 + heads) // 64) * 64


def attend_back(side, do, q, k, v, p, wq, wk, wv, o, da, x, gain, ids, router, norm2, table):
    length, local = do.shape
    width = wq.shape[0]
    heads = p.shape[0]
    experts = router.shape[0]
    span = 2 * local // heads
    extra = small_rows(experts, heads)
    column = pl.BlockSpec((length, span), lambda j: (0, j))
    weight = pl.BlockSpec((width, span), lambda j: (0, j))
    part_a = jax.ShapeDtypeStruct((local, width), bf16)
    part_b = jax.ShapeDtypeStruct((local + extra, width), bf16)
    return pl.pallas_call(
        attend_back_kernel,
        grid=(heads // 2,),
        in_specs=[
            scalars(), column, column, column, column,
            pl.BlockSpec((2, length, length), lambda j: (j, 0, 0)),
            weight, weight, weight, column,
            whole((length, width)), whole((length, width)), whole((1, width)),
            whole(ids.shape), whole((experts, width)), whole((1, width)), whole(table.shape),
        ],
        out_specs=[
            whole((length, width)), whole(part_a.shape), whole(part_a.shape),
            whole(part_b.shape), whole(part_b.shape),
        ],
        out_shape=[
            jax.ShapeDtypeStruct((length, width), bf16), part_a, part_a, part_b, part_b,
        ],
        scratch_shapes=[
            pltpu.VMEM((length, length), bf16),
            pltpu.VMEM((128, 2 * length), f32),
            pltpu.VMEM((length, width), f32),
            pltpu.VMEM((length, width), bf16),
            pltpu.VMEM((extra, width), f32),
        ],
        compiler_params=params(),
        cost_estimate=cost(12_000_000_000, 9_000_000),
        name="attend_back",
    )(side, do, q, k, v, p, wq, wk, wv, o, da, x, gain, ids, router, norm2, table)


def hits(ids, count, axis):
    shape = (count, ids.shape[1]) if axis == 0 else (ids.shape[0], count)
    return jnp.where(lax.broadcasted_iota(jnp.int32, shape, axis) == ids, 1.0, 0.0).astype(bf16)


def place_kernel(ids_ref, rows_ref, out_ref):
    out_ref[...] = dot(hits(ids_ref[...], out_ref.shape[0], 0), rows_ref[...]).astype(bf16)


def place(ids, rows, places):
    return pl.pallas_call(
        place_kernel,
        out_shape=jax.ShapeDtypeStruct((places, rows.shape[1]), bf16),
        compiler_params=params(),
        cost_estimate=cost(1_000_000_000, 3_000_000),
        name="place",
    )(ids, rows)


def pick_kernel(ids_ref, slots_ref, out_ref):
    out_ref[...] = dot(hits(ids_ref[...], slots_ref.shape[0], 1), slots_ref[...]).astype(bf16)


def pick(ids, slots):
    return pl.pallas_call(
        pick_kernel,
        out_shape=jax.ShapeDtypeStruct((ids.shape[0], slots.shape[1]), bf16),
        compiler_params=params(),
        cost_estimate=cost(1_000_000_000, 3_000_000),
        name="pick",
    )(ids, slots)


def finish_kernel(own_ref, got_ref, hmid_ref, out_ref):
    picked = own_ref[...].astype(f32) + got_ref[...].astype(f32)
    out_ref[...] = (hmid_ref[...] + picked).astype(bf16)


def finish(own, got, hmid):
    return pl.pallas_call(
        finish_kernel,
        out_shape=jax.ShapeDtypeStruct(hmid.shape, bf16),
        compiler_params=params(),
        cost_estimate=cost(1_000_000, 5_000_000),
        name="finish",
    )(own, got, hmid)


def middle_kernel(
    mp_ref, o_ref, o_other_ref, w_ref, w_other_ref, x_ref, gain_ref, ids_ref, hmid_ref, out_ref
):
    low = mp_ref[0] == 0
    o, o_other = o_ref[...], o_other_ref[...]
    w, w_other = w_ref[...], w_other_ref[...]
    heads = jnp.concatenate([jnp.where(low, o, o_other), jnp.where(low, o_other, o)], axis=1)
    weight = jnp.concatenate([jnp.where(low, w, w_other), jnp.where(low, w_other, w)], axis=0)
    hmid = x_ref[...].astype(f32) + dot(heads, weight)
    hmid_ref[...] = hmid
    inverse = lax.rsqrt(jnp.mean(hmid * hmid, axis=-1, keepdims=True) + epsilon)
    normed = (hmid * inverse * gain_ref[...]).astype(bf16)
    out_ref[...] = dot(hits(ids_ref[...], out_ref.shape[0], 0), normed).astype(bf16)


def middle(mp, o, o_other, w, w_other, x, gain, ids, places):
    return pl.pallas_call(
        middle_kernel,
        in_specs=[scalars()] + [pl.BlockSpec(memory_space=pltpu.VMEM)] * 7,
        out_shape=[
            jax.ShapeDtypeStruct(x.shape, f32),
            jax.ShapeDtypeStruct((places, x.shape[1]), bf16),
        ],
        compiler_params=params(),
        cost_estimate=cost(2_000_000_000, 6_000_000),
        name="middle",
    )(mp, o, o_other, w, w_other, x, gain, ids)


def middle_back_kernel(
    own_ref, got_ref, hmid_ref, c_ref, gain_ref, w_ref, dh_ref, da_ref, do_ref, norm_ref
):
    hmid = hmid_ref[...]
    dn = own_ref[...].astype(f32) + got_ref[...].astype(f32)
    inverse = lax.rsqrt(jnp.mean(hmid * hmid, axis=-1, keepdims=True) + epsilon)
    scaled = dn * gain_ref[...]
    inner = jnp.mean(scaled * hmid, axis=-1, keepdims=True)
    dh = c_ref[...].astype(f32) + inverse * scaled - hmid * (inverse * inverse * inverse * inner)
    dh_ref[...] = dh
    da = dh.astype(bf16)
    da_ref[...] = da
    do_ref[...] = contract_last(da, w_ref[...]).astype(bf16)
    norm_ref[...] = jnp.sum(dn * hmid * inverse, axis=0, keepdims=True)


def middle_back(own, got, hmid, c, gain, w):
    tokens, width = own.shape
    return pl.pallas_call(
        middle_back_kernel,
        out_shape=[
            jax.ShapeDtypeStruct((tokens, width), f32),
            jax.ShapeDtypeStruct((tokens, width), bf16),
            jax.ShapeDtypeStruct((tokens, w.shape[0]), bf16),
            jax.ShapeDtypeStruct((1, width), f32),
        ],
        compiler_params=params(),
        cost_estimate=cost(1_000_000_000, 6_000_000),
        name="middle_back",
    )(own, got, hmid, c, gain, w)


def input_back_kernel(own_ref, got_ref, x_ref, dh_ref, gain_ref, out_ref):
    x = x_ref[...].astype(f32)
    dn = own_ref[...].astype(f32) + got_ref[...].astype(f32)
    inverse = lax.rsqrt(jnp.mean(x * x, axis=-1, keepdims=True) + epsilon)
    scaled = dn * gain_ref[...]
    inner = jnp.mean(scaled * x, axis=-1, keepdims=True)
    out_ref[...] = dh_ref[...] + inverse * scaled - x * (inverse * inverse * inverse * inner)


def input_back(own, got, x, dh, gain):
    return pl.pallas_call(
        input_back_kernel,
        out_shape=jax.ShapeDtypeStruct(dh.shape, f32),
        compiler_params=params(),
        cost_estimate=cost(100_000_000, 6_000_000),
        name="input_back",
    )(own, got, x, dh, gain)


def unpack_kernel(
    side_ref, a_ref, a_got_ref, b_ref, b_got_ref, s_got_ref,
    q_ref, k_ref, v_ref, o_ref, router_ref, table_ref, norm1_ref, norm2_ref,
):
    even = side_ref[0] == 0
    local, width = a_ref.shape
    experts = router_ref.shape[1]
    buckets, heads = table_ref.shape
    a, a_got = a_ref[...], a_got_ref[...]
    b, b_got = b_ref[0:local, :], b_got_ref[...]
    k_ref[...] = jnp.where(even, a, a_got).T.astype(f32)
    v_ref[...] = jnp.where(even, a_got, a).T.astype(f32)
    q_ref[...] = jnp.where(even, b, b_got).T.astype(f32)
    o_ref[...] = jnp.where(even, b_got, b).astype(f32)
    small = b_ref[local:, :].astype(f32)
    both = small + s_got_ref[...].astype(f32)
    pad = jnp.zeros((-small.shape[0] % 128, width), f32)
    router_ref[...] = jnp.concatenate([both, pad], axis=0).T[:, :experts]
    norm1_ref[...] = both[experts : experts + 1]
    norm2_ref[...] = small[experts + 1 : experts + 2]
    lines = small[experts + 2 : experts + 2 + heads, 0:128]
    pad = jnp.zeros((128 - heads, 128), f32)
    table_ref[...] = jnp.concatenate([lines, pad], axis=0).T[:buckets, :heads]


def unpack(side, a, a_got, b, b_got, s_got, experts, buckets, heads):
    local, width = a.shape
    turned = jax.ShapeDtypeStruct((width, local), f32)
    return pl.pallas_call(
        unpack_kernel,
        in_specs=[scalars()] + [pl.BlockSpec(memory_space=pltpu.VMEM)] * 5,
        out_shape=[
            turned, turned, turned,
            jax.ShapeDtypeStruct((local, width), f32),
            jax.ShapeDtypeStruct((width, experts), f32),
            jax.ShapeDtypeStruct((buckets, heads), f32),
            jax.ShapeDtypeStruct((1, width), f32),
            jax.ShapeDtypeStruct((1, width), f32),
        ],
        compiler_params=params(),
        cost_estimate=cost(100_000_000, 8_000_000),
        name="unpack",
    )(side, a, a_got, b, b_got, s_got)


def expert_kernel(
    x_ref, c_ref, w_in_ref, w_out_ref, router_ref, mine_ref,
    dx_ref, hid_ref, dpre_ref, deo_ref, gate_ref, dlog_ref,
    pre_ref, up_ref, probs_ref, inner_ref, total_ref,
):
    step = pl.program_id(0)
    rows = x_ref.shape[0]
    chunk = 64
    hot = lax.broadcasted_iota(jnp.int32, probs_ref.shape, 1) == mine_ref[0]

    @pl.when(step == 0)
    def _():
        router = router_ref[...]
        high = router.astype(bf16)
        rest = (router - high.astype(f32)).astype(bf16)
        logits = dot(x_ref[...], high) + dot(x_ref[...], rest)
        e = jnp.exp(logits - jnp.max(logits, axis=-1, keepdims=True))
        probs = e / jnp.sum(e, axis=-1, keepdims=True)
        gate = jnp.sum(jnp.where(hot, probs, 0.0), axis=-1, keepdims=True)
        probs_ref[...] = probs
        gate_ref[...] = gate
        deo_ref[...] = (gate * c_ref[...].astype(f32)).astype(bf16)

    pre_ref[...] = dot(x_ref[...], w_in_ref[...])
    up_ref[...] = contract_last(deo_ref[...], w_out_ref[...])
    for r in range(0, rows, chunk):
        part = slice(r, r + chunk)
        u = pre_ref[part, :]
        up = up_ref[part, :]
        square = u * u
        t = jnp.tanh(gelu_scale * u * (1.0 + gelu_cubic * square))
        side = 0.5 * (1.0 + t)
        hid = u * side
        slope = side + (0.5 * gelu_scale) * u * (1.0 - t * t) * (1.0 + (3.0 * gelu_cubic) * square)
        hid_ref[part, :] = hid.astype(bf16)
        dpre_ref[part, :] = (up * slope).astype(bf16)
        inner = jnp.sum(hid * up, axis=-1, keepdims=True)
        before = jnp.where(step == 0, 0.0, inner_ref[part, :])
        inner_ref[part, :] = before + inner
    part = contract_last(dpre_ref[...], w_in_ref[...])

    @pl.when(step == 0)
    def _():
        total_ref[...] = part

    @pl.when(step > 0)
    def _():
        total_ref[...] += part

    @pl.when(step == pl.num_programs(0) - 1)
    def _():
        dlog = inner_ref[...] * (hot.astype(f32) - probs_ref[...])
        dlog_ref[...] = dlog
        dx_ref[...] = (
            total_ref[...] + contract_last(dlog.astype(bf16), router_ref[...].astype(bf16))
        ).astype(bf16)


def expert(x, c, w_in, w_out, router, mine):
    rows, width = x.shape
    hidden = w_in.shape[1]
    experts = router.shape[1]
    step = 512 if hidden % 512 == 0 else hidden
    return pl.pallas_call(
        expert_kernel,
        grid=(hidden // step,),
        in_specs=[
            whole((rows, width)), whole((rows, width)),
            pl.BlockSpec((width, step), lambda j: (0, j)),
            pl.BlockSpec((step, width), lambda j: (j, 0)),
            whole((width, experts)), scalars(),
        ],
        out_specs=[
            whole((rows, width)),
            pl.BlockSpec((rows, step), lambda j: (0, j)),
            pl.BlockSpec((rows, step), lambda j: (0, j)),
            whole((rows, width)), whole((rows, 1)), whole((rows, experts)),
        ],
        out_shape=[
            jax.ShapeDtypeStruct((rows, width), bf16),
            jax.ShapeDtypeStruct((rows, hidden), bf16),
            jax.ShapeDtypeStruct((rows, hidden), bf16),
            jax.ShapeDtypeStruct((rows, width), bf16),
            jax.ShapeDtypeStruct((rows, 1), f32),
            jax.ShapeDtypeStruct((rows, experts), f32),
        ],
        scratch_shapes=[
            pltpu.VMEM((rows, step), f32),
            pltpu.VMEM((rows, step), f32),
            pltpu.VMEM((rows, experts), f32),
            pltpu.VMEM((rows, 1), f32),
            pltpu.VMEM((rows, width), f32),
        ],
        compiler_params=params(),
        cost_estimate=cost(4_500_000_000, 12_000_000),
        name="expert",
    )(x, c, w_in, w_out, router, mine)


def exchange(value, count, bit):
    return lax.ppermute(value, "dp", [(i, i ^ (1 << bit)) for i in range(count)])


def side_of(bit):
    return (lax.axis_index("dp") >> bit) & 1


def add(left, right):
    return (left.astype(f32) + right.astype(f32)).astype(left.dtype)


def halves(value, bit):
    n = value.shape[0] // 2
    first, second = value[:n], value[n:]
    low = side_of(bit) == 0
    return jnp.where(low, first, second), jnp.where(low, second, first)


def join(value, got, bit):
    low = side_of(bit) == 0
    return jnp.concatenate([jnp.where(low, value, got), jnp.where(low, got, value)])


def shards(
    count,
    hidden_in,
    norm1_gain,
    w_query,
    w_key,
    w_value,
    w_output,
    bias_table,
    bucket_ids,
    norm2_gain,
    router,
    w_in,
    w_out,
    expert_ids,
    slot_ids,
    out_grad,
):
    tokens, width = hidden_in.shape
    buckets, heads = bias_table.shape
    experts = router.shape[1]
    capacity = max(2, 5 * tokens // (4 * experts))
    places = experts * capacity
    bits = (count - 1).bit_length()
    swap = [(0, 1), (1, 0)]
    mp = lax.axis_index("mp").astype(jnp.int32)
    dp = lax.axis_index("dp").astype(jnp.int32)
    side = (dp & 1)[None]
    gain1 = norm1_gain[None, :]
    gain2 = norm2_gain[None, :]

    def swapped(value):
        return lax.ppermute(value, "mp", swap)

    def to_experts(rows):
        block = rows.reshape(experts, capacity, width)
        return lax.all_to_all(block, "dp", split_axis=0, concat_axis=0, tiled=True).reshape(
            places, width
        )

    flat_slot = expert_ids * capacity + slot_ids
    slot_row = flat_slot[None, :]
    slot_column = flat_slot[:, None]

    w_output_other = swapped(w_output)
    c_here = to_experts(place(slot_row, out_grad, places))
    o, q, k, v, p, ids = attend(
        hidden_in, gain1, w_query, w_key, w_value, bias_table, bucket_ids
    )
    o, w_output_other = lax.optimization_barrier((o, w_output_other))
    o_other = swapped(o)
    hmid, x_send = middle(
        mp[None], o, o_other, w_output, w_output_other, hidden_in, gain2, slot_row, places
    )
    x_here = to_experts(x_send)

    dx, hid, dpre, deo, gate, dlog = expert(x_here, c_here, w_in[0], w_out[0], router, dp[None])
    dx_home = to_experts(dx)
    eo = (gate * dot(hid, w_out[0])).astype(bf16)
    grad_w_out = contract_rows(hid, deo)[None]
    grad_w_in = contract_rows(x_here, dpre)[None]
    grad_router = contract_rows(dlog, x_here.astype(f32), lax.Precision.HIGHEST)
    dx_home, eo, grad_w_out, grad_w_in, grad_router = lax.optimization_barrier(
        (dx_home, eo, grad_w_out, grad_w_in, grad_router)
    )

    dn2 = pick(slot_column, dx_home)
    dn2_other = swapped(dn2)
    eo_home = to_experts(eo)
    dh, da, do, grad_norm2 = middle_back(dn2, dn2_other, hmid, out_grad, gain2, w_output)
    do, eo_home = lax.optimization_barrier((do, eo_home))
    dn1, keep_a, send_a, keep_b, send_b = attend_back(
        side, do, q, k, v, p, w_query, w_key, w_value, o, da, hidden_in, gain1, ids,
        grad_router, grad_norm2, bias_table,
    )
    dn1_other = swapped(dn1)

    order_a = tuple(range(1, bits))
    order_b = (2, 1) + tuple(range(3, bits))
    a = add(keep_a, exchange(send_a, count, 0))
    b = add(keep_b, exchange(send_b, count, 0))
    picked = pick(slot_column, eo_home)
    for bit_a, bit_b in zip(order_a, order_b):
        keep_a, send_a = halves(a, bit_a)
        keep_b, send_b = halves(b, bit_b)
        got_a = exchange(send_a, count, bit_a)
        got_b = exchange(send_b, count, bit_b)
        a, b = add(keep_a, got_a), add(keep_b, got_b)
    a, b, picked, dn1_other = lax.optimization_barrier((a, b, picked, dn1_other))
    picked_other = swapped(picked)
    grad_hidden = input_back(dn1, dn1_other, hidden_in, dh, gain1)
    for bit_a, bit_b in zip(order_a[::-1], order_b[::-1]):
        got_a = exchange(a, count, bit_a)
        got_b = exchange(b, count, bit_b)
        a, b = join(a, got_a, bit_a), join(b, got_b, bit_b)
    local = a.shape[0]
    a_got = exchange(a, count, 0)
    b_got = exchange(b[:local], count, 0)
    small_got = swapped(b[local:])
    hidden_out = finish(picked, picked_other, hmid)
    hidden_out, grad_hidden, a_got, b_got, small_got = lax.optimization_barrier(
        (hidden_out, grad_hidden, a_got, b_got, small_got)
    )
    grad_q, grad_k, grad_v, grad_w_output, grad_router, grad_table, grad_norm1, grad_norm2 = unpack(
        side, a, a_got, b, b_got, small_got, experts, buckets, heads
    )
    return (
        hidden_out,
        grad_hidden,
        grad_norm1[0],
        grad_q,
        grad_k,
        grad_v,
        grad_w_output,
        grad_table,
        grad_norm2[0],
        grad_router,
        grad_w_in,
        grad_w_out,
    )


def solution(mesh):
    return jax.shard_map(
        functools.partial(shards, mesh.shape["dp"]),
        mesh=mesh,
        in_specs=(
            P("dp", None),
            P(),
            P(None, "mp"),
            P(None, "mp"),
            P(None, "mp"),
            P("mp", None),
            P(None, "mp"),
            P(),
            P(),
            P(),
            P("dp", None, "mp"),
            P("dp", "mp", None),
            P("dp"),
            P("dp"),
            P("dp", None),
        ),
        out_specs=(
            P("dp", None),
            P("dp", None),
            P(),
            P(None, "mp"),
            P(None, "mp"),
            P(None, "mp"),
            P("mp", None),
            P(None, "mp"),
            P(),
            P(),
            P("dp", None, "mp"),
            P("dp", "mp", None),
        ),
        check_vma=False,
    )
```

profile of v0, /device:TPU:0, one launch (start us, length us, event | category | flops | bytes accessed | tf_op | source)
XLA Modules:
  0.0 237.0 jit_solution(1665370406802292953)
XLA Ops:
  1.9 2.8 %place.1 = bf16[640,768]{1,0:T(8,128)(2,1)} custom-call(s32[1,512]{1,0:T(1,128)} %bitcast.37, bf16[512,768]{1,0:T(8,128)(2,1)} %c_ref.1), custom_call_target="tpu_custom_call" | custom-call | flops 1000000000 | bytes 3000000 | tf_op jit(solution)/shard_map/place/pallas_call | solution.py:310
  4.8 7.4 %all-to-all-start.1 = ((bf16[16,40,768]{2,1,0:T(8,128)(2,1)}), bf16[16,40,768]{2,1,0:T(8,128)(2,1)S(1)}, u32[]{:S(2)}, u32[]{:S(2)}) async-start(bf16[16,40,768]{2,1,0:T(8,128)(2,1)} %bitcast.33), calls=%async_computation.1 | async-start | bytes 1966080 | tf_op jit(solution)/shard_map/all_to_all | solution.py:632
  15.0 9.6 %attend.1 = (bf16[512,384]{1,0:T(8,128)(2,1)}, bf16[512,384]{1,0:T(8,128)(2,1)}, bf16[512,384]{1,0:T(8,128)(2,1)}, bf16[512,384]{1,0:T(8,128)(2,1)}, bf16[6,512,512]{2,1,0:T(8,128)(2,1)}, /*index=5*/s32[8,1024]{1,0:T(8,128)}) custom-call(bf16[512,768]{1,0:T(8,128)(2,1)} %x_ref.7, f32[1,768]{1,0:T(1,128)} %broadcast_in_dim.30.gain_ref, ...), custom_call_target="tpu_custom_call" | custom-call | flops 8999999488 | bytes 9000000 | tf_op jit(solution)/shard_map/attend/pallas_call | solution.py:116
  24.6 3.4 %collective-permute-done.w_other_ref = bf16[384,768]{1,0:T(8,128)(2,1)} collective-permute-done((bf16[384,768]{1,0:T(8,128)(2,1)S(1)}, bf16[384,768]{1,0:T(8,128)(2,1)}, u32[]{:S(2)}, u32[]{:S(2)}) %collective-permute-start) | collective-permute-done | bytes 589856 | tf_op jit(solution)/shard_map/ppermute | solution.py:628
  30.1 8.8 %collective-permute-done.1.o_other_ref = bf16[512,384]{1,0:T(8,128)(2,1)S(1)} collective-permute-done((bf16[512,384]{1,0:T(8,128)(2,1)}, bf16[512,384]{1,0:T(8,128)(2,1)S(1)}, u32[]{:S(2)}, u32[]{:S(2)}) %collective-permute-start.1) | collective-permute-done | bytes 393248 | tf_op jit(solution)/shard_map/ppermute | solution.py:628
  39.6 4.5 %middle.1 = (f32[512,768]{1,0:T(8,128)}, bf16[640,768]{1,0:T(8,128)(2,1)}) custom-call(s32[1]{0:T(128)} %bitcast.2.mp_ref, bf16[512,384]{1,0:T(8,128)(2,1)} %get-tuple-element.62.o_ref, bf16[512,384]{1,0:T(8,128)(2,1)} %copy-done.19, bf16[384,768]{1,0:T(8,128)(2,1)} %w_ref.3, bf16[384,768]{1,0:T(8,128)(2,1)} %collective-permute-done.w_other_ref, ...), custom_call_target="tpu_custom_call" | custom-call | flops 2000000000 | bytes 6000000 | tf_op jit(solution)/shard_map/middle/pallas_call | solution.py:364
  44.1 5.4 %all-to-all-start = ((bf16[16,40,768]{2,1,0:T(8,128)(2,1)}), bf16[16,40,768]{2,1,0:T(8,128)(2,1)S(1)}, u32[]{:S(2)}, u32[]{:S(2)}) async-start(bf16[16,40,768]{2,1,0:T(8,128)(2,1)} %bitcast.35), calls=%async_computation | async-start | bytes 1966080 | tf_op jit(solution)/shard_map/all_to_all | solution.py:632
  50.5 20.9 %all-to-all-done = bf16[16,40,768]{2,1,0:T(8,128)(2,1)S(1)} async-done(((bf16[16,40,768]{2,1,0:T(8,128)(2,1)}), bf16[16,40,768]{2,1,0:T(8,128)(2,1)S(1)}, u32[]{:S(2)}, u32[]{:S(2)}) %all-to-all-start) | async-done | bytes 983072 | tf_op jit(solution)/shard_map/all_to_all | solution.py:632
  72.4 12.2 %expert.1 = (bf16[640,768]{1,0:T(8,128)(2,1)}, bf16[640,1536]{1,0:T(8,128)(2,1)}, bf16[640,1536]{1,0:T(8,128)(2,1)}, bf16[640,768]{1,0:T(8,128)(2,1)}, f32[640,1]{1,0:T(8,128)}, /*index=5*/f32[640,16]{1,0:T(8,128)}) custom-call(bf16[640,768]{1,0:T(8,128)(2,1)} %bitcast.28, bf16[640,768]{1,0:T(8,128)(2,1)} %bitcast.32, bf16[768,1536]{1,0:T(8,128)(2,1)} %bitcast.40, ...), custom_call_target="tpu_custom_call" | custom-call | flops 4499999744 | bytes 12000000 | tf_op jit(solution)/shard_map/expert/pallas_call | solution.py:536
  84.6 6.7 %all-to-all-start.2 = ((bf16[16,40,768]{2,1,0:T(8,128)(2,1)}), bf16[16,40,768]{2,1,0:T(8,128)(2,1)S(1)}, u32[]{:S(2)}, u32[]{:S(2)}) async-start(bf16[16,40,768]{2,1,0:T(8,128)(2,1)} %bitcast.36), calls=%async_computation.2 | async-start | bytes 1966080 | tf_op jit(solution)/shard_map/all_to_all | solution.py:632
  92.7 5.9 %convolution_bitcast_fusion = f32[1,768,1536]{2,1,0:T(8,128)} fusion(bf16[640,768]{1,0:T(8,128)(2,1)S(1)} %bitcast.30, bf16[640,1536]{1,0:T(8,128)(2,1)} %get-tuple-element.69), kind=kOutput, calls=%fused_computation | convolution fusion | flops 1509949440 | bytes 7667712 | tf_op jit(solution)/shard_map/dot_general | solution.py:27
  98.6 4.3 %convolution_bitcast_fusion.1 = f32[1,1536,768]{2,1,0:T(8,128)} fusion(bf16[640,1536]{1,0:T(8,128)(2,1)S(1)} %copy-done.20, bf16[640,768]{1,0:T(8,128)(2,1)S(1)} %copy-done.21), kind=kOutput, calls=%fused_computation.1 | convolution fusion | flops 1509949440 | bytes 7667712 | tf_op jit(solution)/shard_map/dot_general | solution.py:27
  102.9 2.6 %multiply_convert_fusion = bf16[640,768]{1,0:T(8,128)(2,1)} fusion(bf16[640,1536]{1,0:T(8,128)(2,1)S(1)} %copy-done.20, f32[640]{0:T(1024)S(1)} %reduce, bf16[1,1536,768]{2,1,0:T(8,128)(2,1)S(1)} %copy-done.18), kind=kOutput, calls=%fused_computation.2 | convolution fusion | flops 1510932480 | bytes 5310976 | tf_op jit(solution)/shard_map/dot_general | solution.py:19
  105.5 7.6 %all-to-all-done.2 = bf16[16,40,768]{2,1,0:T(8,128)(2,1)S(1)} async-done(((bf16[16,40,768]{2,1,0:T(8,128)(2,1)}), bf16[16,40,768]{2,1,0:T(8,128)(2,1)S(1)}, u32[]{:S(2)}, u32[]{:S(2)}) %all-to-all-start.2) | async-done | bytes 983072 | tf_op jit(solution)/shard_map/all_to_all | solution.py:632
  113.1 6.5 %all-to-all-start.3 = ((bf16[16,40,768]{2,1,0:T(8,128)(2,1)}), bf16[16,40,768]{2,1,0:T(8,128)(2,1)S(1)}, u32[]{:S(2)}, u32[]{:S(2)}) async-start(bf16[16,40,768]{2,1,0:T(8,128)(2,1)} %bitcast.15), calls=%async_computation.3 | async-start | bytes 1966080 | tf_op jit(solution)/shard_map/all_to_all | solution.py:632
  120.6 3.0 %pick.2.own_ref = bf16[512,768]{1,0:T(8,128)(2,1)} custom-call(s32[512,1]{1,0:T(8,128)} %copy.34.ids_ref, bf16[640,768]{1,0:T(8,128)(2,1)} %bitcast.34), custom_call_target="tpu_custom_call" | custom-call | flops 1000000000 | bytes 3000000 | tf_op jit(solution)/shard_map/pick/pallas_call | solution.py:324
  125.1 18.6 %collective-permute-done.2.got_ref = bf16[512,768]{1,0:T(8,128)(2,1)S(1)} collective-permute-done((bf16[512,768]{1,0:T(8,128)(2,1)}, bf16[512,768]{1,0:T(8,128)(2,1)S(1)}, u32[]{:S(2)}, u32[]{:S(2)}) %collective-permute-start.2) | collective-permute-done | bytes 786464 | tf_op jit(solution)/shard_map/ppermute | solution.py:628
  144.5 4.7 %middle_back.1 = (f32[512,768]{1,0:T(8,128)}, bf16[512,768]{1,0:T(8,128)(2,1)}, bf16[512,384]{1,0:T(8,128)(2,1)}, f32[1,768]{1,0:T(1,128)}) custom-call(bf16[512,768]{1,0:T(8,128)(2,1)} %pick.2.own_ref, bf16[512,768]{1,0:T(8,128)(2,1)} %copy-done.6, f32[512,768]{1,0:T(8,128)} %get-tuple-element.72.hmid_ref, bf16[512,768]{1,0:T(8,128)(2,1)} %c_ref.1, ...), custom_call_target="tpu_custom_call" | custom-call | flops 1000000000 | bytes 6000000 | tf_op jit(solution)/shard_map/middle_back/pallas_call | solution.py:395
  149.2 13.8 %attend_back.1 = (bf16[512,768]{1,0:T(8,128)(2,1)}, bf16[384,768]{1,0:T(8,128)(2,1)}, bf16[384,768]{1,0:T(8,128)(2,1)}, bf16[448,768]{1,0:T(8,128)(2,1)}, bf16[448,768]{1,0:T(8,128)(2,1)}) custom-call(s32[1]{0:T(128)} %bitcast.side_ref, bf16[512,384]{1,0:T(8,128)(2,1)} %get-tuple-element.75.do_ref, bf16[512,384]{1,0:T(8,128)(2,1)} %get-tuple-element.76.q_ref, ...), custom_call_target="tpu_custom_call" | custom-call | flops 12000000000 | bytes 9000000 | tf_op jit(solution)/shard_map/attend_back/pallas_call | solution.py:270
  165.1 3.0 %pick.3.own_ref = bf16[512,768]{1,0:T(8,128)(2,1)} custom-call(s32[512,1]{1,0:T(8,128)} %copy.34.ids_ref, bf16[640,768]{1,0:T(8,128)(2,1)} %bitcast.31), custom_call_target="tpu_custom_call" | custom-call | flops 1000000000 | bytes 3000000 | tf_op jit(solution)/shard_map/pick/pallas_call | solution.py:324
  173.1 5.3 %collective-permute-done.4 = bf16[192,768]{1,0:T(8,128)(2,1)S(1)} collective-permute-done((bf16[192,768]{1,0:T(8,128)(2,1)S(1)}, bf16[192,768]{1,0:T(8,128)(2,1)S(1)}, u32[]{:S(2)}, u32[]{:S(2)}) %collective-permute-start.4) | collective-permute-done | bytes 294944 | tf_op jit(solution)/shard_map/ppermute | solution.py:573
  184.3 2.4 %collective-permute-start.6 = (bf16[48,768]{1,0:T(8,128)(2,1)S(1)}, bf16[48,768]{1,0:T(8,128)(2,1)S(1)}, u32[]{:S(2)}, u32[]{:S(2)}) collective-permute-start(bf16[48,768]{1,0:T(8,128)(2,1)S(1)} %broadcast_select_fusion.17), channel_id=1, source_target_pairs={{0,16},{2,18},{4,20},{6,22},{8,24},{10,26},{12,28},{14,30},{16,0},... | collective-permute-start | bytes 221192 | tf_op jit(solution)/shard_map/ppermute | solution.py:573
  187.7 2.3 collective-permute-start.10
  190.0 2.1 collective-permute-done.6
  197.7 3.0 %collective-permute-done.13 = bf16[48,768]{1,0:T(8,128)(2,1)S(1)} collective-permute-done((bf16[48,768]{1,0:T(8,128)(2,1)S(1)}, bf16[48,768]{1,0:T(8,128)(2,1)S(1)}, u32[]{:S(2)}, u32[]{:S(2)}) %collective-permute-start.13) | collective-permute-done | bytes 73760 | tf_op jit(solution)/shard_map/ppermute | solution.py:573
  202.2 3.7 %collective-permute-done.14 = bf16[96,768]{1,0:T(8,128)(2,1)S(1)} collective-permute-done((bf16[96,768]{1,0:T(8,128)(2,1)S(1)}, bf16[96,768]{1,0:T(8,128)(2,1)S(1)}, u32[]{:S(2)}, u32[]{:S(2)}) %collective-permute-start.14) | collective-permute-done | bytes 147488 | tf_op jit(solution)/shard_map/ppermute | solution.py:573
  206.5 2.3 collective-permute-done.18
  210.8 2.8 %collective-permute-done.15 = bf16[192,768]{1,0:T(8,128)(2,1)S(1)} collective-permute-done((bf16[192,768]{1,0:T(8,128)(2,1)S(1)}, bf16[192,768]{1,0:T(8,128)(2,1)S(1)}, u32[]{:S(2)}, u32[]{:S(2)}) %collective-permute-start.15) | collective-permute-done | bytes 294944 | tf_op jit(solution)/shard_map/ppermute | solution.py:573
  213.9 2.4 %collective-permute-done.19 = bf16[224,768]{1,0:T(8,128)(2,1)S(1)} collective-permute-done((bf16[224,768]{1,0:T(8,128)(2,1)S(1)}, bf16[224,768]{1,0:T(8,128)(2,1)S(1)}, u32[]{:S(2)}, u32[]{:S(2)}) %collective-permute-start.19) | collective-permute-done | bytes 344096 | tf_op jit(solution)/shard_map/ppermute | solution.py:573
  216.5 3.9 %input_back.1 = f32[512,768]{1,0:T(8,128)} custom-call(bf16[512,768]{1,0:T(8,128)(2,1)} %get-tuple-element.89.own_ref, bf16[512,768]{1,0:T(8,128)(2,1)} %copy-done.7, bf16[512,768]{1,0:T(8,128)(2,1)} %x_ref.7, f32[512,768]{1,0:T(8,128)} %get-tuple-element.92.dh_ref, f32[1,768]{1,0:T(1,128)} %broadcast_in_dim.30.gain_ref), custom_call_target="tpu_custom_call" | custom-call | flops 100000000 | bytes 6000000 | tf_op jit(solution)/shard_map/input_back/pallas_call | solution.py:419
  222.6 3.0 %finish.1 = bf16[512,768]{1,0:T(8,128)(2,1)} custom-call(bf16[512,768]{1,0:T(8,128)(2,1)} %pick.3.own_ref, bf16[512,768]{1,0:T(8,128)(2,1)} %collective-permute-done.12.got_ref, f32[512,768]{1,0:T(8,128)} %get-tuple-element.72.hmid_ref), custom_call_target="tpu_custom_call" | custom-call | flops 1000000 | bytes 5000000 | tf_op jit(solution)/shard_map/finish/pallas_call | solution.py:339
  227.2 4.2 %unpack.1 = (f32[768,384]{1,0:T(8,128)}, f32[768,384]{1,0:T(8,128)}, f32[768,384]{1,0:T(8,128)}, f32[384,768]{1,0:T(8,128)}, f32[768,16]{1,0:T(8,128)}, /*index=...) custom-call(s32[1]{0:T(128)} %bitcast.side_ref, bf16[384,768]{1,0:T(8,128)(2,1)} %copy-done.2, ...), custom_call_target="tpu_custom_call" | custom-call | flops 100000000 | bytes 8000000 | tf_op jit(solution)/shard_map/unpack/pallas_call | solution.py:456
  (118 shorter events, 46.8 us)
Async XLA Ops:
  1.9 12.4 %copy-start.15 = (f32[32,6]{0,1:T(8,128)S(1)}, f32[32,6]{0,1:T(8,128)}, u32[]{:S(2)}) copy-start(f32[32,6]{0,1:T(8,128)} %param.21) | copy-start | bytes 2308
  4.8 39.3 %all-to-all-start.1 = ((bf16[16,40,768]{2,1,0:T(8,128)(2,1)}), bf16[16,40,768]{2,1,0:T(8,128)(2,1)S(1)}, u32[]{:S(2)}, u32[]{:S(2)}) async-start(bf16[16,40,768]{2,1,0:T(8,128)(2,1)} %bitcast.33), calls=%async_computation.1 | async-start | bytes 1966080 | tf_op jit(solution)/shard_map/all_to_all | solution.py:632
  12.1 15.8 %collective-permute-start = (bf16[384,768]{1,0:T(8,128)(2,1)S(1)}, bf16[384,768]{1,0:T(8,128)(2,1)}, u32[]{:S(2)}, u32[]{:S(2)}) collective-permute-start(bf16[384,768]{1,0:T(8,128)(2,1)S(1)} %copy-done.9), channel_id=1, source_target_pairs={{0,1},{1,0},{2,3},{3,2},{4,5},{5,4},{6,7},{7,6},{8,9},{9,8},{10,11... | collective-permute-start | bytes 1769480 | tf_op jit(solution)/shard_map/ppermute | solution.py:628
  15.0 14.5 %copy-start.17 = (f32[768]{0:T(1024)S(1)}, f32[768]{0:T(1024)}, u32[]{:S(2)}) copy-start(f32[768]{0:T(1024)} %param.23) | copy-start | bytes 9220
  28.0 10.9 %collective-permute-start.1 = (bf16[512,384]{1,0:T(8,128)(2,1)}, bf16[512,384]{1,0:T(8,128)(2,1)S(1)}, u32[]{:S(2)}, u32[]{:S(2)}) collective-permute-start(bf16[512,384]{1,0:T(8,128)(2,1)} %get-tuple-element.62.o_ref), channel_id=1, source_target_pairs={{0,1},{1,0},{2,3},{3,2},{4,5},{5,4},{6,7},{7,6},{8,9},{9,8},{10,11... | collective-permute-start | bytes 1179656 | tf_op jit(solution)/shard_map/ppermute | solution.py:628
  44.1 27.3 %copy-start.4 = (bf16[16,40,768]{2,1,0:T(8,128)(2,1)}, bf16[16,40,768]{2,1,0:T(8,128)(2,1)S(1)}, u32[]{:S(2)}) copy-start(bf16[16,40,768]{2,1,0:T(8,128)(2,1)S(1)} %all-to-all-done.1) | copy-start | bytes 2949124
  44.1 27.3 %all-to-all-start = ((bf16[16,40,768]{2,1,0:T(8,128)(2,1)}), bf16[16,40,768]{2,1,0:T(8,128)(2,1)S(1)}, u32[]{:S(2)}, u32[]{:S(2)}) async-start(bf16[16,40,768]{2,1,0:T(8,128)(2,1)} %bitcast.35), calls=%async_computation | async-start | bytes 1966080 | tf_op jit(solution)/shard_map/all_to_all | solution.py:632
  84.6 28.5 %all-to-all-start.2 = ((bf16[16,40,768]{2,1,0:T(8,128)(2,1)}), bf16[16,40,768]{2,1,0:T(8,128)(2,1)S(1)}, u32[]{:S(2)}, u32[]{:S(2)}) async-start(bf16[16,40,768]{2,1,0:T(8,128)(2,1)} %bitcast.36), calls=%async_computation.2 | async-start | bytes 1966080 | tf_op jit(solution)/shard_map/all_to_all | solution.py:632
  105.5 14.2 %copy-start.14 = (s32[512]{0:T(512)S(1)}, s32[512]{0:T(512)}, u32[]{:S(2)}) copy-start(s32[512]{0:T(512)} %multiply_add_fusion) | copy-start | bytes 6148
  113.1 36.1 %all-to-all-start.3 = ((bf16[16,40,768]{2,1,0:T(8,128)(2,1)}), bf16[16,40,768]{2,1,0:T(8,128)(2,1)S(1)}, u32[]{:S(2)}, u32[]{:S(2)}) async-start(bf16[16,40,768]{2,1,0:T(8,128)(2,1)} %bitcast.15), calls=%async_computation.3 | async-start | bytes 1966080 | tf_op jit(solution)/shard_map/all_to_all | solution.py:632
  123.6 20.1 %collective-permute-start.2 = (bf16[512,768]{1,0:T(8,128)(2,1)}, bf16[512,768]{1,0:T(8,128)(2,1)S(1)}, u32[]{:S(2)}, u32[]{:S(2)}) collective-permute-start(bf16[512,768]{1,0:T(8,128)(2,1)} %pick.2.own_ref), channel_id=1, source_target_pairs={{0,1},{1,0},{2,3},{3,2},{4,5},{5,4},{6,7},{7,6},{8,9},{9,8},{10,11... | collective-permute-start | bytes 2359304 | tf_op jit(solution)/shard_map/ppermute | solution.py:628
  149.2 13.8 %copy-start.3 = (bf16[16,40,768]{2,1,0:T(8,128)(2,1)}, bf16[16,40,768]{2,1,0:T(8,128)(2,1)S(1)}, u32[]{:S(2)}) copy-start(bf16[16,40,768]{2,1,0:T(8,128)(2,1)S(1)} %all-to-all-done.3) | copy-start | bytes 2949124
  163.0 5.1 %collective-permute-start.3 = (bf16[384,768]{1,0:T(8,128)(2,1)}, bf16[384,768]{1,0:T(8,128)(2,1)}, u32[]{:S(2)}, u32[]{:S(2)}) collective-permute-start(bf16[384,768]{1,0:T(8,128)(2,1)} %get-tuple-element.85), channel_id=1, source_target_pairs={{0,2},{2,0},{4,6},{6,4},{8,10},{10,8},{12,14},{14,12},{16,18},{18,... | collective-permute-start | bytes 1769480 | tf_op jit(solution)/shard_map/ppermute | solution.py:573
  163.1 8.2 %collective-permute-start.7 = (bf16[448,768]{1,0:T(8,128)(2,1)}, bf16[448,768]{1,0:T(8,128)(2,1)S(1)}, u32[]{:S(2)}, u32[]{:S(2)}) collective-permute-start(bf16[448,768]{1,0:T(8,128)(2,1)} %get-tuple-element.87), channel_id=1, source_target_pairs={{0,2},{2,0},{4,6},{6,4},{8,10},{10,8},{12,14},{14,12},{16,18},{18,... | collective-permute-start | bytes 2064392 | tf_op jit(solution)/shard_map/ppermute | solution.py:573
  163.6 30.6 %collective-permute-start.11 = (bf16[512,768]{1,0:T(8,128)(2,1)}, bf16[512,768]{1,0:T(8,128)(2,1)S(1)}, u32[]{:S(2)}, u32[]{:S(2)}) collective-permute-start(bf16[512,768]{1,0:T(8,128)(2,1)} %get-tuple-element.89.own_ref), channel_id=1, source_target_pairs={{0,1},{1,0},{2,3},{3,2},{4,5},{5,4},{6,7},{7,6},{8,9},{9,8},{10,11... | collective-permute-start | bytes 2359304 | tf_op jit(solution)/shard_map/ppermute | solution.py:628
  169.6 8.8 %collective-permute-start.4 = (bf16[192,768]{1,0:T(8,128)(2,1)S(1)}, bf16[192,768]{1,0:T(8,128)(2,1)S(1)}, u32[]{:S(2)}, u32[]{:S(2)}) collective-permute-start(bf16[192,768]{1,0:T(8,128)(2,1)S(1)} %broadcast_select_fusion.5), channel_id=1, source_target_pairs={{0,4},{2,6},{4,0},{6,2},{8,12},{10,14},{12,8},{14,10},{16,20},{18,... | collective-permute-start | bytes 884744 | tf_op jit(solution)/shard_map/ppermute | solution.py:573
  171.5 10.5 %collective-permute-start.8 = (bf16[224,768]{1,0:T(8,128)(2,1)S(1)}, bf16[224,768]{1,0:T(8,128)(2,1)S(1)}, u32[]{:S(2)}, u32[]{:S(2)}) collective-permute-start(bf16[224,768]{1,0:T(8,128)(2,1)S(1)} %broadcast_select_fusion.2), channel_id=1, source_target_pairs={{0,8},{2,10},{4,12},{6,14},{8,0},{10,2},{12,4},{14,6},{16,24},{18,... | collective-permute-start | bytes 1032200 | tf_op jit(solution)/shard_map/ppermute | solution.py:573
  178.5 5.7 %collective-permute-start.5 = (bf16[96,768]{1,0:T(8,128)(2,1)S(1)}, bf16[96,768]{1,0:T(8,128)(2,1)S(1)}, u32[]{:S(2)}, u32[]{:S(2)}) collective-permute-start(bf16[96,768]{1,0:T(8,128)(2,1)S(1)} %broadcast_select_fusion.11), channel_id=1, source_target_pairs={{0,8},{2,10},{4,12},{6,14},{8,0},{10,2},{12,4},{14,6},{16,24},{18,... | collective-permute-start | bytes 442376 | tf_op jit(solution)/shard_map/ppermute | solution.py:573
  182.1 5.5 %collective-permute-start.9 = (bf16[112,768]{1,0:T(8,128)(2,1)S(1)}, bf16[112,768]{1,0:T(8,128)(2,1)S(1)}, u32[]{:S(2)}, u32[]{:S(2)}) collective-permute-start(bf16[112,768]{1,0:T(8,128)(2,1)S(1)} %broadcast_select_fusion.8), channel_id=1, source_target_pairs={{0,4},{2,6},{4,0},{6,2},{8,12},{10,14},{12,8},{14,10},{16,20},{18,... | collective-permute-start | bytes 516104 | tf_op jit(solution)/shard_map/ppermute | solution.py:573
  184.3 7.7 %collective-permute-start.6 = (bf16[48,768]{1,0:T(8,128)(2,1)S(1)}, bf16[48,768]{1,0:T(8,128)(2,1)S(1)}, u32[]{:S(2)}, u32[]{:S(2)}) collective-permute-start(bf16[48,768]{1,0:T(8,128)(2,1)S(1)} %broadcast_select_fusion.17), channel_id=1, source_target_pairs={{0,16},{2,18},{4,20},{6,22},{8,24},{10,26},{12,28},{14,30},{16,0},... | collective-permute-start | bytes 221192 | tf_op jit(solution)/shard_map/ppermute | solution.py:573
  187.7 6.4 %collective-permute-start.10 = (bf16[56,768]{1,0:T(8,128)(2,1)S(1)}, bf16[56,768]{1,0:T(8,128)(2,1)S(1)}, u32[]{:S(2)}, u32[]{:S(2)}) collective-permute-start(bf16[56,768]{1,0:T(8,128)(2,1)S(1)} %broadcast_select_fusion.14), channel_id=1, source_target_pairs={{0,16},{2,18},{4,20},{6,22},{8,24},{10,26},{12,28},{14,30},{16,0},... | collective-permute-start | bytes 258056 | tf_op jit(solution)/shard_map/ppermute | solution.py:573
  194.2 19.6 %copy-start.7 = (bf16[512,768]{1,0:T(8,128)(2,1)}, bf16[512,768]{1,0:T(8,128)(2,1)S(1)}, u32[]{:S(2)}) copy-start(bf16[512,768]{1,0:T(8,128)(2,1)S(1)} %collective-permute-done.11.got_ref) | copy-start | bytes 2359300
  194.2 6.5 %collective-permute-start.13 = (bf16[48,768]{1,0:T(8,128)(2,1)S(1)}, bf16[48,768]{1,0:T(8,128)(2,1)S(1)}, u32[]{:S(2)}, u32[]{:S(2)}) collective-permute-start(bf16[48,768]{1,0:T(8,128)(2,1)S(1)} %add_convert_fusion.7), channel_id=1, source_target_pairs={{0,16},{2,18},{4,20},{6,22},{8,24},{10,26},{12,28},{14,30},{16,0},... | collective-permute-start | bytes 221192 | tf_op jit(solution)/shard_map/ppermute | solution.py:573
  195.6 6.2 %collective-permute-start.17 = (bf16[56,768]{1,0:T(8,128)(2,1)S(1)}, bf16[56,768]{1,0:T(8,128)(2,1)S(1)}, u32[]{:S(2)}, u32[]{:S(2)}) collective-permute-start(bf16[56,768]{1,0:T(8,128)(2,1)S(1)} %add_convert_fusion.6), channel_id=1, source_target_pairs={{0,16},{2,18},{4,20},{6,22},{8,24},{10,26},{12,28},{14,30},{16,0},... | collective-permute-start | bytes 258056 | tf_op jit(solution)/shard_map/ppermute | solution.py:573
  197.2 25.4 %collective-permute-start.12 = (bf16[512,768]{1,0:T(8,128)(2,1)}, bf16[512,768]{1,0:T(8,128)(2,1)}, u32[]{:S(2)}, u32[]{:S(2)}) collective-permute-start(bf16[512,768]{1,0:T(8,128)(2,1)} %pick.3.own_ref), channel_id=1, source_target_pairs={{0,1},{1,0},{2,3},{3,2},{4,5},{5,4},{6,7},{7,6},{8,9},{9,8},{10,11... | collective-permute-start | bytes 2359304 | tf_op jit(solution)/shard_map/ppermute | solution.py:628
  200.7 5.2 %collective-permute-start.14 = (bf16[96,768]{1,0:T(8,128)(2,1)S(1)}, bf16[96,768]{1,0:T(8,128)(2,1)S(1)}, u32[]{:S(2)}, u32[]{:S(2)}) collective-permute-start(bf16[96,768]{1,0:T(8,128)(2,1)S(1)} %pad_maximum_fusion.5), channel_id=1, source_target_pairs={{0,8},{2,10},{4,12},{6,14},{8,0},{10,2},{12,4},{14,6},{16,24},{18,... | collective-permute-start | bytes 442376 | tf_op jit(solution)/shard_map/ppermute | solution.py:573
  201.8 7.0 %collective-permute-start.18 = (bf16[112,768]{1,0:T(8,128)(2,1)S(1)}, bf16[112,768]{1,0:T(8,128)(2,1)S(1)}, u32[]{:S(2)}, u32[]{:S(2)}) collective-permute-start(bf16[112,768]{1,0:T(8,128)(2,1)S(1)} %pad_maximum_fusion.4), channel_id=1, source_target_pairs={{0,4},{2,6},{4,0},{6,2},{8,12},{10,14},{12,8},{14,10},{16,20},{18,... | collective-permute-start | bytes 516104 | tf_op jit(solution)/shard_map/ppermute | solution.py:573
  206.0 7.6 %collective-permute-start.15 = (bf16[192,768]{1,0:T(8,128)(2,1)S(1)}, bf16[192,768]{1,0:T(8,128)(2,1)S(1)}, u32[]{:S(2)}, u32[]{:S(2)}) collective-permute-start(bf16[192,768]{1,0:T(8,128)(2,1)S(1)} %pad_maximum_fusion.3), channel_id=1, source_target_pairs={{0,4},{2,6},{4,0},{6,2},{8,12},{10,14},{12,8},{14,10},{16,20},{18,... | collective-permute-start | bytes 884744 | tf_op jit(solution)/shard_map/ppermute | solution.py:573
  209.0 7.3 %collective-permute-start.19 = (bf16[224,768]{1,0:T(8,128)(2,1)S(1)}, bf16[224,768]{1,0:T(8,128)(2,1)S(1)}, u32[]{:S(2)}, u32[]{:S(2)}) collective-permute-start(bf16[224,768]{1,0:T(8,128)(2,1)S(1)} %pad_maximum_fusion.2), channel_id=1, source_target_pairs={{0,8},{2,10},{4,12},{6,14},{8,0},{10,2},{12,4},{14,6},{16,24},{18,... | collective-permute-start | bytes 1032200 | tf_op jit(solution)/shard_map/ppermute | solution.py:573
  213.8 12.8 %collective-permute-start.16 = (bf16[384,768]{1,0:T(8,128)(2,1)S(1)}, bf16[384,768]{1,0:T(8,128)(2,1)}, u32[]{:S(2)}, u32[]{:S(2)}) collective-permute-start(bf16[384,768]{1,0:T(8,128)(2,1)S(1)} %pad_maximum_fusion.1.a_ref), channel_id=1, source_target_pairs={{0,2},{2,0},{4,6},{6,4},{8,10},{10,8},{12,14},{14,12},{16,18},{18,... | collective-permute-start | bytes 1769480 | tf_op jit(solution)/shard_map/ppermute | solution.py:573
  216.5 10.1 %collective-permute-start.20 = (bf16[384,768]{1,0:T(8,128)(2,1)S(1)}, bf16[384,768]{1,0:T(8,128)(2,1)}, u32[]{:S(2)}, u32[]{:S(2)}) collective-permute-start(bf16[384,768]{1,0:T(8,128)(2,1)S(1)} %fusion), channel_id=1, source_target_pairs={{0,2},{2,0},{4,6},{6,4},{8,10},{10,8},{12,14},{14,12},{16,18},{18,... | collective-permute-start | bytes 1769480 | tf_op jit(solution)/shard_map/ppermute | solution.py:573
  221.1 5.4 %collective-permute-start.21 = (bf16[64,768]{1,0:T(8,128)(2,1)}, bf16[64,768]{1,0:T(8,128)(2,1)S(1)}, u32[]{:S(2)}, u32[]{:S(2)}) collective-permute-start(bf16[64,768]{1,0:T(8,128)(2,1)} %slice.70), channel_id=1, source_target_pairs={{0,1},{1,0},{2,3},{3,2},{4,5},{5,4},{6,7},{7,6},{8,9},{9,8},{10,11... | collective-permute-start | bytes 294920 | tf_op jit(solution)/shard_map/ppermute | solution.py:628
  (16 other events, 84.6 us)
where the time goes:
time: 238 us; the launch traced here: 237 us
  waiting for transfers between devices  88.8 us (37%)
  Pallas kernels  64.7 us (27%)
  starting transfers between devices  50.2 us (21%)
  matrix products  14 us (6%)
  local copies, waits for them, and re-layouts  10.7 us (4%)
  other arithmetic  7.63 us (3%)
    ppermute x6, waiting for transfers between devices, swapped(): return lax.ppermute(value, 'mp', swap)  31.7 us
    all_to_all x4, waiting for transfers between devices, to_experts(): lax.all_to_all(block, 'dp', split_axis=0, concat_axis=0, tiled=True)  28.6 us
    ppermute x16, waiting for transfers between devices, exchange(): return lax.ppermute(value, 'dp', [(i, i ^ 1 << bit) for i in range(count)])  28.5 us
    all_to_all x4, starting transfers between devices, to_experts(): lax.all_to_all(block, 'dp', split_axis=0, concat_axis=0, tiled=True)  26 us
    ppermute x16, starting transfers between devices, exchange(): return lax.ppermute(value, 'dp', [(i, i ^ 1 << bit) for i in range(count)])  17 us
    pallas_call x1, Pallas kernels, attend_back(): pl.pallas_call(attend_back_kernel, grid=(heads // 2,), in_specs=[scalars(...  13.8 us
    pallas_call x1, Pallas kernels, expert(): pl.pallas_call(expert_kernel, grid=(hidden // step,), in_specs=[whole((ro...  12.2 us
    dot_general x3, matrix products, contract_rows(): lax.dot_general(left, right, (((0,), (0,)), ((), ())), preferred_element_...  11.4 us
  transfers between devices with their start and end apart: 26, of which 18 were waited for; matrix products, arithmetic and copies ran while one was open for 9% of the time, Pallas kernels for 13%

commit v1 on v0

--- a/solution.py
+++ b/solution.py
@@ -10,7 +10,6 @@
 epsilon = 1e-06
 bf16 = jnp.bfloat16
 f32 = jnp.float32
-vmem_bytes = 62 * 1024 * 1024
 gelu_scale = 0.7978845608028654
 gelu_cubic = 0.044715
 
@@ -37,8 +36,8 @@
     return pl.BlockSpec(memory_space=pltpu.SMEM)
 
 
-def params():
-    return pltpu.CompilerParams(vmem_limit_bytes=vmem_bytes)
+def params(mib=62):
+    return pltpu.CompilerParams(vmem_limit_bytes=mib * 1024 * 1024)
 
 
 def cost(flops, moved):
@@ -51,7 +50,7 @@
 ):
     pair = pl.program_id(0)
     length = x_ref.shape[0]
-    buckets = table_ref.shape[0]
+    buckets = table_ref.shape[1]
     half = o_ref.shape[1] // 2
     scale = half ** (-0.5)
     blocks = length // 128
@@ -60,7 +59,7 @@
     def _():
         x = x_ref[...].astype(f32)
         inverse = lax.rsqrt(jnp.mean(x * x, axis=-1, keepdims=True) + epsilon)
-        n_ref[...] = (x * inverse * gain_ref[...]).astype(bf16)
+        n_ref[...] = (x * inverse * gain_ref[...][None, :]).astype(bf16)
         blank = jnp.zeros((8, length), jnp.int32)
         ahead = jnp.concatenate([jnp.broadcast_to(first_ref[0:1, :], (8, length)), blank], axis=1)
         behind = jnp.concatenate([jnp.broadcast_to(last_ref[7:8, :], (8, length)), blank], axis=1)
@@ -88,7 +87,7 @@
         mine = (lane < half) if h == 0 else (lane >= half)
         spread = jnp.zeros(ids.shape, f32)
         for b in range(buckets):
-            spread = jnp.where(ids == b, table_ref[b, head], spread)
+            spread = jnp.where(ids == b, table_ref[head, b], spread)
         for a in range(16):
             left = 127 - 8 * a
             bias_ref[8 * a : 8 * a + 8, :] = pltpu.roll(spread, 2 * length - left, 1)
@@ -98,7 +97,7 @@
             start = 128 * (blocks - 1 - i)
             s = contract_last(q_head[rows], k) * scale + bias_ref[:, start : start + length]
             e = jnp.exp(s - jnp.max(s, axis=-1, keepdims=True))
-            p = e / jnp.sum(e, axis=-1, keepdims=True)
+            p = e * (1.0 / jnp.sum(e, axis=-1, keepdims=True))
             p_ref[h, rows, :] = p.astype(bf16)
         part = dot(p_ref[h], jnp.where(mine, v, zero))
         out = part if out is None else out + part
@@ -108,7 +107,7 @@
 def attend(x, gain, wq, wk, wv, table, bucket_ids):
     length, width = x.shape
     local = wq.shape[1]
-    heads = table.shape[1]
+    heads = table.shape[0]
     span = 2 * local // heads
     column = pl.BlockSpec((length, span), lambda j: (0, j))
     weight = pl.BlockSpec((width, span), lambda j: (0, j))
@@ -117,7 +116,7 @@
         attend_kernel,
         grid=(heads // 2,),
         in_specs=[
-            whole((length, width)), whole((1, width)), weight, weight, weight, scalars(),
+            whole((length, width)), whole((width,)), weight, weight, weight, scalars(),
             pl.BlockSpec((8, length), lambda j: (0, 0)),
             pl.BlockSpec((8, length), lambda j: (length // 8 - 1, 0)),
         ],
@@ -139,9 +138,9 @@
 
 
 def attend_back_kernel(
-    side_ref, do_ref, q_ref, k_ref, v_ref, p_ref, wq_ref, wk_ref, wv_ref,
-    o_ref, da_ref, x_ref, gain_ref, ids_ref, router_ref, norm2_ref, buckets_ref,
-    dn_ref, keep_a_ref, send_a_ref, keep_b_ref, send_b_ref,
+    buckets, side_ref, do_ref, q_ref, k_ref, v_ref, p_ref, wq_ref, wk_ref, wv_ref,
+    o_ref, da_ref, x_ref, gain_ref, ids_ref, router_ref, norm2_ref,
+    dn_ref, keep_ref, send_ref,
     ds_ref, acc_ref, total_ref, n_ref, small_ref,
 ):
     pair = pl.program_id(0)
@@ -151,16 +150,17 @@
     half = span // 2
     scale = half ** (-0.5)
     blocks = length // 128
-    buckets = buckets_ref.shape[0]
     experts = router_ref.shape[0]
-    local = keep_a_ref.shape[0]
+    extra = small_ref.shape[0]
+    local = keep_ref.shape[0] // 2 - extra
+    quarter = local // 2
     even = side_ref[0] == 0
 
     @pl.when(pair == 0)
     def _():
         x = x_ref[...].astype(f32)
         inverse = lax.rsqrt(jnp.mean(x * x, axis=-1, keepdims=True) + epsilon)
-        n_ref[...] = (x * inverse * gain_ref[...]).astype(bf16)
+        n_ref[...] = (x * inverse * gain_ref[...][None, :]).astype(bf16)
         small_ref[...] = jnp.zeros_like(small_ref)
         small_ref[0:experts, :] = router_ref[...]
         small_ref[experts + 1 : experts + 2, :] = norm2_ref[...]
@@ -223,12 +223,18 @@
     here = pl.ds(pl.multiple_of(pair * span, span), span)
     grad_k = dot(dk_turned, normed).astype(bf16)
     grad_v = dot(dv_turned, normed).astype(bf16)
-    keep_a_ref[here, :] = jnp.where(even, grad_k, grad_v)
-    send_a_ref[here, :] = jnp.where(even, grad_v, grad_k)
+    keep_ref[here, :] = jnp.where(even, grad_k, grad_v)
+    send_ref[here, :] = jnp.where(even, grad_v, grad_k)
     grad_q = dot(dq_low.T, normed).astype(bf16)
     grad_o = dot(o_ref[...].T, da_ref[...]).astype(bf16)
-    keep_b_ref[here, :] = jnp.where(even, grad_q, grad_o)
-    send_b_ref[here, :] = jnp.where(even, grad_o, grad_q)
+    keep = jnp.where(even, grad_q, grad_o)
+    send = jnp.where(even, grad_o, grad_q)
+    for i in range(0, span, 64):
+        row = pair * span + i
+        skip = jnp.where(row >= quarter, extra, 0)
+        after = pl.ds(pl.multiple_of(local + row + skip, 64), 64)
+        keep_ref[after, :] = keep[i : i + 64]
+        send_ref[after, :] = send[i : i + 64]
 
     @pl.when(pair == 0)
     def _():
@@ -248,15 +254,16 @@
             total * x * inverse, axis=0, keepdims=True
         )
         small = small_ref[...].astype(bf16)
-        keep_b_ref[local:, :] = small
-        send_b_ref[local:, :] = small
+        for start in (local + quarter, 2 * local + extra):
+            keep_ref[start : start + extra, :] = small
+            send_ref[start : start + extra, :] = small
 
 
 def small_rows(experts, heads):
     return -(-(experts + 2 + heads) // 64) * 64
 
 
-def attend_back(side, do, q, k, v, p, wq, wk, wv, o, da, x, gain, ids, router, norm2, table):
+def attend_back(side, do, q, k, v, p, wq, wk, wv, o, da, x, gain, ids, router, norm2, buckets):
     length, local = do.shape
     width = wq.shape[0]
     heads = p.shape[0]
@@ -265,24 +272,22 @@
     extra = small_rows(experts, heads)
     column = pl.BlockSpec((length, span), lambda j: (0, j))
     weight = pl.BlockSpec((width, span), lambda j: (0, j))
-    part_a = jax.ShapeDtypeStruct((local, width), bf16)
-    part_b = jax.ShapeDtypeStruct((local + extra, width), bf16)
+    part = jax.ShapeDtypeStruct((2 * (local + extra), width), bf16)
     return pl.pallas_call(
-        attend_back_kernel,
+        functools.partial(attend_back_kernel, buckets),
         grid=(heads // 2,),
         in_specs=[
             scalars(), column, column, column, column,
             pl.BlockSpec((2, length, length), lambda j: (j, 0, 0)),
             weight, weight, weight, column,
-            whole((length, width)), whole((length, width)), whole((1, width)),
-            whole(ids.shape), whole((experts, width)), whole((1, width)), whole(table.shape),
+            whole((length, width)), whole((length, width)), whole((width,)),
+            whole(ids.shape), whole((experts, width)), whole((1, width)),
         ],
         out_specs=[
-            whole((length, width)), whole(part_a.shape), whole(part_a.shape),
-            whole(part_b.shape), whole(part_b.shape),
+            whole((length, width)), whole(part.shape), whole(part.shape),
         ],
         out_shape=[
-            jax.ShapeDtypeStruct((length, width), bf16), part_a, part_a, part_b, part_b,
+            jax.ShapeDtypeStruct((length, width), bf16), part, part,
         ],
         scratch_shapes=[
             pltpu.VMEM((length, length), bf16),
@@ -294,7 +299,7 @@
         compiler_params=params(),
         cost_estimate=cost(12_000_000_000, 9_000_000),
         name="attend_back",
-    )(side, do, q, k, v, p, wq, wk, wv, o, da, x, gain, ids, router, norm2, table)
+    )(side, do, q, k, v, p, wq, wk, wv, o, da, x, gain, ids, router, norm2)
 
 
 def hits(ids, count, axis):
@@ -302,68 +307,72 @@
     return jnp.where(lax.broadcasted_iota(jnp.int32, shape, axis) == ids, 1.0, 0.0).astype(bf16)
 
 
-def place_kernel(ids_ref, rows_ref, out_ref):
-    out_ref[...] = dot(hits(ids_ref[...], out_ref.shape[0], 0), rows_ref[...]).astype(bf16)
-
-
-def place(ids, rows, places):
+def row_block(block, width, first=0):
+    return pl.BlockSpec((block, width), lambda i: (first + i, 0))
+
+
+def row_block(block, width, first=0):
+    return pl.BlockSpec((block, width), lambda i: (first + i, 0))
+
+
+def place_kernel(capacity, expert_ref, slot_ref, rows_ref, out_ref):
+    ids = expert_ref[...] * capacity + slot_ref[...]
+    out_ref[...] = dot(hits(ids, out_ref.shape[0], 0), rows_ref[...]).astype(bf16)
+
+
+def place(capacity, ids, rows, places):
     return pl.pallas_call(
-        place_kernel,
+        functools.partial(place_kernel, capacity),
         out_shape=jax.ShapeDtypeStruct((places, rows.shape[1]), bf16),
         compiler_params=params(),
         cost_estimate=cost(1_000_000_000, 3_000_000),
         name="place",
-    )(ids, rows)
-
-
-def pick_kernel(ids_ref, slots_ref, out_ref):
-    out_ref[...] = dot(hits(ids_ref[...], slots_ref.shape[0], 1), slots_ref[...]).astype(bf16)
-
-
-def pick(ids, slots):
+    )(*ids, rows)
+
+
+def pick_kernel(ids_ref, slots_ref, *out_refs):
+    first = 0
+    for out_ref in out_refs:
+        count = out_ref.shape[0]
+        ids = ids_ref[first : first + count, :]
+        out_ref[...] = dot(hits(ids, slots_ref.shape[0], 1), slots_ref[...]).astype(bf16)
+        first += count
+
+
+def pick(ids, slots, parts):
+    part = jax.ShapeDtypeStruct((ids.shape[0] // parts, slots.shape[1]), bf16)
     return pl.pallas_call(
         pick_kernel,
-        out_shape=jax.ShapeDtypeStruct((ids.shape[0], slots.shape[1]), bf16),
+        out_shape=[part] * parts,
         compiler_params=params(),
         cost_estimate=cost(1_000_000_000, 3_000_000),
         name="pick",
     )(ids, slots)
 
 
-def finish_kernel(own_ref, got_ref, hmid_ref, out_ref):
-    picked = own_ref[...].astype(f32) + got_ref[...].astype(f32)
-    out_ref[...] = (hmid_ref[...] + picked).astype(bf16)
-
-
-def finish(own, got, hmid):
-    return pl.pallas_call(
-        finish_kernel,
-        out_shape=jax.ShapeDtypeStruct(hmid.shape, bf16),
-        compiler_params=params(),
-        cost_estimate=cost(1_000_000, 5_000_000),
-        name="finish",
-    )(own, got, hmid)
-
-
 def middle_kernel(
-    mp_ref, o_ref, o_other_ref, w_ref, w_other_ref, x_ref, gain_ref, ids_ref, hmid_ref, out_ref
+    capacity, place_ref, o_ref, o_other_ref, w_ref, w_near_ref, w_far_ref, x_ref, gain_ref,
+    expert_ref, slot_ref, hmid_ref, out_ref,
 ):
-    low = mp_ref[0] == 0
+    low = place_ref[0] == 0
+    even = place_ref[1] == 0
     o, o_other = o_ref[...], o_other_ref[...]
-    w, w_other = w_ref[...], w_other_ref[...]
+    w, near, far = w_ref[...], w_near_ref[...], w_far_ref[...]
+    w_other = jnp.concatenate([jnp.where(even, near, far), jnp.where(even, far, near)], axis=0)
     heads = jnp.concatenate([jnp.where(low, o, o_other), jnp.where(low, o_other, o)], axis=1)
     weight = jnp.concatenate([jnp.where(low, w, w_other), jnp.where(low, w_other, w)], axis=0)
     hmid = x_ref[...].astype(f32) + dot(heads, weight)
     hmid_ref[...] = hmid
     inverse = lax.rsqrt(jnp.mean(hmid * hmid, axis=-1, keepdims=True) + epsilon)
-    normed = (hmid * inverse * gain_ref[...]).astype(bf16)
-    out_ref[...] = dot(hits(ids_ref[...], out_ref.shape[0], 0), normed).astype(bf16)
-
-
-def middle(mp, o, o_other, w, w_other, x, gain, ids, places):
+    normed = (hmid * inverse * gain_ref[...][None, :]).astype(bf16)
+    ids = expert_ref[...] * capacity + slot_ref[...]
+    out_ref[...] = dot(hits(ids, out_ref.shape[0], 0), normed).astype(bf16)
+
+
+def middle(capacity, where, o, o_other, w, w_near, w_far, x, gain, ids, places):
     return pl.pallas_call(
-        middle_kernel,
-        in_specs=[scalars()] + [pl.BlockSpec(memory_space=pltpu.VMEM)] * 7,
+        functools.partial(middle_kernel, capacity),
+        in_specs=[scalars()] + [pl.BlockSpec(memory_space=pltpu.VMEM)] * 9,
         out_shape=[
             jax.ShapeDtypeStruct(x.shape, f32),
             jax.ShapeDtypeStruct((places, x.shape[1]), bf16),
@@ -371,103 +380,145 @@
         compiler_params=params(),
         cost_estimate=cost(2_000_000_000, 6_000_000),
         name="middle",
-    )(mp, o, o_other, w, w_other, x, gain, ids)
+    )(where, o, o_other, w, w_near, w_far, x, gain, *ids)
 
 
 def middle_back_kernel(
-    own_ref, got_ref, hmid_ref, c_ref, gain_ref, w_ref, dh_ref, da_ref, do_ref, norm_ref
+    own_ref, got_ref, hmid_ref, c_ref, gain_ref, w_ref, *refs
 ):
+    dh_ref, da_ref, do_ref, norm_ref = refs[-4:]
     hmid = hmid_ref[...]
     dn = own_ref[...].astype(f32) + got_ref[...].astype(f32)
     inverse = lax.rsqrt(jnp.mean(hmid * hmid, axis=-1, keepdims=True) + epsilon)
-    scaled = dn * gain_ref[...]
+    scaled = dn * gain_ref[...][None, :]
     inner = jnp.mean(scaled * hmid, axis=-1, keepdims=True)
     dh = c_ref[...].astype(f32) + inverse * scaled - hmid * (inverse * inverse * inverse * inner)
     dh_ref[...] = dh
     da = dh.astype(bf16)
     da_ref[...] = da
     do_ref[...] = contract_last(da, w_ref[...]).astype(bf16)
-    norm_ref[...] = jnp.sum(dn * hmid * inverse, axis=0, keepdims=True)
-
-
-def middle_back(own, got, hmid, c, gain, w):
-    tokens, width = own.shape
+    norm = jnp.sum(dn * hmid * inverse, axis=0, keepdims=True)
+    before = refs[3][...] if len(refs) > 4 else jnp.zeros_like(norm)
+
+    @pl.when(pl.program_id(0) == 0)
+    def _():
+        norm_ref[...] = before + norm
+
+    @pl.when(pl.program_id(0) > 0)
+    def _():
+        norm_ref[...] += norm
+
+
+def middle_back(first, own, got, hmid, c, gain, w, before=()):
+    count, width = own.shape
+    tokens = hmid.shape[0]
+    local = w.shape[0]
+    block = count
+    here = first // block
+    anywhere = pl.BlockSpec(memory_space=pl.ANY)
     return pl.pallas_call(
         middle_back_kernel,
+        grid=(count // block,),
+        in_specs=[
+            row_block(block, width), row_block(block, width),
+            row_block(block, width, here), row_block(block, width, here),
+            whole(gain.shape), whole(w.shape),
+        ] + ([anywhere] * 3 + [whole((1, width))] if before else []),
+        out_specs=[
+            row_block(block, width, here), row_block(block, width, here),
+            row_block(block, local, here), whole((1, width)),
+        ],
         out_shape=[
             jax.ShapeDtypeStruct((tokens, width), f32),
             jax.ShapeDtypeStruct((tokens, width), bf16),
-            jax.ShapeDtypeStruct((tokens, w.shape[0]), bf16),
+            jax.ShapeDtypeStruct((tokens, local), bf16),
             jax.ShapeDtypeStruct((1, width), f32),
         ],
+        input_output_aliases={6: 0, 7: 1, 8: 2} if before else {},
         compiler_params=params(),
         cost_estimate=cost(1_000_000_000, 6_000_000),
         name="middle_back",
-    )(own, got, hmid, c, gain, w)
-
-
-def input_back_kernel(own_ref, got_ref, x_ref, dh_ref, gain_ref, out_ref):
+    )(own, got, hmid, c, gain, w, *before)
+
+
+def output_kernel(
+    place_ref, own_ref, got_ref, x_ref, dh_ref, gain_ref, y_ref, y_other_ref, hmid_ref,
+    grad_ref, out_ref,
+):
+    low = place_ref[0] == 0
     x = x_ref[...].astype(f32)
     dn = own_ref[...].astype(f32) + got_ref[...].astype(f32)
     inverse = lax.rsqrt(jnp.mean(x * x, axis=-1, keepdims=True) + epsilon)
-    scaled = dn * gain_ref[...]
+    scaled = dn * gain_ref[...][None, :]
     inner = jnp.mean(scaled * x, axis=-1, keepdims=True)
-    out_ref[...] = dh_ref[...] + inverse * scaled - x * (inverse * inverse * inverse * inner)
-
-
-def input_back(own, got, x, dh, gain):
+    grad_ref[...] = dh_ref[...] + inverse * scaled - x * (inverse * inverse * inverse * inner)
+    y, y_other = y_ref[...], y_other_ref[...]
+    moved = jnp.concatenate([jnp.where(low, y, y_other), jnp.where(low, y_other, y)], axis=1)
+    out_ref[...] = (hmid_ref[...] + moved.astype(f32)).astype(bf16)
+
+
+def outputs(where, own, got, x, dh, gain, y, y_other, hmid):
     return pl.pallas_call(
-        input_back_kernel,
-        out_shape=jax.ShapeDtypeStruct(dh.shape, f32),
+        output_kernel,
+        in_specs=[scalars()] + [pl.BlockSpec(memory_space=pltpu.VMEM)] * 8,
+        out_shape=[
+            jax.ShapeDtypeStruct(dh.shape, f32),
+            jax.ShapeDtypeStruct(x.shape, bf16),
+        ],
         compiler_params=params(),
-        cost_estimate=cost(100_000_000, 6_000_000),
-        name="input_back",
-    )(own, got, x, dh, gain)
+        cost_estimate=cost(100_000_000, 10_000_000),
+        name="outputs",
+    )(where, own, got, x, dh, gain, y, y_other, hmid)
+
+
+def split(value, low):
+    n = value.shape[0] // 2
+    first, second = value[:n], value[n:]
+    return jnp.where(low, first, second), jnp.where(low, second, first)
+
+
+def pair_up(value, got, low):
+    return jnp.concatenate([jnp.where(low, value, got), jnp.where(low, got, value)], axis=0)
 
 
 def unpack_kernel(
-    side_ref, a_ref, a_got_ref, b_ref, b_got_ref, s_got_ref,
+    experts, place_ref, a_ref, a_got_ref, b_ref, b_got_ref, small_ref, s_got_ref,
     q_ref, k_ref, v_ref, o_ref, router_ref, table_ref, norm1_ref, norm2_ref,
 ):
-    even = side_ref[0] == 0
-    local, width = a_ref.shape
-    experts = router_ref.shape[1]
-    buckets, heads = table_ref.shape
+    even = place_ref[1] == 0
+    heads, buckets = table_ref.shape
     a, a_got = a_ref[...], a_got_ref[...]
-    b, b_got = b_ref[0:local, :], b_got_ref[...]
+    b, b_got = b_ref[...], b_got_ref[...]
     k_ref[...] = jnp.where(even, a, a_got).T.astype(f32)
     v_ref[...] = jnp.where(even, a_got, a).T.astype(f32)
     q_ref[...] = jnp.where(even, b, b_got).T.astype(f32)
     o_ref[...] = jnp.where(even, b_got, b).astype(f32)
-    small = b_ref[local:, :].astype(f32)
+    small = small_ref[...].astype(f32)
     both = small + s_got_ref[...].astype(f32)
-    pad = jnp.zeros((-small.shape[0] % 128, width), f32)
-    router_ref[...] = jnp.concatenate([both, pad], axis=0).T[:, :experts]
-    norm1_ref[...] = both[experts : experts + 1]
-    norm2_ref[...] = small[experts + 1 : experts + 2]
-    lines = small[experts + 2 : experts + 2 + heads, 0:128]
-    pad = jnp.zeros((128 - heads, 128), f32)
-    table_ref[...] = jnp.concatenate([lines, pad], axis=0).T[:buckets, :heads]
-
-
-def unpack(side, a, a_got, b, b_got, s_got, experts, buckets, heads):
+    router_ref[...] = both[:experts]
+    norm1_ref[...] = both[experts]
+    norm2_ref[...] = small[experts + 1]
+    table_ref[...] = small[experts + 2 : experts + 2 + heads, :buckets]
+
+
+def unpack(where, a, a_got, b, b_got, small, s_got, experts, buckets, heads):
     local, width = a.shape
     turned = jax.ShapeDtypeStruct((width, local), f32)
+    flat = jax.ShapeDtypeStruct((width,), f32)
     return pl.pallas_call(
-        unpack_kernel,
-        in_specs=[scalars()] + [pl.BlockSpec(memory_space=pltpu.VMEM)] * 5,
+        functools.partial(unpack_kernel, experts),
+        in_specs=[scalars()] + [pl.BlockSpec(memory_space=pltpu.VMEM)] * 6,
         out_shape=[
             turned, turned, turned,
             jax.ShapeDtypeStruct((local, width), f32),
-            jax.ShapeDtypeStruct((width, experts), f32),
-            jax.ShapeDtypeStruct((buckets, heads), f32),
-            jax.ShapeDtypeStruct((1, width), f32),
-            jax.ShapeDtypeStruct((1, width), f32),
+            jax.ShapeDtypeStruct((experts, width), f32),
+            jax.ShapeDtypeStruct((heads, buckets), f32),
+            flat, flat,
         ],
         compiler_params=params(),
         cost_estimate=cost(100_000_000, 8_000_000),
         name="unpack",
-    )(side, a, a_got, b, b_got, s_got)
+    )(where, a, a_got, b, b_got, small, s_got)
 
 
 def expert_kernel(
@@ -485,7 +536,7 @@
         router = router_ref[...]
         high = router.astype(bf16)
         rest = (router - high.astype(f32)).astype(bf16)
-        logits = dot(x_ref[...], high) + dot(x_ref[...], rest)
+        logits = contract_last(x_ref[...], high) + contract_last(x_ref[...], rest)
         e = jnp.exp(logits - jnp.max(logits, axis=-1, keepdims=True))
         probs = e / jnp.sum(e, axis=-1, keepdims=True)
         gate = jnp.sum(jnp.where(hot, probs, 0.0), axis=-1, keepdims=True)
@@ -524,14 +575,14 @@
         dlog = inner_ref[...] * (hot.astype(f32) - probs_ref[...])
         dlog_ref[...] = dlog
         dx_ref[...] = (
-            total_ref[...] + contract_last(dlog.astype(bf16), router_ref[...].astype(bf16))
+            total_ref[...] + dot(dlog.astype(bf16), router_ref[...].astype(bf16))
         ).astype(bf16)
 
 
 def expert(x, c, w_in, w_out, router, mine):
     rows, width = x.shape
     hidden = w_in.shape[1]
-    experts = router.shape[1]
+    experts = router.shape[0]
     step = 512 if hidden % 512 == 0 else hidden
     return pl.pallas_call(
         expert_kernel,
@@ -540,7 +591,7 @@
             whole((rows, width)), whole((rows, width)),
             pl.BlockSpec((width, step), lambda j: (0, j)),
             pl.BlockSpec((step, width), lambda j: (j, 0)),
-            whole((width, experts)), scalars(),
+            whole((experts, width)), scalars(),
         ],
         out_specs=[
             whole((rows, width)),
@@ -573,24 +624,8 @@
     return lax.ppermute(value, "dp", [(i, i ^ (1 << bit)) for i in range(count)])
 
 
-def side_of(bit):
-    return (lax.axis_index("dp") >> bit) & 1
-
-
 def add(left, right):
     return (left.astype(f32) + right.astype(f32)).astype(left.dtype)
-
-
-def halves(value, bit):
-    n = value.shape[0] // 2
-    first, second = value[:n], value[n:]
-    low = side_of(bit) == 0
-    return jnp.where(low, first, second), jnp.where(low, second, first)
-
-
-def join(value, got, bit):
-    low = side_of(bit) == 0
-    return jnp.concatenate([jnp.where(low, value, got), jnp.where(low, got, value)])
 
 
 def shards(
@@ -621,95 +656,114 @@
     mp = lax.axis_index("mp").astype(jnp.int32)
     dp = lax.axis_index("dp").astype(jnp.int32)
     side = (dp & 1)[None]
-    gain1 = norm1_gain[None, :]
-    gain2 = norm2_gain[None, :]
+    where = jnp.stack([mp] + [(dp >> bit) & 1 for bit in range(bits)])
 
     def swapped(value):
         return lax.ppermute(value, "mp", swap)
 
     def to_experts(rows):
-        block = rows.reshape(experts, capacity, width)
+        block = rows.reshape(experts, capacity, -1)
         return lax.all_to_all(block, "dp", split_axis=0, concat_axis=0, tiled=True).reshape(
-            places, width
+            places, -1
         )
 
-    flat_slot = expert_ids * capacity + slot_ids
-    slot_row = flat_slot[None, :]
-    slot_column = flat_slot[:, None]
-
-    w_output_other = swapped(w_output)
-    c_here = to_experts(place(slot_row, out_grad, places))
+    slot_row = (expert_ids[None, :], slot_ids[None, :])
+    slot_column = (expert_ids * capacity + slot_ids)[:, None]
+
+    w_near, _ = split(w_output, (dp & 1) == 0)
+    w_near = swapped(w_near)
+    c_here = to_experts(place(capacity, slot_row, out_grad, places))
     o, q, k, v, p, ids = attend(
-        hidden_in, gain1, w_query, w_key, w_value, bias_table, bucket_ids
-    )
-    o, w_output_other = lax.optimization_barrier((o, w_output_other))
+        hidden_in, norm1_gain, w_query, w_key, w_value, bias_table.T, bucket_ids
+    )
+    o, w_near = lax.optimization_barrier((o, w_near))
     o_other = swapped(o)
+    w_far = exchange(w_near, count, 0)
     hmid, x_send = middle(
-        mp[None], o, o_other, w_output, w_output_other, hidden_in, gain2, slot_row, places
+        capacity, where, o, o_other, w_output, w_near, w_far, hidden_in, norm2_gain, slot_row, places
     )
     x_here = to_experts(x_send)
 
-    dx, hid, dpre, deo, gate, dlog = expert(x_here, c_here, w_in[0], w_out[0], router, dp[None])
+    dx, hid, dpre, deo, gate, dlog = expert(x_here, c_here, w_in[0], w_out[0], router.T, dp[None])
     dx_home = to_experts(dx)
     eo = (gate * dot(hid, w_out[0])).astype(bf16)
+    eo_mine = jnp.where(mp == 0, eo[:, : width // 2], eo[:, width // 2 :])
+    eo_other = swapped(jnp.where(mp == 0, eo[:, width // 2 :], eo[:, : width // 2]))
     grad_w_out = contract_rows(hid, deo)[None]
     grad_w_in = contract_rows(x_here, dpre)[None]
     grad_router = contract_rows(dlog, x_here.astype(f32), lax.Precision.HIGHEST)
-    dx_home, eo, grad_w_out, grad_w_in, grad_router = lax.optimization_barrier(
-        (dx_home, eo, grad_w_out, grad_w_in, grad_router)
-    )
-
-    dn2 = pick(slot_column, dx_home)
-    dn2_other = swapped(dn2)
+    eo = add(eo_mine, eo_other)
+    dx_home, grad_w_out, grad_w_in, grad_router = lax.optimization_barrier(
+        (dx_home, grad_w_out, grad_w_in, grad_router)
+    )
+
+    low, high = pick(slot_column, dx_home, 2)
+    low, high, eo = lax.optimization_barrier((low, high, eo))
+    low_other = swapped(low)
+    high_other = swapped(high)
     eo_home = to_experts(eo)
-    dh, da, do, grad_norm2 = middle_back(dn2, dn2_other, hmid, out_grad, gain2, w_output)
-    do, eo_home = lax.optimization_barrier((do, eo_home))
-    dn1, keep_a, send_a, keep_b, send_b = attend_back(
-        side, do, q, k, v, p, w_query, w_key, w_value, o, da, hidden_in, gain1, ids,
-        grad_router, grad_norm2, bias_table,
-    )
+    before = middle_back(0, low, low_other, hmid, out_grad, norm2_gain, w_output)
+    dh, da, do, grad_norm2 = middle_back(
+        tokens // 2, high, high_other, hmid, out_grad, norm2_gain, w_output, before
+    )
+    dn1, keep, send = attend_back(
+        side, do, q, k, v, p, w_query, w_key, w_value, o, da, hidden_in, norm1_gain, ids,
+        grad_router, grad_norm2, buckets,
+    )
+    dn1, keep, send, eo_home = lax.optimization_barrier((dn1, keep, send, eo_home))
     dn1_other = swapped(dn1)
 
+    local = q.shape[1]
     order_a = tuple(range(1, bits))
     order_b = (2, 1) + tuple(range(3, bits))
-    a = add(keep_a, exchange(send_a, count, 0))
-    b = add(keep_b, exchange(send_b, count, 0))
-    picked = pick(slot_column, eo_home)
-    for bit_a, bit_b in zip(order_a, order_b):
-        keep_a, send_a = halves(a, bit_a)
-        keep_b, send_b = halves(b, bit_b)
+    total = add(keep, exchange(send, count, 0))
+    a, b = total[:local], total[local:]
+    for stage, (bit_a, bit_b) in enumerate(zip(order_a[:-1], order_b[:-1])):
+        keep_a, send_a = split(a, where[bit_a + 1] == 0)
+        keep_b, send_b = split(b, where[bit_b + 1] == 0)
         got_a = exchange(send_a, count, bit_a)
         got_b = exchange(send_b, count, bit_b)
+        if stage == 0:
+            (picked,) = pick(slot_column, eo_home, 1)
+            got_a, got_b, picked = lax.optimization_barrier((got_a, got_b, picked))
         a, b = add(keep_a, got_a), add(keep_b, got_b)
-    a, b, picked, dn1_other = lax.optimization_barrier((a, b, picked, dn1_other))
+    got_a = exchange(a, count, order_a[-1])
+    got_b = exchange(b, count, order_b[-1])
+    got_a, got_b, dn1_other = lax.optimization_barrier((got_a, got_b, dn1_other))
     picked_other = swapped(picked)
-    grad_hidden = input_back(dn1, dn1_other, hidden_in, dh, gain1)
-    for bit_a, bit_b in zip(order_a[::-1], order_b[::-1]):
+    a, b = add(a, got_a), add(b, got_b)
+    for bit_a, bit_b in zip(order_a[-2::-1], order_b[-2::-1]):
         got_a = exchange(a, count, bit_a)
         got_b = exchange(b, count, bit_b)
-        a, b = join(a, got_a, bit_a), join(b, got_b, bit_b)
-    local = a.shape[0]
-    a_got = exchange(a, count, 0)
-    b_got = exchange(b[:local], count, 0)
-    small_got = swapped(b[local:])
-    hidden_out = finish(picked, picked_other, hmid)
-    hidden_out, grad_hidden, a_got, b_got, small_got = lax.optimization_barrier(
-        (hidden_out, grad_hidden, a_got, b_got, small_got)
-    )
+        if bit_b == 1:
+            grad_hidden, hidden_out = outputs(
+                where, dn1, dn1_other, hidden_in, dh, norm1_gain, picked, picked_other, hmid
+            )
+            got_a, got_b, grad_hidden, hidden_out = lax.optimization_barrier(
+                (got_a, got_b, grad_hidden, hidden_out)
+            )
+        a = pair_up(a, got_a, where[bit_a + 1] == 0)
+        b = pair_up(b, got_b, where[bit_b + 1] == 0)
+        if bit_b == 1:
+            small = b[local // 2 :]
+            b = b[: local // 2]
+            small_other = swapped(small)
+    a, b, small_other = lax.optimization_barrier((a, b, small_other))
     grad_q, grad_k, grad_v, grad_w_output, grad_router, grad_table, grad_norm1, grad_norm2 = unpack(
-        side, a, a_got, b, b_got, small_got, experts, buckets, heads
+        where, a, exchange(a, count, 0), b, exchange(b, count, 0), small, small_other,
+        experts, buckets, heads,
     )
     return (
         hidden_out,
         grad_hidden,
-        grad_norm1[0],
+        grad_norm1,
         grad_q,
         grad_k,
         grad_v,
         grad_w_output,
-        grad_table,
-        grad_norm2[0],
-        grad_router,
+        grad_table.T,
+        grad_norm2,
+        grad_router.T,
         grad_w_in,
         grad_w_out,
     )

time: 238 us -> 220 us (0.924)
  waiting for transfers between devices: 88.8 us -> 77 us
  local copies, waits for them, and re-layouts: 10.7 us -> 7.95 us
    ppermute x6 -> x8, waiting for transfers between devices: 31.7 us -> 20 us  [swapped(): return lax.ppermute(value, 'mp', swap)]
    all_to_all x4, waiting for transfers between devices: 28.6 us -> 23.9 us  [to_experts(): lax.all_to_all(block, 'dp', split_axis=0, concat_axis=0, tiled=True)]
    ppermute x16 -> x14, waiting for transfers between devices: 28.5 us -> 33.1 us  [exchange(): return lax.ppermute(value, 'dp', [(i, i ^ 1 << bit) for i in range(count)])]
    convert_element_type x8, other arithmetic: 2.04 us -> 5.12 us  [add(): return (left.astype(f32) + right.astype(f32)).astype(left.dtype)]
    pallas_call x2 -> x0, other arithmetic: 2.56 us -> none  [unpack(): pl.pallas_call(unpack_kernel, in_specs=[scalars()] + [pl.BlockSpec(memory...]
    unnamed x48 -> x52, local copies, waits for them, and re-layouts: 8 us -> 6.41 us
    ppermute x16 -> x14, starting transfers between devices: 17 us -> 15.7 us  [exchange(): return lax.ppermute(value, 'dp', [(i, i ^ 1 << bit) for i in range(count)])]
    ppermute x6 -> x8, starting transfers between devices: 7.15 us -> 6.31 us  [swapped(): return lax.ppermute(value, 'mp', swap)]
  transfers between devices with their start and end apart: 26 -> 26, of which waited for: 18 -> 15; matrix products, arithmetic and copies ran while one was open for 9% -> 9% of each run, Pallas kernels for 13% -> 19%
where the time goes in v1:
time: 220 us; the launch traced here: 219 us
  waiting for transfers between devices  77 us (35%)
  Pallas kernels  63.5 us (29%)
  starting transfers between devices  48.3 us (22%)
  matrix products  13.8 us (6%)
  local copies, waits for them, and re-layouts  7.95 us (4%)
  other arithmetic  7.29 us (3%)
    ppermute x14, waiting for transfers between devices, exchange(): return lax.ppermute(value, 'dp', [(i, i ^ 1 << bit) for i in range(count)])  33.1 us
    all_to_all x4, starting transfers between devices, to_experts(): lax.all_to_all(block, 'dp', split_axis=0, concat_axis=0, tiled=True)  26.3 us
    all_to_all x4, waiting for transfers between devices, to_experts(): lax.all_to_all(block, 'dp', split_axis=0, concat_axis=0, tiled=True)  23.9 us
    ppermute x8, waiting for transfers between devices, swapped(): return lax.ppermute(value, 'mp', swap)  20 us
    ppermute x14, starting transfers between devices, exchange(): return lax.ppermute(value, 'dp', [(i, i ^ 1 << bit) for i in range(count)])  15.7 us
    pallas_call x1, Pallas kernels, attend_back(): pl.pallas_call(functools.partial(attend_back_kernel, buckets), grid=(head...  13.6 us
    pallas_call x1, Pallas kernels, expert(): pl.pallas_call(expert_kernel, grid=(hidden // step,), in_specs=[whole((ro...  12.1 us
    dot_general x3, matrix products, contract_rows(): lax.dot_general(left, right, (((0,), (0,)), ((), ())), preferred_element_...  9.7 us
  transfers between devices with their start and end apart: 26, of which 15 were waited for; matrix products, arithmetic and copies ran while one was open for 9% of the time, Pallas kernels for 19%

profile of v1, /device:TPU:0, one launch (start us, length us, event | category | flops | bytes accessed | tf_op | source)
XLA Modules:
  0.0 219.1 jit_solution(2674952684576027194)
XLA Ops:
  0.7 2.8 %place.1 = bf16[640,768]{1,0:T(8,128)(2,1)} custom-call(s32[1,512]{1,0:T(1,128)} %bitcast.49, s32[1,512]{1,0:T(1,128)} %bitcast.47, bf16[512,768]{1,0:T(8,128)(2,1)} %c_ref.3), custom_call_target="tpu_custom_call" | custom-call | flops 1000000000 | bytes 3000000 | tf_op jit(solution)/shard_map/place/pallas_call | solution.py:324
  3.5 7.4 %all-to-all-start.1 = ((bf16[16,40,768]{2,1,0:T(8,128)(2,1)}), bf16[16,40,768]{2,1,0:T(8,128)(2,1)S(1)}, u32[]{:S(2)}, u32[]{:S(2)}) async-start(bf16[16,40,768]{2,1,0:T(8,128)(2,1)} %bitcast.41), calls=%async_computation.1 | async-start | bytes 1966080 | tf_op jit(solution)/shard_map/all_to_all | solution.py:666
  12.5 9.6 %attend.1 = (bf16[512,384]{1,0:T(8,128)(2,1)}, bf16[512,384]{1,0:T(8,128)(2,1)}, bf16[512,384]{1,0:T(8,128)(2,1)}, bf16[512,384]{1,0:T(8,128)(2,1)}, bf16[6,512,512]{2,1,0:T(8,128)(2,1)}, /*index=5*/s32[8,1024]{1,0:T(8,128)}) custom-call(bf16[512,768]{1,0:T(8,128)(2,1)} %x_ref.7, f32[768]{0:T(1024)} %gain_ref.11, bf16[768,384]{1,0:T(8,128)(2,1)} %wq_ref.3, ...), custom_call_target="tpu_custom_call" | custom-call | flops 8999999488 | bytes 9000000 | tf_op jit(solution)/shard_map/attend/pallas_call | solution.py:115
  25.2 9.1 %collective-permute-done.1.o_other_ref = bf16[512,384]{1,0:T(8,128)(2,1)S(1)} collective-permute-done((bf16[512,384]{1,0:T(8,128)(2,1)}, bf16[512,384]{1,0:T(8,128)(2,1)S(1)}, u32[]{:S(2)}, u32[]{:S(2)}) %collective-permute-start.1) | collective-permute-done | bytes 393248 | tf_op jit(solution)/shard_map/ppermute | solution.py:662
  35.0 4.5 %middle.1 = (f32[512,768]{1,0:T(8,128)}, bf16[640,768]{1,0:T(8,128)(2,1)}) custom-call(s32[5]{0:T(128)} %stack.23.place_ref, bf16[512,384]{1,0:T(8,128)(2,1)} %get-tuple-element.76.o_ref, bf16[512,384]{1,0:T(8,128)(2,1)} %copy-done.20, bf16[384,768]{1,0:T(8,128)(2,1)} %w_ref.5, bf16[192,768]{1,0:T(8,128)(2,1)} %copy-done.21, bf16[192,768]{1,0:T(8,128)(2,1)} %copy-done.22, ...), custom_call_target="tpu_custom_call" | custom-call | flops 2000000000 | bytes 6000000 | tf_op jit(solution)/shard_map/middle/pallas_call | solution.py:373
  39.5 5.7 %all-to-all-start = ((bf16[16,40,768]{2,1,0:T(8,128)(2,1)}), bf16[16,40,768]{2,1,0:T(8,128)(2,1)S(1)}, u32[]{:S(2)}, u32[]{:S(2)}) async-start(bf16[16,40,768]{2,1,0:T(8,128)(2,1)} %bitcast.44), calls=%async_computation | async-start | bytes 1966080 | tf_op jit(solution)/shard_map/all_to_all | solution.py:666
  46.2 21.0 %all-to-all-done = bf16[16,40,768]{2,1,0:T(8,128)(2,1)S(1)} async-done(((bf16[16,40,768]{2,1,0:T(8,128)(2,1)}), bf16[16,40,768]{2,1,0:T(8,128)(2,1)S(1)}, u32[]{:S(2)}, u32[]{:S(2)}) %all-to-all-start) | async-done | bytes 983072 | tf_op jit(solution)/shard_map/all_to_all | solution.py:666
  68.1 12.1 %expert.1 = (bf16[640,768]{1,0:T(8,128)(2,1)}, bf16[640,1536]{1,0:T(8,128)(2,1)}, bf16[640,1536]{1,0:T(8,128)(2,1)}, bf16[640,768]{1,0:T(8,128)(2,1)}, f32[640,1]{1,0:T(8,128)}, /*index=5*/f32[640,16]{1,0:T(8,128)}) custom-call(bf16[640,768]{1,0:T(8,128)(2,1)} %bitcast.37, bf16[640,768]{1,0:T(8,128)(2,1)} %bitcast.40, bf16[768,1536]{1,0:T(8,128)(2,1)} %bitcast.51, ...), custom_call_target="tpu_custom_call" | custom-call | flops 4499999744 | bytes 12000000 | tf_op jit(solution)/shard_map/expert/pallas_call | solution.py:587
  80.1 6.7 %all-to-all-start.2 = ((bf16[16,40,768]{2,1,0:T(8,128)(2,1)}), bf16[16,40,768]{2,1,0:T(8,128)(2,1)S(1)}, u32[]{:S(2)}, u32[]{:S(2)}) async-start(bf16[16,40,768]{2,1,0:T(8,128)(2,1)} %bitcast.43), calls=%async_computation.2 | async-start | bytes 1966080 | tf_op jit(solution)/shard_map/all_to_all | solution.py:666
  87.0 4.1 %multiply_convert_fusion = bf16[640,768]{1,0:T(8,128)(2,1)S(1)} fusion(bf16[640,1536]{1,0:T(8,128)(2,1)} %get-tuple-element.80, f32[640]{0:T(1024)S(1)} %reduce, bf16[1,1536,768]{2,1,0:T(8,128)(2,1)} %param.26), kind=kOutput, calls=%fused_computation.3 | convolution fusion | flops 1510932480 | bytes 5310976 | tf_op jit(solution)/shard_map/dot_general | solution.py:18
  91.8 4.3 %convolution_bitcast_fusion.1 = f32[1,1536,768]{2,1,0:T(8,128)} fusion(bf16[640,1536]{1,0:T(8,128)(2,1)S(1)} %copy-done.24, bf16[640,768]{1,0:T(8,128)(2,1)S(1)} %copy-done.25), kind=kOutput, calls=%fused_computation.1 | convolution fusion | flops 1509949440 | bytes 7667712 | tf_op jit(solution)/shard_map/dot_general | solution.py:26
  97.3 4.2 %convolution_bitcast_fusion = f32[1,768,1536]{2,1,0:T(8,128)} fusion(bf16[640,768]{1,0:T(8,128)(2,1)S(1)} %bitcast.39, bf16[640,1536]{1,0:T(8,128)(2,1)S(1)} %copy-done.23), kind=kOutput, calls=%fused_computation | convolution fusion | flops 1509949440 | bytes 7667712 | tf_op jit(solution)/shard_map/dot_general | solution.py:26
  101.5 3.3 %collective-permute-done.3 = bf16[640,384]{1,0:T(8,128)(2,1)S(1)} collective-permute-done((bf16[640,384]{1,0:T(8,128)(2,1)S(1)}, bf16[640,384]{1,0:T(8,128)(2,1)S(1)}, u32[]{:S(2)}, u32[]{:S(2)}) %collective-permute-start.3) | collective-permute-done | bytes 491552 | tf_op jit(solution)/shard_map/ppermute | solution.py:662
  105.8 2.9 %all-to-all-done.2 = bf16[16,40,768]{2,1,0:T(8,128)(2,1)S(1)} async-done(((bf16[16,40,768]{2,1,0:T(8,128)(2,1)}), bf16[16,40,768]{2,1,0:T(8,128)(2,1)S(1)}, u32[]{:S(2)}, u32[]{:S(2)}) %all-to-all-start.2) | async-done | bytes 983072 | tf_op jit(solution)/shard_map/all_to_all | solution.py:666
  109.6 2.9 %pick.2 = (bf16[256,768]{1,0:T(8,128)(2,1)}, bf16[256,768]{1,0:T(8,128)(2,1)}) custom-call(s32[512,1]{1,0:T(8,128)} %copy.30.ids_ref, bf16[640,768]{1,0:T(8,128)(2,1)} %bitcast.42), custom_call_target="tpu_custom_call" | custom-call | flops 1000000000 | bytes 3000000 | tf_op jit(solution)/shard_map/pick/pallas_call | solution.py:344
  114.5 6.5 %all-to-all-start.3 = ((bf16[16,40,384]{2,1,0:T(8,128)(2,1)}), bf16[16,40,384]{2,1,0:T(8,128)(2,1)S(1)}, u32[]{:S(2)}, u32[]{:S(2)}) async-start(bf16[16,40,384]{2,1,0:T(8,128)(2,1)} %bitcast.22), calls=%async_computation.3 | async-start | bytes 983040 | tf_op jit(solution)/shard_map/all_to_all | solution.py:666
  121.1 3.5 %collective-permute-done.5.got_ref = bf16[256,768]{1,0:T(8,128)(2,1)S(1)} collective-permute-done((bf16[256,768]{1,0:T(8,128)(2,1)}, bf16[256,768]{1,0:T(8,128)(2,1)S(1)}, u32[]{:S(2)}, u32[]{:S(2)}) %collective-permute-start.5) | collective-permute-done | bytes 393248 | tf_op jit(solution)/shard_map/ppermute | solution.py:662
  125.4 3.2 %middle_back.2 = (f32[512,768]{1,0:T(8,128)}, bf16[512,768]{1,0:T(8,128)(2,1)}, bf16[512,384]{1,0:T(8,128)(2,1)}, f32[1,768]{1,0:T(1,128)}) custom-call(bf16[256,768]{1,0:T(8,128)(2,1)} %get-tuple-element.90.own_ref, bf16[256,768]{1,0:T(8,128)(2,1)} %copy-done.14, f32[512,768]{1,0:T(8,128)} %get-tuple-element.89.hmid_ref, bf16[512,768]{1,0:T(8,128)(2,1)} %c_ref.3, ...), custom_call_target="tpu_custom_call" | custom-call | flops 1000000000 | bytes 6000000 | tf_op jit(solution)/shard_map/middle_back/pallas_call | solution.py:419
  128.6 4.1 %collective-permute-done.4.got_ref = bf16[256,768]{1,0:T(8,128)(2,1)S(1)} collective-permute-done((bf16[256,768]{1,0:T(8,128)(2,1)}, bf16[256,768]{1,0:T(8,128)(2,1)S(1)}, u32[]{:S(2)}, u32[]{:S(2)}) %collective-permute-start.4) | collective-permute-done | bytes 393248 | tf_op jit(solution)/shard_map/ppermute | solution.py:662
  133.4 3.2 %middle_back.3 = (f32[512,768]{1,0:T(8,128)}, bf16[512,768]{1,0:T(8,128)(2,1)}, bf16[512,384]{1,0:T(8,128)(2,1)}, f32[1,768]{1,0:T(1,128)}) custom-call(bf16[256,768]{1,0:T(8,128)(2,1)} %get-tuple-element.88.own_ref, bf16[256,768]{1,0:T(8,128)(2,1)} %copy-done.12, ...), custom_call_target="tpu_custom_call", output_to_operand_aliasing={{0}: (6, {}), {1}: (7, {}), {2}: (8, {})} | custom-call | flops 1000000000 | bytes 6000000 | tf_op jit(solution)/shard_map/middle_back/pallas_call | solution.py:419
  136.6 13.6 %attend_back.1 = (bf16[512,768]{1,0:T(8,128)(2,1)}, bf16[896,768]{1,0:T(8,128)(2,1)}, bf16[896,768]{1,0:T(8,128)(2,1)}) custom-call(s32[1]{0:T(128)} %bitcast.side_ref, bf16[512,384]{1,0:T(8,128)(2,1)} %get-tuple-element.95.do_ref, bf16[512,384]{1,0:T(8,128)(2,1)} %get-tuple-element.96.q_ref, bf16[512,384]{1,0:T(8,128)(2,1)} %get-tuple-element.97.k_ref, ...), custom_call_target="tpu_custom_call" | custom-call | flops 12000000000 | bytes 9000000 | tf_op jit(solution)/shard_map/attend_back/pallas_call | solution.py:276
  150.3 3.3 %collective-permute-done.6 = bf16[896,768]{1,0:T(8,128)(2,1)S(1)} collective-permute-done((bf16[896,768]{1,0:T(8,128)(2,1)}, bf16[896,768]{1,0:T(8,128)(2,1)S(1)}, u32[]{:S(2)}, u32[]{:S(2)}) %collective-permute-start.6) | collective-permute-done | bytes 1376288 | tf_op jit(solution)/shard_map/ppermute | solution.py:624
  156.1 3.2 %collective-permute-start.8 = (bf16[256,768]{1,0:T(8,128)(2,1)}, bf16[256,768]{1,0:T(8,128)(2,1)S(1)}, u32[]{:S(2)}, u32[]{:S(2)}) collective-permute-start(bf16[256,768]{1,0:T(8,128)(2,1)} %broadcast_select_fusion.1), channel_id=1, source_target_pairs={{0,8},{2,10},{4,12},{6,14},{8,0},{10,2},{12,4},{14,6},{16,24},{18,... | collective-permute-start | bytes 1179656 | tf_op jit(solution)/shard_map/ppermute | solution.py:624
  162.0 2.5 %pick.3.y_ref = bf16[512,384]{1,0:T(8,128)(2,1)} custom-call(s32[512,1]{1,0:T(8,128)} %copy.30.ids_ref, bf16[640,384]{1,0:T(8,128)(2,1)} %bitcast.45), custom_call_target="tpu_custom_call" | custom-call | flops 1000000000 | bytes 3000000 | tf_op jit(solution)/shard_map/pick/pallas_call | solution.py:344
  164.5 4.7 %collective-permute-done.7 = bf16[192,768]{1,0:T(8,128)(2,1)} collective-permute-done((bf16[192,768]{1,0:T(8,128)(2,1)}, bf16[192,768]{1,0:T(8,128)(2,1)}, u32[]{:S(2)}, u32[]{:S(2)}) %collective-permute-start.7) | collective-permute-done | bytes 294944 | tf_op jit(solution)/shard_map/ppermute | solution.py:624
  175.3 3.3 %collective-permute-done.11 = bf16[128,768]{1,0:T(8,128)(2,1)S(1)} collective-permute-done((bf16[128,768]{1,0:T(8,128)(2,1)S(1)}, bf16[128,768]{1,0:T(8,128)(2,1)S(1)}, u32[]{:S(2)}, u32[]{:S(2)}) %collective-permute-start.11) | collective-permute-done | bytes 196640 | tf_op jit(solution)/shard_map/ppermute | solution.py:624
  178.7 2.1 collective-permute-start.12
  182.3 13.4 %collective-permute-done.10 = bf16[96,768]{1,0:T(8,128)(2,1)S(1)} collective-permute-done((bf16[96,768]{1,0:T(8,128)(2,1)S(1)}, bf16[96,768]{1,0:T(8,128)(2,1)S(1)}, u32[]{:S(2)}, u32[]{:S(2)}) %collective-permute-start.10) | collective-permute-done | bytes 147488 | tf_op jit(solution)/shard_map/ppermute | solution.py:624
  198.1 5.0 %outputs.1 = (f32[512,768]{1,0:T(8,128)}, bf16[512,768]{1,0:T(8,128)(2,1)}) custom-call(s32[5]{0:T(128)} %stack.23.place_ref, bf16[512,768]{1,0:T(8,128)(2,1)} %get-tuple-element.113.own_ref, bf16[512,768]{1,0:T(8,128)(2,1)} %collective-permute-done.13.got_ref, bf16[512,768]{1,0:T(8,128)(2,1)} %x_ref.7, f32[512,768]{1,0:T(8,128)} %get-tuple-element.117.dh_ref, ...), custom_call_target="tpu_custom_call" | custom-call | flops 100000000 | bytes 10000000 | tf_op jit(solution)/shard_map/outputs/pallas_call | solution.py:461
  204.0 2.1 collective-permute-start.18
  206.6 4.5 %collective-permute-done.17 = bf16[192,768]{1,0:T(8,128)(2,1)S(1)} collective-permute-done((bf16[192,768]{1,0:T(8,128)(2,1)S(1)}, bf16[192,768]{1,0:T(8,128)(2,1)S(1)}, u32[]{:S(2)}, u32[]{:S(2)}) %collective-permute-start.17) | collective-permute-done | bytes 294944 | tf_op jit(solution)/shard_map/ppermute | solution.py:624
  214.8 4.1 %unpack.1 = (f32[768,384]{1,0:T(8,128)}, f32[768,384]{1,0:T(8,128)}, f32[768,384]{1,0:T(8,128)}, f32[384,768]{1,0:T(8,128)}, f32[16,768]{1,0:T(8,128)}, /*index=...) custom-call(s32[5]{0:T(128)} %stack.23.place_ref, bf16[384,768]{1,0:T(8,128)(2,1)} %copy-done.3, bf16[384,768]{1,0:T(8,128)(2,1)} %copy-done.7, ...), custom_call_target="tpu_custom_call" | custom-call | flops 100000000 | bytes 8000000 | tf_op jit(solution)/shard_map/unpack/pallas_call | solution.py:508
  (113 shorter events, 35.0 us)
Async XLA Ops:
  0.6 10.2 %copy-start = (bf16[384,768]{1,0:T(8,128)(2,1)S(1)}, bf16[384,768]{1,0:T(8,128)(2,1)}, u32[]{:S(2)}) copy-start(bf16[384,768]{1,0:T(8,128)(2,1)} %w_ref.5) | copy-start | bytes 1769476
  3.5 36.0 %all-to-all-start.1 = ((bf16[16,40,768]{2,1,0:T(8,128)(2,1)}), bf16[16,40,768]{2,1,0:T(8,128)(2,1)S(1)}, u32[]{:S(2)}, u32[]{:S(2)}) async-start(bf16[16,40,768]{2,1,0:T(8,128)(2,1)} %bitcast.41), calls=%async_computation.1 | async-start | bytes 1966080 | tf_op jit(solution)/shard_map/all_to_all | solution.py:666
  10.9 11.2 %collective-permute-start = (bf16[192,768]{1,0:T(8,128)(2,1)S(1)}, bf16[192,768]{1,0:T(8,128)(2,1)S(1)}, u32[]{:S(2)}, u32[]{:S(2)}) collective-permute-start(bf16[192,768]{1,0:T(8,128)(2,1)S(1)} %slice_select_fusion), channel_id=1, source_target_pairs={{0,1},{1,0},{2,3},{3,2},{4,5},{5,4},{6,7},{7,6},{8,9},{9,8},{10,11... | collective-permute-start | bytes 884744 | tf_op jit(solution)/shard_map/ppermute | solution.py:662
  22.9 11.4 %collective-permute-start.1 = (bf16[512,384]{1,0:T(8,128)(2,1)}, bf16[512,384]{1,0:T(8,128)(2,1)S(1)}, u32[]{:S(2)}, u32[]{:S(2)}) collective-permute-start(bf16[512,384]{1,0:T(8,128)(2,1)} %get-tuple-element.76.o_ref), channel_id=1, source_target_pairs={{0,1},{1,0},{2,3},{3,2},{4,5},{5,4},{6,7},{7,6},{8,9},{9,8},{10,11... | collective-permute-start | bytes 1179656 | tf_op jit(solution)/shard_map/ppermute | solution.py:662
  23.4 1.8 collective-permute-start.2
  25.2 9.1 %copy-start.22 = (bf16[192,768]{1,0:T(8,128)(2,1)}, bf16[192,768]{1,0:T(8,128)(2,1)S(1)}, u32[]{:S(2)}) copy-start(bf16[192,768]{1,0:T(8,128)(2,1)S(1)} %collective-permute-done.2.w_far_ref) | copy-start | bytes 884740
  39.5 5.8 %copy-start.19 = (s32[512]{0:T(512)S(1)}, s32[512]{0:T(512)}, u32[]{:S(2)}) copy-start(s32[512]{0:T(512)} %param.27) | copy-start | bytes 6148
  39.5 27.6 %copy-start.5 = (bf16[16,40,768]{2,1,0:T(8,128)(2,1)}, bf16[16,40,768]{2,1,0:T(8,128)(2,1)S(1)}, u32[]{:S(2)}) copy-start(bf16[16,40,768]{2,1,0:T(8,128)(2,1)S(1)} %all-to-all-done.1) | copy-start | bytes 2949124
  39.5 27.6 %all-to-all-start = ((bf16[16,40,768]{2,1,0:T(8,128)(2,1)}), bf16[16,40,768]{2,1,0:T(8,128)(2,1)S(1)}, u32[]{:S(2)}, u32[]{:S(2)}) async-start(bf16[16,40,768]{2,1,0:T(8,128)(2,1)} %bitcast.44), calls=%async_computation | async-start | bytes 1966080 | tf_op jit(solution)/shard_map/all_to_all | solution.py:666
  80.1 6.7 %copy-start.15 = (f32[640,1]{1,0:T(8,128)S(1)}, f32[640,1]{1,0:T(8,128)}, u32[]{:S(2)}) copy-start(f32[640,1]{1,0:T(8,128)} %get-tuple-element.87) | copy-start | bytes 7684
  80.1 28.5 %all-to-all-start.2 = ((bf16[16,40,768]{2,1,0:T(8,128)(2,1)}), bf16[16,40,768]{2,1,0:T(8,128)(2,1)S(1)}, u32[]{:S(2)}, u32[]{:S(2)}) async-start(bf16[16,40,768]{2,1,0:T(8,128)(2,1)} %bitcast.43), calls=%async_computation.2 | async-start | bytes 1966080 | tf_op jit(solution)/shard_map/all_to_all | solution.py:666
  91.2 13.6 %collective-permute-start.3 = (bf16[640,384]{1,0:T(8,128)(2,1)S(1)}, bf16[640,384]{1,0:T(8,128)(2,1)S(1)}, u32[]{:S(2)}, u32[]{:S(2)}) collective-permute-start(bf16[640,384]{1,0:T(8,128)(2,1)S(1)} %broadcast_select_fusion), channel_id=1, source_target_pairs={{0,1},{1,0},{2,3},{3,2},{4,5},{5,4},{6,7},{7,6},{8,9},{9,8},{10,11... | collective-permute-start | bytes 1474568 | tf_op jit(solution)/shard_map/ppermute | solution.py:662
  112.5 12.1 %collective-permute-start.5 = (bf16[256,768]{1,0:T(8,128)(2,1)}, bf16[256,768]{1,0:T(8,128)(2,1)S(1)}, u32[]{:S(2)}, u32[]{:S(2)}) collective-permute-start(bf16[256,768]{1,0:T(8,128)(2,1)} %get-tuple-element.90.own_ref), channel_id=1, source_target_pairs={{0,1},{1,0},{2,3},{3,2},{4,5},{5,4},{6,7},{7,6},{8,9},{9,8},{10,11... | collective-permute-start | bytes 1179656 | tf_op jit(solution)/shard_map/ppermute | solution.py:662
  113.0 19.7 %collective-permute-start.4 = (bf16[256,768]{1,0:T(8,128)(2,1)}, bf16[256,768]{1,0:T(8,128)(2,1)S(1)}, u32[]{:S(2)}, u32[]{:S(2)}) collective-permute-start(bf16[256,768]{1,0:T(8,128)(2,1)} %get-tuple-element.88.own_ref), channel_id=1, source_target_pairs={{0,1},{1,0},{2,3},{3,2},{4,5},{5,4},{6,7},{7,6},{8,9},{9,8},{10,11... | collective-permute-start | bytes 1179656 | tf_op jit(solution)/shard_map/ppermute | solution.py:662
  114.5 35.7 %all-to-all-start.3 = ((bf16[16,40,384]{2,1,0:T(8,128)(2,1)}), bf16[16,40,384]{2,1,0:T(8,128)(2,1)S(1)}, u32[]{:S(2)}, u32[]{:S(2)}) async-start(bf16[16,40,384]{2,1,0:T(8,128)(2,1)} %bitcast.22), calls=%async_computation.3 | async-start | bytes 983040 | tf_op jit(solution)/shard_map/all_to_all | solution.py:666
  150.3 3.4 %collective-permute-start.6 = (bf16[896,768]{1,0:T(8,128)(2,1)}, bf16[896,768]{1,0:T(8,128)(2,1)S(1)}, u32[]{:S(2)}, u32[]{:S(2)}) collective-permute-start(bf16[896,768]{1,0:T(8,128)(2,1)} %get-tuple-element.109), channel_id=1, source_target_pairs={{0,2},{2,0},{4,6},{6,4},{8,10},{10,8},{12,14},{14,12},{16,18},{18,... | collective-permute-start | bytes 4128776 | tf_op jit(solution)/shard_map/ppermute | solution.py:624
  156.1 13.0 %collective-permute-start.8 = (bf16[256,768]{1,0:T(8,128)(2,1)}, bf16[256,768]{1,0:T(8,128)(2,1)S(1)}, u32[]{:S(2)}, u32[]{:S(2)}) collective-permute-start(bf16[256,768]{1,0:T(8,128)(2,1)} %broadcast_select_fusion.1), channel_id=1, source_target_pairs={{0,8},{2,10},{4,12},{6,14},{8,0},{10,2},{12,4},{14,6},{16,24},{18,... | collective-permute-start | bytes 1179656 | tf_op jit(solution)/shard_map/ppermute | solution.py:624
  160.1 9.1 %collective-permute-start.7 = (bf16[192,768]{1,0:T(8,128)(2,1)}, bf16[192,768]{1,0:T(8,128)(2,1)}, u32[]{:S(2)}, u32[]{:S(2)}) collective-permute-start(bf16[192,768]{1,0:T(8,128)(2,1)} %broadcast_select_fusion.6), channel_id=1, source_target_pairs={{0,4},{2,6},{4,0},{6,2},{8,12},{10,14},{12,8},{14,10},{16,20},{18,... | collective-permute-start | bytes 884744 | tf_op jit(solution)/shard_map/ppermute | solution.py:624
  161.5 20.8 %collective-permute-start.13 = (bf16[512,768]{1,0:T(8,128)(2,1)}, bf16[512,768]{1,0:T(8,128)(2,1)}, u32[]{:S(2)}, u32[]{:S(2)}) collective-permute-start(bf16[512,768]{1,0:T(8,128)(2,1)} %get-tuple-element.113.own_ref), channel_id=1, source_target_pairs={{0,1},{1,0},{2,3},{3,2},{4,5},{5,4},{6,7},{7,6},{8,9},{9,8},{10,11... | collective-permute-start | bytes 2359304 | tf_op jit(solution)/shard_map/ppermute | solution.py:662
  171.0 10.8 %copy-start.10 = (bf16[512,384]{1,0:T(8,128)(2,1)S(1)}, bf16[512,384]{1,0:T(8,128)(2,1)}, u32[]{:S(2)}) copy-start(bf16[512,384]{1,0:T(8,128)(2,1)} %pick.3.y_ref) | copy-start | bytes 1179652
  172.2 6.4 %collective-permute-start.11 = (bf16[128,768]{1,0:T(8,128)(2,1)S(1)}, bf16[128,768]{1,0:T(8,128)(2,1)S(1)}, u32[]{:S(2)}, u32[]{:S(2)}) collective-permute-start(bf16[128,768]{1,0:T(8,128)(2,1)S(1)} %broadcast_select_fusion.9), channel_id=1, source_target_pairs={{0,4},{2,6},{4,0},{6,2},{8,12},{10,14},{12,8},{14,10},{16,20},{18,... | collective-permute-start | bytes 589832 | tf_op jit(solution)/shard_map/ppermute | solution.py:624
  173.7 7.1 %collective-permute-start.9 = (bf16[96,768]{1,0:T(8,128)(2,1)S(1)}, bf16[96,768]{1,0:T(8,128)(2,1)S(1)}, u32[]{:S(2)}, u32[]{:S(2)}) collective-permute-start(bf16[96,768]{1,0:T(8,128)(2,1)S(1)} %broadcast_select_fusion.12), channel_id=1, source_target_pairs={{0,8},{2,10},{4,12},{6,14},{8,0},{10,2},{12,4},{14,6},{16,24},{18,... | collective-permute-start | bytes 442376 | tf_op jit(solution)/shard_map/ppermute | solution.py:624
  178.7 17.0 %collective-permute-start.12 = (bf16[128,768]{1,0:T(8,128)(2,1)S(1)}, bf16[128,768]{1,0:T(8,128)(2,1)S(1)}, u32[]{:S(2)}, u32[]{:S(2)}) collective-permute-start(bf16[128,768]{1,0:T(8,128)(2,1)S(1)} %add_convert_fusion.5), channel_id=1, source_target_pairs={{0,16},{2,18},{4,20},{6,22},{8,24},{10,26},{12,28},{14,30},{16,0},... | collective-permute-start | bytes 589832 | tf_op jit(solution)/shard_map/ppermute | solution.py:624
  180.9 14.8 %collective-permute-start.10 = (bf16[96,768]{1,0:T(8,128)(2,1)S(1)}, bf16[96,768]{1,0:T(8,128)(2,1)S(1)}, u32[]{:S(2)}, u32[]{:S(2)}) collective-permute-start(bf16[96,768]{1,0:T(8,128)(2,1)S(1)} %add_convert_fusion.7), channel_id=1, source_target_pairs={{0,16},{2,18},{4,20},{6,22},{8,24},{10,26},{12,28},{14,30},{16,0},... | collective-permute-start | bytes 442376 | tf_op jit(solution)/shard_map/ppermute | solution.py:624
  181.8 15.5 %collective-permute-start.16 = (bf16[512,384]{1,0:T(8,128)(2,1)S(1)}, bf16[512,384]{1,0:T(8,128)(2,1)S(1)}, u32[]{:S(2)}, u32[]{:S(2)}) collective-permute-start(bf16[512,384]{1,0:T(8,128)(2,1)S(1)} %copy-done.10), channel_id=1, source_target_pairs={{0,1},{1,0},{2,3},{3,2},{4,5},{5,4},{6,7},{7,6},{8,9},{9,8},{10,11... | collective-permute-start | bytes 1179656 | tf_op jit(solution)/shard_map/ppermute | solution.py:662
  195.8 7.4 %collective-permute-start.15 = (bf16[128,768]{1,0:T(8,128)(2,1)S(1)}, bf16[128,768]{1,0:T(8,128)(2,1)S(1)}, u32[]{:S(2)}, u32[]{:S(2)}) collective-permute-start(bf16[128,768]{1,0:T(8,128)(2,1)S(1)} %add_convert_fusion.4), channel_id=1, source_target_pairs={{0,4},{2,6},{4,0},{6,2},{8,12},{10,14},{12,8},{14,10},{16,20},{18,... | collective-permute-start | bytes 589832 | tf_op jit(solution)/shard_map/ppermute | solution.py:624
  197.3 5.8 %collective-permute-start.14 = (bf16[96,768]{1,0:T(8,128)(2,1)S(1)}, bf16[96,768]{1,0:T(8,128)(2,1)S(1)}, u32[]{:S(2)}, u32[]{:S(2)}) collective-permute-start(bf16[96,768]{1,0:T(8,128)(2,1)S(1)} %add_convert_fusion.6), channel_id=1, source_target_pairs={{0,8},{2,10},{4,12},{6,14},{8,0},{10,2},{12,4},{14,6},{16,24},{18,... | collective-permute-start | bytes 442376 | tf_op jit(solution)/shard_map/ppermute | solution.py:624
  203.2 7.9 %collective-permute-start.17 = (bf16[192,768]{1,0:T(8,128)(2,1)S(1)}, bf16[192,768]{1,0:T(8,128)(2,1)S(1)}, u32[]{:S(2)}, u32[]{:S(2)}) collective-permute-start(bf16[192,768]{1,0:T(8,128)(2,1)S(1)} %pad_maximum_fusion.3), channel_id=1, source_target_pairs={{0,4},{2,6},{4,0},{6,2},{8,12},{10,14},{12,8},{14,10},{16,20},{18,... | collective-permute-start | bytes 884744 | tf_op jit(solution)/shard_map/ppermute | solution.py:624
  204.0 7.6 %collective-permute-start.18 = (bf16[192,768]{1,0:T(8,128)(2,1)S(1)}, bf16[192,768]{1,0:T(8,128)(2,1)S(1)}, u32[]{:S(2)}, u32[]{:S(2)}) collective-permute-start(bf16[192,768]{1,0:T(8,128)(2,1)S(1)} %pad_maximum_fusion.2), channel_id=1, source_target_pairs={{0,8},{2,10},{4,12},{6,14},{8,0},{10,2},{12,4},{14,6},{16,24},{18,... | collective-permute-start | bytes 884744 | tf_op jit(solution)/shard_map/ppermute | solution.py:624
  206.0 5.7 %collective-permute-start.19 = (bf16[64,768]{1,0:T(8,128)(2,1)S(1)}, bf16[64,768]{1,0:T(8,128)(2,1)S(1)}, u32[]{:S(2)}, u32[]{:S(2)}) collective-permute-start(bf16[64,768]{1,0:T(8,128)(2,1)S(1)} %slice.74.small_ref), channel_id=1, source_target_pairs={{0,1},{1,0},{2,3},{3,2},{4,5},{5,4},{6,7},{7,6},{8,9},{9,8},{10,11... | collective-permute-start | bytes 294920 | tf_op jit(solution)/shard_map/ppermute | solution.py:662
  211.8 2.1 collective-permute-start.20
  211.8 3.0 %collective-permute-start.21 = (bf16[384,768]{1,0:T(8,128)(2,1)S(1)}, bf16[384,768]{1,0:T(8,128)(2,1)}, u32[]{:S(2)}, u32[]{:S(2)}) collective-permute-start(bf16[384,768]{1,0:T(8,128)(2,1)S(1)} %get-tuple-element.126.b_ref), channel_id=1, source_target_pairs={{0,2},{2,0},{4,6},{6,4},{8,10},{10,8},{12,14},{14,12},{16,18},{18,... | collective-permute-start | bytes 1769480 | tf_op jit(solution)/shard_map/ppermute | solution.py:624
  (20 other events, 56.6 us)

commit v2 on v1

--- a/solution.py
+++ b/solution.py
@@ -232,7 +232,7 @@
     for i in range(0, span, 64):
         row = pair * span + i
         skip = jnp.where(row >= quarter, extra, 0)
-        after = pl.ds(pl.multiple_of(local + row + skip, 64), 64)
+        after = pl.ds(pl.multiple_of(local + row + skip, 32), 64)
         keep_ref[after, :] = keep[i : i + 64]
         send_ref[after, :] = send[i : i + 64]
 
@@ -260,7 +260,7 @@
 
 
 def small_rows(experts, heads):
-    return -(-(experts + 2 + heads) // 64) * 64
+    return -(-(experts + 2 + heads) // 32) * 32
 
 
 def attend_back(side, do, q, k, v, p, wq, wk, wv, o, da, x, gain, ids, router, norm2, buckets):
@@ -344,7 +344,7 @@
     return pl.pallas_call(
         pick_kernel,
         out_shape=[part] * parts,
-        compiler_params=params(),
+        compiler_params=params(58),
         cost_estimate=cost(1_000_000_000, 3_000_000),
         name="pick",
     )(ids, slots)
@@ -377,7 +377,7 @@
             jax.ShapeDtypeStruct(x.shape, f32),
             jax.ShapeDtypeStruct((places, x.shape[1]), bf16),
         ],
-        compiler_params=params(),
+        compiler_params=params(58),
         cost_estimate=cost(2_000_000_000, 6_000_000),
         name="middle",
     )(where, o, o_other, w, w_near, w_far, x, gain, *ids)
@@ -435,7 +435,7 @@
             jax.ShapeDtypeStruct((1, width), f32),
         ],
         input_output_aliases={6: 0, 7: 1, 8: 2} if before else {},
-        compiler_params=params(),
+        compiler_params=params(58),
         cost_estimate=cost(1_000_000_000, 6_000_000),
         name="middle_back",
     )(own, got, hmid, c, gain, w, *before)
@@ -465,7 +465,7 @@
             jax.ShapeDtypeStruct(dh.shape, f32),
             jax.ShapeDtypeStruct(x.shape, bf16),
         ],
-        compiler_params=params(),
+        compiler_params=params(58),
         cost_estimate=cost(100_000_000, 10_000_000),
         name="outputs",
     )(where, own, got, x, dh, gain, y, y_other, hmid)
@@ -475,6 +475,11 @@
     n = value.shape[0] // 2
     first, second = value[:n], value[n:]
     return jnp.where(low, first, second), jnp.where(low, second, first)
+
+
+def split_sum(pair, low):
+    (keep, send), (got_keep, got_send) = split(pair[0], low), split(pair[1], low)
+    return add(keep, got_keep), add(send, got_send)
 
 
 def pair_up(value, got, low):
@@ -515,7 +520,7 @@
             jax.ShapeDtypeStruct((heads, buckets), f32),
             flat, flat,
         ],
-        compiler_params=params(),
+        compiler_params=params(58),
         cost_estimate=cost(100_000_000, 8_000_000),
         name="unpack",
     )(where, a, a_got, b, b_got, small, s_got)
@@ -614,7 +619,7 @@
             pltpu.VMEM((rows, 1), f32),
             pltpu.VMEM((rows, width), f32),
         ],
-        compiler_params=params(),
+        compiler_params=params(58),
         cost_estimate=cost(4_500_000_000, 12_000_000),
         name="expert",
     )(x, c, w_in, w_out, router, mine)
@@ -716,17 +721,18 @@
     local = q.shape[1]
     order_a = tuple(range(1, bits))
     order_b = (2, 1) + tuple(range(3, bits))
-    total = add(keep, exchange(send, count, 0))
-    a, b = total[:local], total[local:]
+    got = exchange(send, count, 0)
+    a, b = (keep[:local], got[:local]), (keep[local:], got[local:])
     for stage, (bit_a, bit_b) in enumerate(zip(order_a[:-1], order_b[:-1])):
-        keep_a, send_a = split(a, where[bit_a + 1] == 0)
-        keep_b, send_b = split(b, where[bit_b + 1] == 0)
+        keep_a, send_a = split_sum(a, where[bit_a + 1] == 0)
+        keep_b, send_b = split_sum(b, where[bit_b + 1] == 0)
         got_a = exchange(send_a, count, bit_a)
         got_b = exchange(send_b, count, bit_b)
         if stage == 0:
             (picked,) = pick(slot_column, eo_home, 1)
             got_a, got_b, picked = lax.optimization_barrier((got_a, got_b, picked))
-        a, b = add(keep_a, got_a), add(keep_b, got_b)
+        a, b = (keep_a, got_a), (keep_b, got_b)
+    a, b = add(*a), add(*b)
     got_a = exchange(a, count, order_a[-1])
     got_b = exchange(b, count, order_b[-1])
     got_a, got_b, dn1_other = lax.optimization_barrier((got_a, got_b, dn1_other))

time: 220 us -> 214 us (0.973)
  other arithmetic: 7.29 us -> 4.6 us
    ppermute x14, waiting for transfers between devices: 33.1 us -> 27.7 us  [exchange(): return lax.ppermute(value, 'dp', [(i, i ^ 1 << bit) for i in range(count)])]
    ppermute x8, waiting for transfers between devices: 20 us -> 24 us  [swapped(): return lax.ppermute(value, 'mp', swap)]
    convert_element_type x8 -> x9, other arithmetic: 5.12 us -> 4.01 us  [add(): return (left.astype(f32) + right.astype(f32)).astype(left.dtype)]
    unnamed x52 -> x56, local copies, waits for them, and re-layouts: 6.41 us -> 5.76 us
  transfers between devices with their start and end apart: 26 -> 26, of which waited for: 15 -> 16; matrix products, arithmetic and copies ran while one was open for 9% -> 8% of each run, Pallas kernels for 19% -> 20%
where the time goes in v2:
time: 214 us; the launch traced here: 213 us
  waiting for transfers between devices  76.2 us (36%)
  Pallas kernels  63.4 us (30%)
  starting transfers between devices  47.2 us (22%)
  matrix products  13.1 us (6%)
  local copies, waits for them, and re-layouts  7.2 us (3%)
  other arithmetic  4.6 us (2%)
    ppermute x14, waiting for transfers between devices, exchange(): return lax.ppermute(value, 'dp', [(i, i ^ 1 << bit) for i in range(count)])  27.7 us
    all_to_all x4, starting transfers between devices, to_experts(): lax.all_to_all(block, 'dp', split_axis=0, concat_axis=0, tiled=True)  26.3 us
    all_to_all x4, waiting for transfers between devices, to_experts(): lax.all_to_all(block, 'dp', split_axis=0, concat_axis=0, tiled=True)  24.5 us
    ppermute x8, waiting for transfers between devices, swapped(): return lax.ppermute(value, 'mp', swap)  24 us
    ppermute x14, starting transfers between devices, exchange(): return lax.ppermute(value, 'dp', [(i, i ^ 1 << bit) for i in range(count)])  14.6 us
    pallas_call x1, Pallas kernels, attend_back(): pl.pallas_call(functools.partial(attend_back_kernel, buckets), grid=(head...  13.5 us
    pallas_call x1, Pallas kernels, expert(): pl.pallas_call(expert_kernel, grid=(hidden // step,), in_specs=[whole((ro...  12.1 us
    dot_general x3, matrix products, contract_rows(): lax.dot_general(left, right, (((0,), (0,)), ((), ())), preferred_element_...  9.69 us
  transfers between devices with their start and end apart: 26, of which 16 were waited for; matrix products, arithmetic and copies ran while one was open for 8% of the time, Pallas kernels for 20%

profile of v2, /device:TPU:0, one launch (start us, length us, event | category | flops | bytes accessed | tf_op | source)
XLA Modules:
  0.0 213.0 jit_solution(1345429370526052606)
XLA Ops:
  0.7 2.8 %place.1 = bf16[640,768]{1,0:T(8,128)(2,1)} custom-call(s32[1,512]{1,0:T(1,128)} %bitcast.49, s32[1,512]{1,0:T(1,128)} %bitcast.47, bf16[512,768]{1,0:T(8,128)(2,1)} %c_ref.3), custom_call_target="tpu_custom_call" | custom-call | flops 1000000000 | bytes 3000000 | tf_op jit(solution)/shard_map/place/pallas_call | solution.py:324
  3.5 7.4 %all-to-all-start.1 = ((bf16[16,40,768]{2,1,0:T(8,128)(2,1)}), bf16[16,40,768]{2,1,0:T(8,128)(2,1)S(1)}, u32[]{:S(2)}, u32[]{:S(2)}) async-start(bf16[16,40,768]{2,1,0:T(8,128)(2,1)} %bitcast.41), calls=%async_computation.1 | async-start | bytes 1966080 | tf_op jit(solution)/shard_map/all_to_all | solution.py:671
  12.5 9.6 %attend.1 = (bf16[512,384]{1,0:T(8,128)(2,1)}, bf16[512,384]{1,0:T(8,128)(2,1)}, bf16[512,384]{1,0:T(8,128)(2,1)}, bf16[512,384]{1,0:T(8,128)(2,1)}, bf16[6,512,512]{2,1,0:T(8,128)(2,1)}, /*index=5*/s32[8,1024]{1,0:T(8,128)}) custom-call(bf16[512,768]{1,0:T(8,128)(2,1)} %x_ref.7, f32[768]{0:T(1024)} %gain_ref.11, bf16[768,384]{1,0:T(8,128)(2,1)} %wq_ref.3, ...), custom_call_target="tpu_custom_call" | custom-call | flops 8999999488 | bytes 9000000 | tf_op jit(solution)/shard_map/attend/pallas_call | solution.py:115
  24.3 9.3 %collective-permute-done.1.o_other_ref = bf16[512,384]{1,0:T(8,128)(2,1)S(1)} collective-permute-done((bf16[512,384]{1,0:T(8,128)(2,1)}, bf16[512,384]{1,0:T(8,128)(2,1)S(1)}, u32[]{:S(2)}, u32[]{:S(2)}) %collective-permute-start.1) | collective-permute-done | bytes 393248 | tf_op jit(solution)/shard_map/ppermute | solution.py:667
  34.4 4.5 %middle.1 = (f32[512,768]{1,0:T(8,128)}, bf16[640,768]{1,0:T(8,128)(2,1)}) custom-call(s32[5]{0:T(128)} %stack.23.place_ref, bf16[512,384]{1,0:T(8,128)(2,1)} %get-tuple-element.76.o_ref, bf16[512,384]{1,0:T(8,128)(2,1)} %copy-done.22, bf16[384,768]{1,0:T(8,128)(2,1)} %w_ref.5, bf16[192,768]{1,0:T(8,128)(2,1)} %copy-done.23, bf16[192,768]{1,0:T(8,128)(2,1)} %copy-done.24, ...), custom_call_target="tpu_custom_call" | custom-call | flops 2000000000 | bytes 6000000 | tf_op jit(solution)/shard_map/middle/pallas_call | solution.py:373
  38.9 5.7 %all-to-all-start = ((bf16[16,40,768]{2,1,0:T(8,128)(2,1)}), bf16[16,40,768]{2,1,0:T(8,128)(2,1)S(1)}, u32[]{:S(2)}, u32[]{:S(2)}) async-start(bf16[16,40,768]{2,1,0:T(8,128)(2,1)} %bitcast.44), calls=%async_computation | async-start | bytes 1966080 | tf_op jit(solution)/shard_map/all_to_all | solution.py:671
  45.5 21.0 %all-to-all-done = bf16[16,40,768]{2,1,0:T(8,128)(2,1)S(1)} async-done(((bf16[16,40,768]{2,1,0:T(8,128)(2,1)}), bf16[16,40,768]{2,1,0:T(8,128)(2,1)S(1)}, u32[]{:S(2)}, u32[]{:S(2)}) %all-to-all-start) | async-done | bytes 983072 | tf_op jit(solution)/shard_map/all_to_all | solution.py:671
  67.4 12.1 %expert.1 = (bf16[640,768]{1,0:T(8,128)(2,1)}, bf16[640,1536]{1,0:T(8,128)(2,1)}, bf16[640,1536]{1,0:T(8,128)(2,1)}, bf16[640,768]{1,0:T(8,128)(2,1)}, f32[640,1]{1,0:T(8,128)}, /*index=5*/f32[640,16]{1,0:T(8,128)}) custom-call(bf16[640,768]{1,0:T(8,128)(2,1)} %bitcast.37, bf16[640,768]{1,0:T(8,128)(2,1)} %bitcast.40, bf16[768,1536]{1,0:T(8,128)(2,1)} %bitcast.51, ...), custom_call_target="tpu_custom_call" | custom-call | flops 4499999744 | bytes 12000000 | tf_op jit(solution)/shard_map/expert/pallas_call | solution.py:592
  79.5 6.7 %all-to-all-start.2 = ((bf16[16,40,768]{2,1,0:T(8,128)(2,1)}), bf16[16,40,768]{2,1,0:T(8,128)(2,1)S(1)}, u32[]{:S(2)}, u32[]{:S(2)}) async-start(bf16[16,40,768]{2,1,0:T(8,128)(2,1)} %bitcast.43), calls=%async_computation.2 | async-start | bytes 1966080 | tf_op jit(solution)/shard_map/all_to_all | solution.py:671
  86.4 3.4 %multiply_convert_fusion = bf16[640,768]{1,0:T(8,128)(2,1)S(1)} fusion(bf16[640,1536]{1,0:T(8,128)(2,1)S(1)} %copy-done.26, f32[640]{0:T(1024)S(1)} %reduce, bf16[1,1536,768]{2,1,0:T(8,128)(2,1)} %param.26), kind=kOutput, calls=%fused_computation.2 | convolution fusion | flops 1510932480 | bytes 5310976 | tf_op jit(solution)/shard_map/dot_general | solution.py:18
  90.5 4.3 %convolution_bitcast_fusion.1 = f32[1,1536,768]{2,1,0:T(8,128)} fusion(bf16[640,1536]{1,0:T(8,128)(2,1)S(1)} %copy-done.26, bf16[640,768]{1,0:T(8,128)(2,1)S(1)} %copy-done.27), kind=kOutput, calls=%fused_computation.1 | convolution fusion | flops 1509949440 | bytes 7667712 | tf_op jit(solution)/shard_map/dot_general | solution.py:26
  96.0 4.2 %convolution_bitcast_fusion = f32[1,768,1536]{2,1,0:T(8,128)} fusion(bf16[640,768]{1,0:T(8,128)(2,1)S(1)} %bitcast.39, bf16[640,1536]{1,0:T(8,128)(2,1)S(1)} %copy-done.25), kind=kOutput, calls=%fused_computation | convolution fusion | flops 1509949440 | bytes 7667712 | tf_op jit(solution)/shard_map/dot_general | solution.py:26
  100.2 3.3 %collective-permute-done.3 = bf16[640,384]{1,0:T(8,128)(2,1)S(1)} collective-permute-done((bf16[640,384]{1,0:T(8,128)(2,1)S(1)}, bf16[640,384]{1,0:T(8,128)(2,1)S(1)}, u32[]{:S(2)}, u32[]{:S(2)}) %collective-permute-start.3) | collective-permute-done | bytes 491552 | tf_op jit(solution)/shard_map/ppermute | solution.py:667
  104.5 3.6 %all-to-all-done.2 = bf16[16,40,768]{2,1,0:T(8,128)(2,1)S(1)} async-done(((bf16[16,40,768]{2,1,0:T(8,128)(2,1)}), bf16[16,40,768]{2,1,0:T(8,128)(2,1)S(1)}, u32[]{:S(2)}, u32[]{:S(2)}) %all-to-all-start.2) | async-done | bytes 983072 | tf_op jit(solution)/shard_map/all_to_all | solution.py:671
  109.0 2.9 %pick.2 = (bf16[256,768]{1,0:T(8,128)(2,1)}, bf16[256,768]{1,0:T(8,128)(2,1)}) custom-call(s32[512,1]{1,0:T(8,128)} %copy.30.ids_ref, bf16[640,768]{1,0:T(8,128)(2,1)} %bitcast.42), custom_call_target="tpu_custom_call" | custom-call | flops 1000000000 | bytes 3000000 | tf_op jit(solution)/shard_map/pick/pallas_call | solution.py:344
  113.9 6.5 %all-to-all-start.3 = ((bf16[16,40,384]{2,1,0:T(8,128)(2,1)}), bf16[16,40,384]{2,1,0:T(8,128)(2,1)S(1)}, u32[]{:S(2)}, u32[]{:S(2)}) async-start(bf16[16,40,384]{2,1,0:T(8,128)(2,1)} %bitcast.22), calls=%async_computation.3 | async-start | bytes 983040 | tf_op jit(solution)/shard_map/all_to_all | solution.py:671
  120.5 3.6 %collective-permute-done.5.got_ref = bf16[256,768]{1,0:T(8,128)(2,1)S(1)} collective-permute-done((bf16[256,768]{1,0:T(8,128)(2,1)}, bf16[256,768]{1,0:T(8,128)(2,1)S(1)}, u32[]{:S(2)}, u32[]{:S(2)}) %collective-permute-start.5) | collective-permute-done | bytes 393248 | tf_op jit(solution)/shard_map/ppermute | solution.py:667
  124.8 3.2 %middle_back.2 = (f32[512,768]{1,0:T(8,128)}, bf16[512,768]{1,0:T(8,128)(2,1)}, bf16[512,384]{1,0:T(8,128)(2,1)}, f32[1,768]{1,0:T(1,128)}) custom-call(bf16[256,768]{1,0:T(8,128)(2,1)} %get-tuple-element.90.own_ref, bf16[256,768]{1,0:T(8,128)(2,1)} %copy-done.15, f32[512,768]{1,0:T(8,128)} %get-tuple-element.89.hmid_ref, bf16[512,768]{1,0:T(8,128)(2,1)} %c_ref.3, ...), custom_call_target="tpu_custom_call" | custom-call | flops 1000000000 | bytes 6000000 | tf_op jit(solution)/shard_map/middle_back/pallas_call | solution.py:419
  128.0 4.1 %collective-permute-done.4.got_ref = bf16[256,768]{1,0:T(8,128)(2,1)S(1)} collective-permute-done((bf16[256,768]{1,0:T(8,128)(2,1)}, bf16[256,768]{1,0:T(8,128)(2,1)S(1)}, u32[]{:S(2)}, u32[]{:S(2)}) %collective-permute-start.4) | collective-permute-done | bytes 393248 | tf_op jit(solution)/shard_map/ppermute | solution.py:667
  132.8 3.2 %middle_back.3 = (f32[512,768]{1,0:T(8,128)}, bf16[512,768]{1,0:T(8,128)(2,1)}, bf16[512,384]{1,0:T(8,128)(2,1)}, f32[1,768]{1,0:T(1,128)}) custom-call(bf16[256,768]{1,0:T(8,128)(2,1)} %get-tuple-element.88.own_ref, bf16[256,768]{1,0:T(8,128)(2,1)} %copy-done.14, ...), custom_call_target="tpu_custom_call", output_to_operand_aliasing={{0}: (6, {}), {1}: (7, {}), {2}: (8, {})} | custom-call | flops 1000000000 | bytes 6000000 | tf_op jit(solution)/shard_map/middle_back/pallas_call | solution.py:419
  136.0 13.5 %attend_back.1 = (bf16[512,768]{1,0:T(8,128)(2,1)}, bf16[832,768]{1,0:T(8,128)(2,1)}, bf16[832,768]{1,0:T(8,128)(2,1)}) custom-call(s32[1]{0:T(128)} %bitcast.side_ref, bf16[512,384]{1,0:T(8,128)(2,1)} %get-tuple-element.95.do_ref, bf16[512,384]{1,0:T(8,128)(2,1)} %get-tuple-element.96.q_ref, bf16[512,384]{1,0:T(8,128)(2,1)} %get-tuple-element.97.k_ref, ...), custom_call_target="tpu_custom_call" | custom-call | flops 12000000000 | bytes 9000000 | tf_op jit(solution)/shard_map/attend_back/pallas_call | solution.py:276
  149.7 3.2 %collective-permute-done.6 = bf16[832,768]{1,0:T(8,128)(2,1)S(1)} collective-permute-done((bf16[832,768]{1,0:T(8,128)(2,1)}, bf16[832,768]{1,0:T(8,128)(2,1)S(1)}, u32[]{:S(2)}, u32[]{:S(2)}) %collective-permute-start.6) | collective-permute-done | bytes 1277984 | tf_op jit(solution)/shard_map/ppermute | solution.py:629
  154.2 3.3 %collective-permute-start.8 = (bf16[224,768]{1,0:T(8,128)(2,1)S(1)}, bf16[224,768]{1,0:T(8,128)(2,1)S(1)}, u32[]{:S(2)}, u32[]{:S(2)}) collective-permute-start(bf16[224,768]{1,0:T(8,128)(2,1)S(1)} %get-tuple-element.139), channel_id=1, source_target_pairs={{0,8},{2,10},{4,12},{6,14},{8,0},{10,2},{12,4},{14,6},{16,24},{18,... | collective-permute-start | bytes 1032200 | tf_op jit(solution)/shard_map/ppermute | solution.py:629
  160.7 2.5 %pick.3.y_ref = bf16[512,384]{1,0:T(8,128)(2,1)} custom-call(s32[512,1]{1,0:T(8,128)} %copy.30.ids_ref, bf16[640,384]{1,0:T(8,128)(2,1)} %bitcast.45), custom_call_target="tpu_custom_call" | custom-call | flops 1000000000 | bytes 3000000 | tf_op jit(solution)/shard_map/pick/pallas_call | solution.py:344
  163.2 4.4 %collective-permute-done.7 = bf16[192,768]{1,0:T(8,128)(2,1)S(1)} collective-permute-done((bf16[192,768]{1,0:T(8,128)(2,1)S(1)}, bf16[192,768]{1,0:T(8,128)(2,1)S(1)}, u32[]{:S(2)}, u32[]{:S(2)}) %collective-permute-start.7) | collective-permute-done | bytes 294944 | tf_op jit(solution)/shard_map/ppermute | solution.py:629
  169.6 3.6 %collective-permute-done.11 = bf16[112,768]{1,0:T(8,128)(2,1)S(1)} collective-permute-done((bf16[112,768]{1,0:T(8,128)(2,1)S(1)}, bf16[112,768]{1,0:T(8,128)(2,1)S(1)}, u32[]{:S(2)}, u32[]{:S(2)}) %collective-permute-start.11) | collective-permute-done | bytes 172064 | tf_op jit(solution)/shard_map/ppermute | solution.py:629
  176.9 3.7 %collective-permute-done.13.got_ref = bf16[512,768]{1,0:T(8,128)(2,1)S(1)} collective-permute-done((bf16[512,768]{1,0:T(8,128)(2,1)S(1)}, bf16[512,768]{1,0:T(8,128)(2,1)S(1)}, u32[]{:S(2)}, u32[]{:S(2)}) %collective-permute-start.13) | collective-permute-done | bytes 786464 | tf_op jit(solution)/shard_map/ppermute | solution.py:667
  180.7 8.0 %collective-permute-done.10 = bf16[96,768]{1,0:T(8,128)(2,1)S(1)} collective-permute-done((bf16[96,768]{1,0:T(8,128)(2,1)S(1)}, bf16[96,768]{1,0:T(8,128)(2,1)S(1)}, u32[]{:S(2)}, u32[]{:S(2)}) %collective-permute-start.10) | collective-permute-done | bytes 147488 | tf_op jit(solution)/shard_map/ppermute | solution.py:629
  191.0 5.0 %outputs.1 = (f32[512,768]{1,0:T(8,128)}, bf16[512,768]{1,0:T(8,128)(2,1)}) custom-call(s32[5]{0:T(128)} %stack.23.place_ref, bf16[512,768]{1,0:T(8,128)(2,1)} %get-tuple-element.113.own_ref, bf16[512,768]{1,0:T(8,128)(2,1)} %copy-done.8, bf16[512,768]{1,0:T(8,128)(2,1)} %x_ref.7, f32[512,768]{1,0:T(8,128)} %get-tuple-element.117.dh_ref, f32[768]{0:T(1024)} %gain_ref.11, ...), custom_call_target="tpu_custom_call" | custom-call | flops 100000000 | bytes 10000000 | tf_op jit(solution)/shard_map/outputs/pallas_call | solution.py:461
  196.8 2.1 collective-permute-start.18
  199.4 5.2 %collective-permute-done.17 = bf16[192,768]{1,0:T(8,128)(2,1)S(1)} collective-permute-done((bf16[192,768]{1,0:T(8,128)(2,1)S(1)}, bf16[192,768]{1,0:T(8,128)(2,1)S(1)}, u32[]{:S(2)}, u32[]{:S(2)}) %collective-permute-start.17) | collective-permute-done | bytes 294944 | tf_op jit(solution)/shard_map/ppermute | solution.py:629
  208.8 4.0 %unpack.1 = (f32[768,384]{1,0:T(8,128)}, f32[768,384]{1,0:T(8,128)}, f32[768,384]{1,0:T(8,128)}, f32[384,768]{1,0:T(8,128)}, f32[16,768]{1,0:T(8,128)}, /*index=...) custom-call(s32[5]{0:T(128)} %stack.23.place_ref, bf16[384,768]{1,0:T(8,128)(2,1)} %copy-done.3, bf16[384,768]{1,0:T(8,128)(2,1)} %copy-done.9, ...), custom_call_target="tpu_custom_call" | custom-call | flops 100000000 | bytes 8000000 | tf_op jit(solution)/shard_map/unpack/pallas_call | solution.py:513
  (114 shorter events, 32.0 us)
Async XLA Ops:
  0.6 10.2 %copy-start = (bf16[384,768]{1,0:T(8,128)(2,1)S(1)}, bf16[384,768]{1,0:T(8,128)(2,1)}, u32[]{:S(2)}) copy-start(bf16[384,768]{1,0:T(8,128)(2,1)} %w_ref.5) | copy-start | bytes 1769476
  3.5 35.4 %all-to-all-start.1 = ((bf16[16,40,768]{2,1,0:T(8,128)(2,1)}), bf16[16,40,768]{2,1,0:T(8,128)(2,1)S(1)}, u32[]{:S(2)}, u32[]{:S(2)}) async-start(bf16[16,40,768]{2,1,0:T(8,128)(2,1)} %bitcast.41), calls=%async_computation.1 | async-start | bytes 1966080 | tf_op jit(solution)/shard_map/all_to_all | solution.py:671
  10.9 11.2 %collective-permute-start = (bf16[192,768]{1,0:T(8,128)(2,1)S(1)}, bf16[192,768]{1,0:T(8,128)(2,1)S(1)}, u32[]{:S(2)}, u32[]{:S(2)}) collective-permute-start(bf16[192,768]{1,0:T(8,128)(2,1)S(1)} %slice_select_fusion), channel_id=1, source_target_pairs={{0,1},{1,0},{2,3},{3,2},{4,5},{5,4},{6,7},{7,6},{8,9},{9,8},{10,11... | collective-permute-start | bytes 884744 | tf_op jit(solution)/shard_map/ppermute | solution.py:667
  22.2 11.5 %copy-start.23 = (bf16[192,768]{1,0:T(8,128)(2,1)}, bf16[192,768]{1,0:T(8,128)(2,1)S(1)}, u32[]{:S(2)}) copy-start(bf16[192,768]{1,0:T(8,128)(2,1)S(1)} %collective-permute-done.w_near_ref) | copy-start | bytes 884740
  22.2 11.4 %collective-permute-start.1 = (bf16[512,384]{1,0:T(8,128)(2,1)}, bf16[512,384]{1,0:T(8,128)(2,1)S(1)}, u32[]{:S(2)}, u32[]{:S(2)}) collective-permute-start(bf16[512,384]{1,0:T(8,128)(2,1)} %get-tuple-element.76.o_ref), channel_id=1, source_target_pairs={{0,1},{1,0},{2,3},{3,2},{4,5},{5,4},{6,7},{7,6},{8,9},{9,8},{10,11... | collective-permute-start | bytes 1179656 | tf_op jit(solution)/shard_map/ppermute | solution.py:667
  22.8 1.6 collective-permute-start.2
  38.9 27.6 %copy-start.5 = (bf16[16,40,768]{2,1,0:T(8,128)(2,1)}, bf16[16,40,768]{2,1,0:T(8,128)(2,1)S(1)}, u32[]{:S(2)}) copy-start(bf16[16,40,768]{2,1,0:T(8,128)(2,1)S(1)} %all-to-all-done.1) | copy-start | bytes 2949124
  38.9 27.6 %all-to-all-start = ((bf16[16,40,768]{2,1,0:T(8,128)(2,1)}), bf16[16,40,768]{2,1,0:T(8,128)(2,1)S(1)}, u32[]{:S(2)}, u32[]{:S(2)}) async-start(bf16[16,40,768]{2,1,0:T(8,128)(2,1)} %bitcast.44), calls=%async_computation | async-start | bytes 1966080 | tf_op jit(solution)/shard_map/all_to_all | solution.py:671
  79.5 28.6 %all-to-all-start.2 = ((bf16[16,40,768]{2,1,0:T(8,128)(2,1)}), bf16[16,40,768]{2,1,0:T(8,128)(2,1)S(1)}, u32[]{:S(2)}, u32[]{:S(2)}) async-start(bf16[16,40,768]{2,1,0:T(8,128)(2,1)} %bitcast.43), calls=%async_computation.2 | async-start | bytes 1966080 | tf_op jit(solution)/shard_map/all_to_all | solution.py:671
  89.9 13.6 %collective-permute-start.3 = (bf16[640,384]{1,0:T(8,128)(2,1)S(1)}, bf16[640,384]{1,0:T(8,128)(2,1)S(1)}, u32[]{:S(2)}, u32[]{:S(2)}) collective-permute-start(bf16[640,384]{1,0:T(8,128)(2,1)S(1)} %broadcast_select_fusion), channel_id=1, source_target_pairs={{0,1},{1,0},{2,3},{3,2},{4,5},{5,4},{6,7},{7,6},{8,9},{9,8},{10,11... | collective-permute-start | bytes 1474568 | tf_op jit(solution)/shard_map/ppermute | solution.py:667
  111.9 12.1 %collective-permute-start.5 = (bf16[256,768]{1,0:T(8,128)(2,1)}, bf16[256,768]{1,0:T(8,128)(2,1)S(1)}, u32[]{:S(2)}, u32[]{:S(2)}) collective-permute-start(bf16[256,768]{1,0:T(8,128)(2,1)} %get-tuple-element.90.own_ref), channel_id=1, source_target_pairs={{0,1},{1,0},{2,3},{3,2},{4,5},{5,4},{6,7},{7,6},{8,9},{9,8},{10,11... | collective-permute-start | bytes 1179656 | tf_op jit(solution)/shard_map/ppermute | solution.py:667
  112.4 19.7 %collective-permute-start.4 = (bf16[256,768]{1,0:T(8,128)(2,1)}, bf16[256,768]{1,0:T(8,128)(2,1)S(1)}, u32[]{:S(2)}, u32[]{:S(2)}) collective-permute-start(bf16[256,768]{1,0:T(8,128)(2,1)} %get-tuple-element.88.own_ref), channel_id=1, source_target_pairs={{0,1},{1,0},{2,3},{3,2},{4,5},{5,4},{6,7},{7,6},{8,9},{9,8},{10,11... | collective-permute-start | bytes 1179656 | tf_op jit(solution)/shard_map/ppermute | solution.py:667
  113.9 35.6 %all-to-all-start.3 = ((bf16[16,40,384]{2,1,0:T(8,128)(2,1)}), bf16[16,40,384]{2,1,0:T(8,128)(2,1)S(1)}, u32[]{:S(2)}, u32[]{:S(2)}) async-start(bf16[16,40,384]{2,1,0:T(8,128)(2,1)} %bitcast.22), calls=%async_computation.3 | async-start | bytes 983040 | tf_op jit(solution)/shard_map/all_to_all | solution.py:671
  149.6 10.6 %copy-start.7 = (bf16[512,768]{1,0:T(8,128)(2,1)S(1)}, bf16[512,768]{1,0:T(8,128)(2,1)}, u32[]{:S(2)}) copy-start(bf16[512,768]{1,0:T(8,128)(2,1)} %get-tuple-element.113.own_ref) | copy-start | bytes 2359300
  149.6 11.1 %copy-start.11 = (bf16[16,40,384]{2,1,0:T(8,128)(2,1)}, bf16[16,40,384]{2,1,0:T(8,128)(2,1)S(1)}, u32[]{:S(2)}) copy-start(bf16[16,40,384]{2,1,0:T(8,128)(2,1)S(1)} %all-to-all-done.3) | copy-start | bytes 1474564
  149.6 3.3 %collective-permute-start.6 = (bf16[832,768]{1,0:T(8,128)(2,1)}, bf16[832,768]{1,0:T(8,128)(2,1)S(1)}, u32[]{:S(2)}, u32[]{:S(2)}) collective-permute-start(bf16[832,768]{1,0:T(8,128)(2,1)} %get-tuple-element.109), channel_id=1, source_target_pairs={{0,2},{2,0},{4,6},{6,4},{8,10},{10,8},{12,14},{14,12},{16,18},{18,... | collective-permute-start | bytes 3833864 | tf_op jit(solution)/shard_map/ppermute | solution.py:629
  154.2 13.4 %collective-permute-start.8 = (bf16[224,768]{1,0:T(8,128)(2,1)S(1)}, bf16[224,768]{1,0:T(8,128)(2,1)S(1)}, u32[]{:S(2)}, u32[]{:S(2)}) collective-permute-start(bf16[224,768]{1,0:T(8,128)(2,1)S(1)} %get-tuple-element.139), channel_id=1, source_target_pairs={{0,8},{2,10},{4,12},{6,14},{8,0},{10,2},{12,4},{14,6},{16,24},{18,... | collective-permute-start | bytes 1032200 | tf_op jit(solution)/shard_map/ppermute | solution.py:629
  158.7 8.8 %collective-permute-start.7 = (bf16[192,768]{1,0:T(8,128)(2,1)S(1)}, bf16[192,768]{1,0:T(8,128)(2,1)S(1)}, u32[]{:S(2)}, u32[]{:S(2)}) collective-permute-start(bf16[192,768]{1,0:T(8,128)(2,1)S(1)} %get-tuple-element.140), channel_id=1, source_target_pairs={{0,4},{2,6},{4,0},{6,2},{8,12},{10,14},{12,8},{14,10},{16,20},{18,... | collective-permute-start | bytes 884744 | tf_op jit(solution)/shard_map/ppermute | solution.py:629
  160.2 20.5 %collective-permute-start.13 = (bf16[512,768]{1,0:T(8,128)(2,1)S(1)}, bf16[512,768]{1,0:T(8,128)(2,1)S(1)}, u32[]{:S(2)}, u32[]{:S(2)}) collective-permute-start(bf16[512,768]{1,0:T(8,128)(2,1)S(1)} %copy-done.7), channel_id=1, source_target_pairs={{0,1},{1,0},{2,3},{3,2},{4,5},{5,4},{6,7},{7,6},{8,9},{9,8},{10,11... | collective-permute-start | bytes 2359304 | tf_op jit(solution)/shard_map/ppermute | solution.py:667
  163.2 13.2 %copy-start.12 = (bf16[512,384]{1,0:T(8,128)(2,1)S(1)}, bf16[512,384]{1,0:T(8,128)(2,1)}, u32[]{:S(2)}) copy-start(bf16[512,384]{1,0:T(8,128)(2,1)} %pick.3.y_ref) | copy-start | bytes 1179652
  167.6 5.5 %collective-permute-start.11 = (bf16[112,768]{1,0:T(8,128)(2,1)S(1)}, bf16[112,768]{1,0:T(8,128)(2,1)S(1)}, u32[]{:S(2)}, u32[]{:S(2)}) collective-permute-start(bf16[112,768]{1,0:T(8,128)(2,1)S(1)} %add_convert_fusion.7), channel_id=1, source_target_pairs={{0,4},{2,6},{4,0},{6,2},{8,12},{10,14},{12,8},{14,10},{16,20},{18,... | collective-permute-start | bytes 516104 | tf_op jit(solution)/shard_map/ppermute | solution.py:629
  169.2 5.4 %collective-permute-start.9 = (bf16[96,768]{1,0:T(8,128)(2,1)S(1)}, bf16[96,768]{1,0:T(8,128)(2,1)S(1)}, u32[]{:S(2)}, u32[]{:S(2)}) collective-permute-start(bf16[96,768]{1,0:T(8,128)(2,1)S(1)} %add_convert_fusion.11), channel_id=1, source_target_pairs={{0,8},{2,10},{4,12},{6,14},{8,0},{10,2},{12,4},{14,6},{16,24},{18,... | collective-permute-start | bytes 442376 | tf_op jit(solution)/shard_map/ppermute | solution.py:629
  173.2 15.4 %collective-permute-start.12 = (bf16[112,768]{1,0:T(8,128)(2,1)S(1)}, bf16[112,768]{1,0:T(8,128)(2,1)S(1)}, u32[]{:S(2)}, u32[]{:S(2)}) collective-permute-start(bf16[112,768]{1,0:T(8,128)(2,1)S(1)} %add_convert_fusion.6), channel_id=1, source_target_pairs={{0,16},{2,18},{4,20},{6,22},{8,24},{10,26},{12,28},{14,30},{16,0},... | collective-permute-start | bytes 516104 | tf_op jit(solution)/shard_map/ppermute | solution.py:629
  174.7 13.9 %collective-permute-start.10 = (bf16[96,768]{1,0:T(8,128)(2,1)S(1)}, bf16[96,768]{1,0:T(8,128)(2,1)S(1)}, u32[]{:S(2)}, u32[]{:S(2)}) collective-permute-start(bf16[96,768]{1,0:T(8,128)(2,1)S(1)} %add_convert_fusion.10), channel_id=1, source_target_pairs={{0,16},{2,18},{4,20},{6,22},{8,24},{10,26},{12,28},{14,30},{16,0},... | collective-permute-start | bytes 442376 | tf_op jit(solution)/shard_map/ppermute | solution.py:629
  176.4 13.9 %collective-permute-start.16 = (bf16[512,384]{1,0:T(8,128)(2,1)S(1)}, bf16[512,384]{1,0:T(8,128)(2,1)S(1)}, u32[]{:S(2)}, u32[]{:S(2)}) collective-permute-start(bf16[512,384]{1,0:T(8,128)(2,1)S(1)} %copy-done.12), channel_id=1, source_target_pairs={{0,1},{1,0},{2,3},{3,2},{4,5},{5,4},{6,7},{7,6},{8,9},{9,8},{10,11... | collective-permute-start | bytes 1179656 | tf_op jit(solution)/shard_map/ppermute | solution.py:667
  188.7 7.4 %collective-permute-start.15 = (bf16[112,768]{1,0:T(8,128)(2,1)S(1)}, bf16[112,768]{1,0:T(8,128)(2,1)S(1)}, u32[]{:S(2)}, u32[]{:S(2)}) collective-permute-start(bf16[112,768]{1,0:T(8,128)(2,1)S(1)} %add_convert_fusion.5), channel_id=1, source_target_pairs={{0,4},{2,6},{4,0},{6,2},{8,12},{10,14},{12,8},{14,10},{16,20},{18,... | collective-permute-start | bytes 516104 | tf_op jit(solution)/shard_map/ppermute | solution.py:629
  190.2 5.8 %collective-permute-start.14 = (bf16[96,768]{1,0:T(8,128)(2,1)S(1)}, bf16[96,768]{1,0:T(8,128)(2,1)S(1)}, u32[]{:S(2)}, u32[]{:S(2)}) collective-permute-start(bf16[96,768]{1,0:T(8,128)(2,1)S(1)} %add_convert_fusion.9), channel_id=1, source_target_pairs={{0,8},{2,10},{4,12},{6,14},{8,0},{10,2},{12,4},{14,6},{16,24},{18,... | collective-permute-start | bytes 442376 | tf_op jit(solution)/shard_map/ppermute | solution.py:629
  196.1 8.5 %collective-permute-start.17 = (bf16[192,768]{1,0:T(8,128)(2,1)S(1)}, bf16[192,768]{1,0:T(8,128)(2,1)S(1)}, u32[]{:S(2)}, u32[]{:S(2)}) collective-permute-start(bf16[192,768]{1,0:T(8,128)(2,1)S(1)} %pad_maximum_fusion.3), channel_id=1, source_target_pairs={{0,4},{2,6},{4,0},{6,2},{8,12},{10,14},{12,8},{14,10},{16,20},{18,... | collective-permute-start | bytes 884744 | tf_op jit(solution)/shard_map/ppermute | solution.py:629
  196.8 8.0 %collective-permute-start.18 = (bf16[192,768]{1,0:T(8,128)(2,1)S(1)}, bf16[192,768]{1,0:T(8,128)(2,1)S(1)}, u32[]{:S(2)}, u32[]{:S(2)}) collective-permute-start(bf16[192,768]{1,0:T(8,128)(2,1)S(1)} %pad_maximum_fusion.2), channel_id=1, source_target_pairs={{0,8},{2,10},{4,12},{6,14},{8,0},{10,2},{12,4},{14,6},{16,24},{18,... | collective-permute-start | bytes 884744 | tf_op jit(solution)/shard_map/ppermute | solution.py:629
  198.9 6.1 %collective-permute-start.19 = (bf16[32,768]{1,0:T(8,128)(2,1)S(1)}, bf16[32,768]{1,0:T(8,128)(2,1)S(1)}, u32[]{:S(2)}, u32[]{:S(2)}) collective-permute-start(bf16[32,768]{1,0:T(8,128)(2,1)S(1)} %slice.112.small_ref), channel_id=1, source_target_pairs={{0,1},{1,0},{2,3},{3,2},{4,5},{5,4},{6,7},{7,6},{8,9},{9,8},{10,11... | collective-permute-start | bytes 147464 | tf_op jit(solution)/shard_map/ppermute | solution.py:667
  205.0 2.1 collective-permute-start.20
  205.1 2.8 %collective-permute-start.21 = (bf16[384,768]{1,0:T(8,128)(2,1)S(1)}, bf16[384,768]{1,0:T(8,128)(2,1)S(1)}, u32[]{:S(2)}, u32[]{:S(2)}) collective-permute-start(bf16[384,768]{1,0:T(8,128)(2,1)S(1)} %get-tuple-element.126.b_ref), channel_id=1, source_target_pairs={{0,2},{2,0},{4,6},{6,4},{8,10},{10,8},{12,14},{14,12},{16,18},{18,... | collective-permute-start | bytes 1769480 | tf_op jit(solution)/shard_map/ppermute | solution.py:629
  (22 other events, 83.6 us)

commit v3 on v2

--- a/solution.py
+++ b/solution.py
@@ -339,12 +339,11 @@
         first += count
 
 
-def pick(ids, slots, parts):
-    part = jax.ShapeDtypeStruct((ids.shape[0] // parts, slots.shape[1]), bf16)
+def pick(ids, slots, *counts):
     return pl.pallas_call(
         pick_kernel,
-        out_shape=[part] * parts,
-        compiler_params=params(58),
+        out_shape=[jax.ShapeDtypeStruct((n, slots.shape[1]), bf16) for n in counts],
+        compiler_params=params(16),
         cost_estimate=cost(1_000_000_000, 3_000_000),
         name="pick",
     )(ids, slots)
@@ -441,34 +440,41 @@
     )(own, got, hmid, c, gain, w, *before)
 
 
-def output_kernel(
-    place_ref, own_ref, got_ref, x_ref, dh_ref, gain_ref, y_ref, y_other_ref, hmid_ref,
-    grad_ref, out_ref,
-):
-    low = place_ref[0] == 0
+def input_back_kernel(own_ref, got_ref, x_ref, dh_ref, gain_ref, grad_ref):
     x = x_ref[...].astype(f32)
     dn = own_ref[...].astype(f32) + got_ref[...].astype(f32)
     inverse = lax.rsqrt(jnp.mean(x * x, axis=-1, keepdims=True) + epsilon)
     scaled = dn * gain_ref[...][None, :]
     inner = jnp.mean(scaled * x, axis=-1, keepdims=True)
     grad_ref[...] = dh_ref[...] + inverse * scaled - x * (inverse * inverse * inverse * inner)
+
+
+def input_back(own, got, x, dh, gain):
+    return pl.pallas_call(
+        input_back_kernel,
+        out_shape=jax.ShapeDtypeStruct(dh.shape, f32),
+        compiler_params=params(58),
+        cost_estimate=cost(100_000_000, 6_000_000),
+        name="input_back",
+    )(own, got, x, dh, gain)
+
+
+def finish_kernel(place_ref, y_ref, y_other_ref, hmid_ref, out_ref):
+    low = place_ref[0] == 0
     y, y_other = y_ref[...], y_other_ref[...]
     moved = jnp.concatenate([jnp.where(low, y, y_other), jnp.where(low, y_other, y)], axis=1)
     out_ref[...] = (hmid_ref[...] + moved.astype(f32)).astype(bf16)
 
 
-def outputs(where, own, got, x, dh, gain, y, y_other, hmid):
-    return pl.pallas_call(
-        output_kernel,
-        in_specs=[scalars()] + [pl.BlockSpec(memory_space=pltpu.VMEM)] * 8,
-        out_shape=[
-            jax.ShapeDtypeStruct(dh.shape, f32),
-            jax.ShapeDtypeStruct(x.shape, bf16),
-        ],
+def finish(where, y, y_other, hmid):
+    return pl.pallas_call(
+        finish_kernel,
+        in_specs=[scalars()] + [pl.BlockSpec(memory_space=pltpu.VMEM)] * 3,
+        out_shape=jax.ShapeDtypeStruct(hmid.shape, bf16),
         compiler_params=params(58),
-        cost_estimate=cost(100_000_000, 10_000_000),
-        name="outputs",
-    )(where, own, got, x, dh, gain, y, y_other, hmid)
+        cost_estimate=cost(1_000_000, 4_000_000),
+        name="finish",
+    )(where, y, y_other, hmid)
 
 
 def split(value, low):
@@ -520,7 +526,7 @@
             jax.ShapeDtypeStruct((heads, buckets), f32),
             flat, flat,
         ],
-        compiler_params=params(58),
+        compiler_params=params(24),
         cost_estimate=cost(100_000_000, 8_000_000),
         name="unpack",
     )(where, a, a_got, b, b_got, small, s_got)
@@ -702,14 +708,15 @@
         (dx_home, grad_w_out, grad_w_in, grad_router)
     )
 
-    low, high = pick(slot_column, dx_home, 2)
+    first = 3 * tokens // 4
+    low, high = pick(slot_column, dx_home, first, tokens - first)
     low, high, eo = lax.optimization_barrier((low, high, eo))
     low_other = swapped(low)
     high_other = swapped(high)
     eo_home = to_experts(eo)
     before = middle_back(0, low, low_other, hmid, out_grad, norm2_gain, w_output)
     dh, da, do, grad_norm2 = middle_back(
-        tokens // 2, high, high_other, hmid, out_grad, norm2_gain, w_output, before
+        first, high, high_other, hmid, out_grad, norm2_gain, w_output, before
     )
     dn1, keep, send = attend_back(
         side, do, q, k, v, p, w_query, w_key, w_value, o, da, hidden_in, norm1_gain, ids,
@@ -729,32 +736,27 @@
         got_a = exchange(send_a, count, bit_a)
         got_b = exchange(send_b, count, bit_b)
         if stage == 0:
-            (picked,) = pick(slot_column, eo_home, 1)
+            (picked,) = pick(slot_column, eo_home, tokens)
             got_a, got_b, picked = lax.optimization_barrier((got_a, got_b, picked))
         a, b = (keep_a, got_a), (keep_b, got_b)
     a, b = add(*a), add(*b)
     got_a = exchange(a, count, order_a[-1])
     got_b = exchange(b, count, order_b[-1])
-    got_a, got_b, dn1_other = lax.optimization_barrier((got_a, got_b, dn1_other))
+    grad_hidden = input_back(dn1, dn1_other, hidden_in, dh, norm1_gain)
+    got_a, got_b, grad_hidden = lax.optimization_barrier((got_a, got_b, grad_hidden))
     picked_other = swapped(picked)
     a, b = add(a, got_a), add(b, got_b)
     for bit_a, bit_b in zip(order_a[-2::-1], order_b[-2::-1]):
         got_a = exchange(a, count, bit_a)
         got_b = exchange(b, count, bit_b)
-        if bit_b == 1:
-            grad_hidden, hidden_out = outputs(
-                where, dn1, dn1_other, hidden_in, dh, norm1_gain, picked, picked_other, hmid
-            )
-            got_a, got_b, grad_hidden, hidden_out = lax.optimization_barrier(
-                (got_a, got_b, grad_hidden, hidden_out)
-            )
         a = pair_up(a, got_a, where[bit_a + 1] == 0)
         b = pair_up(b, got_b, where[bit_b + 1] == 0)
         if bit_b == 1:
             small = b[local // 2 :]
             b = b[: local // 2]
             small_other = swapped(small)
-    a, b, small_other = lax.optimization_barrier((a, b, small_other))
+    hidden_out = finish(where, picked, picked_other, hmid)
+    a, b, small_other, hidden_out = lax.optimization_barrier((a, b, small_other, hidden_out))
     grad_q, grad_k, grad_v, grad_w_output, grad_router, grad_table, grad_norm1, grad_norm2 = unpack(
         where, a, exchange(a, count, 0), b, exchange(b, count, 0), small, small_other,
         experts, buckets, heads,

time: 214 us -> 209 us (0.977)
  Pallas kernels: 63.4 us -> 60.2 us
    pallas_call x3 -> x4, Pallas kernels: 10.4 us -> 8.16 us  [the longest x1 3.94 us: input_back(): pl.pallas_call(input_back_kernel, out_shape=jax.ShapeDtypeStruct(dh.shape...]
    unnamed x56 -> x46, local copies, waits for them, and re-layouts: 5.76 us -> 4.88 us
  transfers between devices with their start and end apart: 26 -> 26, of which waited for: 16 -> 17; matrix products, arithmetic and copies ran while one was open for 8% -> 9% of each run, Pallas kernels for 20% -> 20%
where the time goes in v3:
time: 209 us; the launch traced here: 208 us
  waiting for transfers between devices  74.1 us (35%)
  Pallas kernels  60.2 us (29%)
  starting transfers between devices  47.9 us (23%)
  matrix products  13.8 us (7%)
  local copies, waits for them, and re-layouts  5.65 us (3%)
  other arithmetic  5.33 us (3%)
    all_to_all x4, starting transfers between devices, to_experts(): lax.all_to_all(block, 'dp', split_axis=0, concat_axis=0, tiled=True)  26.3 us
    ppermute x14, waiting for transfers between devices, exchange(): return lax.ppermute(value, 'dp', [(i, i ^ 1 << bit) for i in range(count)])  25.8 us
    all_to_all x4, waiting for transfers between devices, to_experts(): lax.all_to_all(block, 'dp', split_axis=0, concat_axis=0, tiled=True)  24.6 us
    ppermute x8, waiting for transfers between devices, swapped(): return lax.ppermute(value, 'mp', swap)  23.7 us
    ppermute x14, starting transfers between devices, exchange(): return lax.ppermute(value, 'dp', [(i, i ^ 1 << bit) for i in range(count)])  15.4 us
    pallas_call x1, Pallas kernels, attend_back(): pl.pallas_call(functools.partial(attend_back_kernel, buckets), grid=(head...  13.5 us
    pallas_call x1, Pallas kernels, expert(): pl.pallas_call(expert_kernel, grid=(hidden // step,), in_specs=[whole((ro...  12.1 us
    dot_general x3, matrix products, contract_rows(): lax.dot_general(left, right, (((0,), (0,)), ((), ())), preferred_element_...  9.69 us
  transfers between devices with their start and end apart: 26, of which 17 were waited for; matrix products, arithmetic and copies ran while one was open for 9% of the time, Pallas kernels for 20%

profile of v3, /device:TPU:0, one launch (start us, length us, event | category | flops | bytes accessed | tf_op | source)
XLA Modules:
  0.0 207.9 jit_solution(6812227300992033164)
XLA Ops:
  0.7 2.8 %place.1 = bf16[640,768]{1,0:T(8,128)(2,1)} custom-call(s32[1,512]{1,0:T(1,128)} %bitcast.49, s32[1,512]{1,0:T(1,128)} %bitcast.47, bf16[512,768]{1,0:T(8,128)(2,1)} %c_ref.3), custom_call_target="tpu_custom_call" | custom-call | flops 1000000000 | bytes 3000000 | tf_op jit(solution)/shard_map/place/pallas_call | solution.py:324
  3.5 7.4 %all-to-all-start.1 = ((bf16[16,40,768]{2,1,0:T(8,128)(2,1)}), bf16[16,40,768]{2,1,0:T(8,128)(2,1)S(1)}, u32[]{:S(2)}, u32[]{:S(2)}) async-start(bf16[16,40,768]{2,1,0:T(8,128)(2,1)} %bitcast.43), calls=%async_computation.1 | async-start | bytes 1966080 | tf_op jit(solution)/shard_map/all_to_all | solution.py:677
  13.2 9.6 %attend.1 = (bf16[512,384]{1,0:T(8,128)(2,1)}, bf16[512,384]{1,0:T(8,128)(2,1)}, bf16[512,384]{1,0:T(8,128)(2,1)}, bf16[512,384]{1,0:T(8,128)(2,1)}, bf16[6,512,512]{2,1,0:T(8,128)(2,1)}, /*index=5*/s32[8,1024]{1,0:T(8,128)}) custom-call(bf16[512,768]{1,0:T(8,128)(2,1)} %x_ref.7, f32[768]{0:T(1024)} %gain_ref.11, bf16[768,384]{1,0:T(8,128)(2,1)} %wq_ref.3, ...), custom_call_target="tpu_custom_call" | custom-call | flops 8999999488 | bytes 9000000 | tf_op jit(solution)/shard_map/attend/pallas_call | solution.py:115
  25.0 9.3 %collective-permute-done.1.o_other_ref = bf16[512,384]{1,0:T(8,128)(2,1)S(1)} collective-permute-done((bf16[512,384]{1,0:T(8,128)(2,1)}, bf16[512,384]{1,0:T(8,128)(2,1)S(1)}, u32[]{:S(2)}, u32[]{:S(2)}) %collective-permute-start.1) | collective-permute-done | bytes 393248 | tf_op jit(solution)/shard_map/ppermute | solution.py:673
  35.0 4.5 %middle.1 = (f32[512,768]{1,0:T(8,128)}, bf16[640,768]{1,0:T(8,128)(2,1)}) custom-call(s32[5]{0:T(128)} %stack.23.place_ref, bf16[512,384]{1,0:T(8,128)(2,1)} %get-tuple-element.71.o_ref, bf16[512,384]{1,0:T(8,128)(2,1)} %copy-done.17, bf16[384,768]{1,0:T(8,128)(2,1)} %w_ref.5, bf16[192,768]{1,0:T(8,128)(2,1)} %copy-done.18, bf16[192,768]{1,0:T(8,128)(2,1)} %copy-done.19, ...), custom_call_target="tpu_custom_call" | custom-call | flops 2000000000 | bytes 6000000 | tf_op jit(solution)/shard_map/middle/pallas_call | solution.py:372
  39.5 5.8 %all-to-all-start = ((bf16[16,40,768]{2,1,0:T(8,128)(2,1)}), bf16[16,40,768]{2,1,0:T(8,128)(2,1)S(1)}, u32[]{:S(2)}, u32[]{:S(2)}) async-start(bf16[16,40,768]{2,1,0:T(8,128)(2,1)} %bitcast.45), calls=%async_computation | async-start | bytes 1966080 | tf_op jit(solution)/shard_map/all_to_all | solution.py:677
  45.5 21.7 %all-to-all-done = bf16[16,40,768]{2,1,0:T(8,128)(2,1)S(1)} async-done(((bf16[16,40,768]{2,1,0:T(8,128)(2,1)}), bf16[16,40,768]{2,1,0:T(8,128)(2,1)S(1)}, u32[]{:S(2)}, u32[]{:S(2)}) %all-to-all-start) | async-done | bytes 983072 | tf_op jit(solution)/shard_map/all_to_all | solution.py:677
  68.1 12.1 %expert.1 = (bf16[640,768]{1,0:T(8,128)(2,1)}, bf16[640,1536]{1,0:T(8,128)(2,1)}, bf16[640,1536]{1,0:T(8,128)(2,1)}, bf16[640,768]{1,0:T(8,128)(2,1)}, f32[640,1]{1,0:T(8,128)}, /*index=5*/f32[640,16]{1,0:T(8,128)}) custom-call(bf16[640,768]{1,0:T(8,128)(2,1)} %bitcast.39, bf16[640,768]{1,0:T(8,128)(2,1)} %bitcast.42, bf16[768,1536]{1,0:T(8,128)(2,1)} %bitcast.51, ...), custom_call_target="tpu_custom_call" | custom-call | flops 4499999744 | bytes 12000000 | tf_op jit(solution)/shard_map/expert/pallas_call | solution.py:598
  80.2 6.7 %all-to-all-start.2 = ((bf16[16,40,768]{2,1,0:T(8,128)(2,1)}), bf16[16,40,768]{2,1,0:T(8,128)(2,1)S(1)}, u32[]{:S(2)}, u32[]{:S(2)}) async-start(bf16[16,40,768]{2,1,0:T(8,128)(2,1)} %bitcast.44), calls=%async_computation.2 | async-start | bytes 1966080 | tf_op jit(solution)/shard_map/all_to_all | solution.py:677
  87.1 4.1 %multiply_convert_fusion = bf16[640,768]{1,0:T(8,128)(2,1)S(1)} fusion(bf16[640,1536]{1,0:T(8,128)(2,1)} %get-tuple-element.75, f32[640]{0:T(1024)S(1)} %reduce, bf16[1,1536,768]{2,1,0:T(8,128)(2,1)} %param.26), kind=kOutput, calls=%fused_computation.2 | convolution fusion | flops 1510932480 | bytes 5310976 | tf_op jit(solution)/shard_map/dot_general | solution.py:18
  91.8 4.3 %convolution_bitcast_fusion.1 = f32[1,1536,768]{2,1,0:T(8,128)} fusion(bf16[640,1536]{1,0:T(8,128)(2,1)S(1)} %copy-done.21, bf16[640,768]{1,0:T(8,128)(2,1)S(1)} %copy-done.22), kind=kOutput, calls=%fused_computation.1 | convolution fusion | flops 1509949440 | bytes 7667712 | tf_op jit(solution)/shard_map/dot_general | solution.py:26
  97.3 4.2 %convolution_bitcast_fusion = f32[1,768,1536]{2,1,0:T(8,128)} fusion(bf16[640,768]{1,0:T(8,128)(2,1)S(1)} %bitcast.41, bf16[640,1536]{1,0:T(8,128)(2,1)S(1)} %copy-done.20), kind=kOutput, calls=%fused_computation | convolution fusion | flops 1509949440 | bytes 7667712 | tf_op jit(solution)/shard_map/dot_general | solution.py:26
  101.5 3.4 %collective-permute-done.3 = bf16[640,384]{1,0:T(8,128)(2,1)S(1)} collective-permute-done((bf16[640,384]{1,0:T(8,128)(2,1)S(1)}, bf16[640,384]{1,0:T(8,128)(2,1)S(1)}, u32[]{:S(2)}, u32[]{:S(2)}) %collective-permute-start.3) | collective-permute-done | bytes 491552 | tf_op jit(solution)/shard_map/ppermute | solution.py:673
  105.8 2.9 %all-to-all-done.2 = bf16[16,40,768]{2,1,0:T(8,128)(2,1)S(1)} async-done(((bf16[16,40,768]{2,1,0:T(8,128)(2,1)}), bf16[16,40,768]{2,1,0:T(8,128)(2,1)S(1)}, u32[]{:S(2)}, u32[]{:S(2)}) %all-to-all-start.2) | async-done | bytes 983072 | tf_op jit(solution)/shard_map/all_to_all | solution.py:677
  111.7 6.5 %all-to-all-start.3 = ((bf16[16,40,384]{2,1,0:T(8,128)(2,1)}), bf16[16,40,384]{2,1,0:T(8,128)(2,1)S(1)}, u32[]{:S(2)}, u32[]{:S(2)}) async-start(bf16[16,40,384]{2,1,0:T(8,128)(2,1)} %bitcast.22), calls=%async_computation.3 | async-start | bytes 983040 | tf_op jit(solution)/shard_map/all_to_all | solution.py:677
  118.2 7.6 %collective-permute-done.5.got_ref = bf16[384,768]{1,0:T(8,128)(2,1)S(1)} collective-permute-done((bf16[384,768]{1,0:T(8,128)(2,1)S(1)}, bf16[384,768]{1,0:T(8,128)(2,1)S(1)}, u32[]{:S(2)}, u32[]{:S(2)}) %collective-permute-start.5) | collective-permute-done | bytes 589856 | tf_op jit(solution)/shard_map/ppermute | solution.py:673
  126.6 3.9 %middle_back.2 = (f32[512,768]{1,0:T(8,128)}, bf16[512,768]{1,0:T(8,128)(2,1)}, bf16[512,384]{1,0:T(8,128)(2,1)}, f32[1,768]{1,0:T(1,128)}) custom-call(bf16[384,768]{1,0:T(8,128)(2,1)} %copy-done, bf16[384,768]{1,0:T(8,128)(2,1)} %copy-done.10, f32[512,768]{1,0:T(8,128)} %get-tuple-element.84.hmid_ref, bf16[512,768]{1,0:T(8,128)(2,1)} %c_ref.3, ...), custom_call_target="tpu_custom_call" | custom-call | flops 1000000000 | bytes 6000000 | tf_op jit(solution)/shard_map/middle_back/pallas_call | solution.py:418
  131.2 2.5 %middle_back.3 = (f32[512,768]{1,0:T(8,128)}, bf16[512,768]{1,0:T(8,128)(2,1)}, bf16[512,384]{1,0:T(8,128)(2,1)}, f32[1,768]{1,0:T(1,128)}) custom-call(bf16[128,768]{1,0:T(8,128)(2,1)} %copy-done.2, bf16[128,768]{1,0:T(8,128)(2,1)} %copy-done.14, f32[512,768]{1,0:T(8,128)} %get-tuple-element.84.hmid_ref, ...), custom_call_target="tpu_custom_call", output_to_operand_aliasing={{0}: (6, {}), {1}: (7, {}), {2}: (8, {})} | custom-call | flops 1000000000 | bytes 6000000 | tf_op jit(solution)/shard_map/middle_back/pallas_call | solution.py:418
  133.7 13.5 %attend_back.1 = (bf16[512,768]{1,0:T(8,128)(2,1)}, bf16[832,768]{1,0:T(8,128)(2,1)}, bf16[832,768]{1,0:T(8,128)(2,1)}) custom-call(s32[1]{0:T(128)} %bitcast.side_ref, bf16[512,384]{1,0:T(8,128)(2,1)} %get-tuple-element.90.do_ref, bf16[512,384]{1,0:T(8,128)(2,1)} %get-tuple-element.91.q_ref, bf16[512,384]{1,0:T(8,128)(2,1)} %get-tuple-element.92.k_ref, ...), custom_call_target="tpu_custom_call" | custom-call | flops 12000000000 | bytes 9000000 | tf_op jit(solution)/shard_map/attend_back/pallas_call | solution.py:276
  147.3 3.2 %collective-permute-done.6 = bf16[832,768]{1,0:T(8,128)(2,1)S(1)} collective-permute-done((bf16[832,768]{1,0:T(8,128)(2,1)}, bf16[832,768]{1,0:T(8,128)(2,1)S(1)}, u32[]{:S(2)}, u32[]{:S(2)}) %collective-permute-start.6) | collective-permute-done | bytes 1277984 | tf_op jit(solution)/shard_map/ppermute | solution.py:635
  151.8 3.1 %collective-permute-start.8 = (bf16[224,768]{1,0:T(8,128)(2,1)S(1)}, bf16[224,768]{1,0:T(8,128)(2,1)S(1)}, u32[]{:S(2)}, u32[]{:S(2)}) collective-permute-start(bf16[224,768]{1,0:T(8,128)(2,1)S(1)} %get-tuple-element.129), channel_id=1, source_target_pairs={{0,8},{2,10},{4,12},{6,14},{8,0},{10,2},{12,4},{14,6},{16,24},{18,... | collective-permute-start | bytes 1032200 | tf_op jit(solution)/shard_map/ppermute | solution.py:635
  156.2 1.9 collective-permute-start.7
  159.2 5.9 %collective-permute-done.7 = bf16[192,768]{1,0:T(8,128)(2,1)S(1)} collective-permute-done((bf16[192,768]{1,0:T(8,128)(2,1)S(1)}, bf16[192,768]{1,0:T(8,128)(2,1)S(1)}, u32[]{:S(2)}, u32[]{:S(2)}) %collective-permute-start.7) | collective-permute-done | bytes 294944 | tf_op jit(solution)/shard_map/ppermute | solution.py:635
  167.5 3.2 %collective-permute-done.11 = bf16[112,768]{1,0:T(8,128)(2,1)S(1)} collective-permute-done((bf16[112,768]{1,0:T(8,128)(2,1)S(1)}, bf16[112,768]{1,0:T(8,128)(2,1)S(1)}, u32[]{:S(2)}, u32[]{:S(2)}) %collective-permute-start.11) | collective-permute-done | bytes 172064 | tf_op jit(solution)/shard_map/ppermute | solution.py:635
  170.8 2.3 %collective-permute-start.12 = (bf16[112,768]{1,0:T(8,128)(2,1)S(1)}, bf16[112,768]{1,0:T(8,128)(2,1)S(1)}, u32[]{:S(2)}, u32[]{:S(2)}) collective-permute-start(bf16[112,768]{1,0:T(8,128)(2,1)S(1)} %add_convert_fusion.6), channel_id=1, source_target_pairs={{0,16},{2,18},{4,20},{6,22},{8,24},{10,26},{12,28},{14,30},{16,0},... | collective-permute-start | bytes 516104 | tf_op jit(solution)/shard_map/ppermute | solution.py:635
  174.0 3.1 %collective-permute-done.13.got_ref = bf16[512,768]{1,0:T(8,128)(2,1)S(1)} collective-permute-done((bf16[512,768]{1,0:T(8,128)(2,1)S(1)}, bf16[512,768]{1,0:T(8,128)(2,1)S(1)}, u32[]{:S(2)}, u32[]{:S(2)}) %collective-permute-start.13) | collective-permute-done | bytes 786464 | tf_op jit(solution)/shard_map/ppermute | solution.py:673
  178.0 3.9 %input_back.1 = f32[512,768]{1,0:T(8,128)} custom-call(bf16[512,768]{1,0:T(8,128)(2,1)} %get-tuple-element.108.own_ref, bf16[512,768]{1,0:T(8,128)(2,1)} %copy-done.9, bf16[512,768]{1,0:T(8,128)(2,1)} %x_ref.7, f32[512,768]{1,0:T(8,128)} %get-tuple-element.109.dh_ref, f32[768]{0:T(1024)} %gain_ref.11), custom_call_target="tpu_custom_call" | custom-call | flops 100000000 | bytes 6000000 | tf_op jit(solution)/shard_map/input_back/pallas_call | solution.py:453
  182.4 3.9 %collective-permute-done.10 = bf16[96,768]{1,0:T(8,128)(2,1)S(1)} collective-permute-done((bf16[96,768]{1,0:T(8,128)(2,1)S(1)}, bf16[96,768]{1,0:T(8,128)(2,1)S(1)}, u32[]{:S(2)}, u32[]{:S(2)}) %collective-permute-start.10) | collective-permute-done | bytes 147488 | tf_op jit(solution)/shard_map/ppermute | solution.py:635
  188.2 3.4 %collective-permute-done.14 = bf16[96,768]{1,0:T(8,128)(2,1)S(1)} collective-permute-done((bf16[96,768]{1,0:T(8,128)(2,1)S(1)}, bf16[96,768]{1,0:T(8,128)(2,1)S(1)}, u32[]{:S(2)}, u32[]{:S(2)}) %collective-permute-start.14) | collective-permute-done | bytes 147488 | tf_op jit(solution)/shard_map/ppermute | solution.py:635
  191.6 2.2 %collective-permute-start.15 = (bf16[192,768]{1,0:T(8,128)(2,1)S(1)}, bf16[192,768]{1,0:T(8,128)(2,1)S(1)}, u32[]{:S(2)}, u32[]{:S(2)}) collective-permute-start(bf16[192,768]{1,0:T(8,128)(2,1)S(1)} %pad_maximum_fusion.3), channel_id=1, source_target_pairs={{0,4},{2,6},{4,0},{6,2},{8,12},{10,14},{12,8},{14,10},{16,20},{18,... | collective-permute-start | bytes 884744 | tf_op jit(solution)/shard_map/ppermute | solution.py:635
  195.2 2.7 %finish.1 = bf16[512,768]{1,0:T(8,128)(2,1)} custom-call(s32[5]{0:T(128)} %stack.23.place_ref, bf16[512,384]{1,0:T(8,128)(2,1)} %copy-done.1, bf16[512,384]{1,0:T(8,128)(2,1)} %copy-done.11, f32[512,768]{1,0:T(8,128)} %get-tuple-element.84.hmid_ref), custom_call_target="tpu_custom_call" | custom-call | flops 1000000 | bytes 4000000 | tf_op jit(solution)/shard_map/finish/pallas_call | solution.py:470
  204.9 3.1 %unpack.1 = (f32[768,384]{1,0:T(8,128)}, f32[768,384]{1,0:T(8,128)}, f32[768,384]{1,0:T(8,128)}, f32[384,768]{1,0:T(8,128)}, f32[16,768]{1,0:T(8,128)}, /*index=...) custom-call(s32[5]{0:T(128)S(1)} %copy-done.3, bf16[384,768]{1,0:T(8,128)(2,1)S(1)} %get-tuple-element.115.a_ref, ...), custom_call_target="tpu_custom_call" | custom-call | flops 100000000 | bytes 8000000 | tf_op jit(solution)/shard_map/unpack/pallas_call | solution.py:519
  (105 shorter events, 32.5 us)
Async XLA Ops:
  3.5 36.0 %all-to-all-start.1 = ((bf16[16,40,768]{2,1,0:T(8,128)(2,1)}), bf16[16,40,768]{2,1,0:T(8,128)(2,1)S(1)}, u32[]{:S(2)}, u32[]{:S(2)}) async-start(bf16[16,40,768]{2,1,0:T(8,128)(2,1)} %bitcast.43), calls=%async_computation.1 | async-start | bytes 1966080 | tf_op jit(solution)/shard_map/all_to_all | solution.py:677
  11.6 11.2 %collective-permute-start = (bf16[192,768]{1,0:T(8,128)(2,1)}, bf16[192,768]{1,0:T(8,128)(2,1)S(1)}, u32[]{:S(2)}, u32[]{:S(2)}) collective-permute-start(bf16[192,768]{1,0:T(8,128)(2,1)} %slice_select_fusion), channel_id=1, source_target_pairs={{0,1},{1,0},{2,3},{3,2},{4,5},{5,4},{6,7},{7,6},{8,9},{9,8},{10,11... | collective-permute-start | bytes 884744 | tf_op jit(solution)/shard_map/ppermute | solution.py:673
  22.8 11.5 %copy-start.18 = (bf16[192,768]{1,0:T(8,128)(2,1)}, bf16[192,768]{1,0:T(8,128)(2,1)S(1)}, u32[]{:S(2)}) copy-start(bf16[192,768]{1,0:T(8,128)(2,1)S(1)} %collective-permute-done.w_near_ref) | copy-start | bytes 884740
  22.8 11.4 %collective-permute-start.1 = (bf16[512,384]{1,0:T(8,128)(2,1)}, bf16[512,384]{1,0:T(8,128)(2,1)S(1)}, u32[]{:S(2)}, u32[]{:S(2)}) collective-permute-start(bf16[512,384]{1,0:T(8,128)(2,1)} %get-tuple-element.71.o_ref), channel_id=1, source_target_pairs={{0,1},{1,0},{2,3},{3,2},{4,5},{5,4},{6,7},{7,6},{8,9},{9,8},{10,11... | collective-permute-start | bytes 1179656 | tf_op jit(solution)/shard_map/ppermute | solution.py:673
  23.4 1.6 collective-permute-start.2
  39.5 27.7 %copy-start.7 = (bf16[16,40,768]{2,1,0:T(8,128)(2,1)}, bf16[16,40,768]{2,1,0:T(8,128)(2,1)S(1)}, u32[]{:S(2)}) copy-start(bf16[16,40,768]{2,1,0:T(8,128)(2,1)S(1)} %all-to-all-done.1) | copy-start | bytes 2949124
  39.5 27.6 %all-to-all-start = ((bf16[16,40,768]{2,1,0:T(8,128)(2,1)}), bf16[16,40,768]{2,1,0:T(8,128)(2,1)S(1)}, u32[]{:S(2)}, u32[]{:S(2)}) async-start(bf16[16,40,768]{2,1,0:T(8,128)(2,1)} %bitcast.45), calls=%async_computation | async-start | bytes 1966080 | tf_op jit(solution)/shard_map/all_to_all | solution.py:677
  80.2 28.5 %all-to-all-start.2 = ((bf16[16,40,768]{2,1,0:T(8,128)(2,1)}), bf16[16,40,768]{2,1,0:T(8,128)(2,1)S(1)}, u32[]{:S(2)}, u32[]{:S(2)}) async-start(bf16[16,40,768]{2,1,0:T(8,128)(2,1)} %bitcast.44), calls=%async_computation.2 | async-start | bytes 1966080 | tf_op jit(solution)/shard_map/all_to_all | solution.py:677
  91.2 13.6 %collective-permute-start.3 = (bf16[640,384]{1,0:T(8,128)(2,1)S(1)}, bf16[640,384]{1,0:T(8,128)(2,1)S(1)}, u32[]{:S(2)}, u32[]{:S(2)}) collective-permute-start(bf16[640,384]{1,0:T(8,128)(2,1)S(1)} %broadcast_select_fusion), channel_id=1, source_target_pairs={{0,1},{1,0},{2,3},{3,2},{4,5},{5,4},{6,7},{7,6},{8,9},{9,8},{10,11... | collective-permute-start | bytes 1474568 | tf_op jit(solution)/shard_map/ppermute | solution.py:673
  109.6 16.2 %copy-start = (bf16[384,768]{1,0:T(8,128)(2,1)}, bf16[384,768]{1,0:T(8,128)(2,1)S(1)}, u32[]{:S(2)}) copy-start(bf16[384,768]{1,0:T(8,128)(2,1)S(1)} %get-tuple-element.85.own_ref) | copy-start | bytes 1769476
  109.6 21.0 %copy-start.2 = (bf16[128,768]{1,0:T(8,128)(2,1)}, bf16[128,768]{1,0:T(8,128)(2,1)S(1)}, u32[]{:S(2)}) copy-start(bf16[128,768]{1,0:T(8,128)(2,1)S(1)} %get-tuple-element.83.own_ref) | copy-start | bytes 589828
  109.6 16.2 %collective-permute-start.5 = (bf16[384,768]{1,0:T(8,128)(2,1)S(1)}, bf16[384,768]{1,0:T(8,128)(2,1)S(1)}, u32[]{:S(2)}, u32[]{:S(2)}) collective-permute-start(bf16[384,768]{1,0:T(8,128)(2,1)S(1)} %get-tuple-element.85.own_ref), channel_id=1, source_target_pairs={{0,1},{1,0},{2,3},{3,2},{4,5},{5,4},{6,7},{7,6},{8,9},{9,8},{10,11... | collective-permute-start | bytes 1769480 | tf_op jit(solution)/shard_map/ppermute | solution.py:673
  110.1 20.4 %collective-permute-start.4 = (bf16[128,768]{1,0:T(8,128)(2,1)S(1)}, bf16[128,768]{1,0:T(8,128)(2,1)S(1)}, u32[]{:S(2)}, u32[]{:S(2)}) collective-permute-start(bf16[128,768]{1,0:T(8,128)(2,1)S(1)} %get-tuple-element.83.own_ref), channel_id=1, source_target_pairs={{0,1},{1,0},{2,3},{3,2},{4,5},{5,4},{6,7},{7,6},{8,9},{9,8},{10,11... | collective-permute-start | bytes 589832 | tf_op jit(solution)/shard_map/ppermute | solution.py:673
  111.7 35.6 %all-to-all-start.3 = ((bf16[16,40,384]{2,1,0:T(8,128)(2,1)}), bf16[16,40,384]{2,1,0:T(8,128)(2,1)S(1)}, u32[]{:S(2)}, u32[]{:S(2)}) async-start(bf16[16,40,384]{2,1,0:T(8,128)(2,1)} %bitcast.22), calls=%async_computation.3 | async-start | bytes 983040 | tf_op jit(solution)/shard_map/all_to_all | solution.py:677
  147.2 10.9 %copy-start.8 = (bf16[512,768]{1,0:T(8,128)(2,1)S(1)}, bf16[512,768]{1,0:T(8,128)(2,1)}, u32[]{:S(2)}) copy-start(bf16[512,768]{1,0:T(8,128)(2,1)} %get-tuple-element.108.own_ref) | copy-start | bytes 2359300
  147.2 3.3 %collective-permute-start.6 = (bf16[832,768]{1,0:T(8,128)(2,1)}, bf16[832,768]{1,0:T(8,128)(2,1)S(1)}, u32[]{:S(2)}, u32[]{:S(2)}) collective-permute-start(bf16[832,768]{1,0:T(8,128)(2,1)} %get-tuple-element.104), channel_id=1, source_target_pairs={{0,2},{2,0},{4,6},{6,4},{8,10},{10,8},{12,14},{14,12},{16,18},{18,... | collective-permute-start | bytes 3833864 | tf_op jit(solution)/shard_map/ppermute | solution.py:635
  151.8 13.3 %collective-permute-start.8 = (bf16[224,768]{1,0:T(8,128)(2,1)S(1)}, bf16[224,768]{1,0:T(8,128)(2,1)S(1)}, u32[]{:S(2)}, u32[]{:S(2)}) collective-permute-start(bf16[224,768]{1,0:T(8,128)(2,1)S(1)} %get-tuple-element.129), channel_id=1, source_target_pairs={{0,8},{2,10},{4,12},{6,14},{8,0},{10,2},{12,4},{14,6},{16,24},{18,... | collective-permute-start | bytes 1032200 | tf_op jit(solution)/shard_map/ppermute | solution.py:635
  156.2 8.9 %collective-permute-start.7 = (bf16[192,768]{1,0:T(8,128)(2,1)S(1)}, bf16[192,768]{1,0:T(8,128)(2,1)S(1)}, u32[]{:S(2)}, u32[]{:S(2)}) collective-permute-start(bf16[192,768]{1,0:T(8,128)(2,1)S(1)} %get-tuple-element.130), channel_id=1, source_target_pairs={{0,4},{2,6},{4,0},{6,2},{8,12},{10,14},{12,8},{14,10},{16,20},{18,... | collective-permute-start | bytes 884744 | tf_op jit(solution)/shard_map/ppermute | solution.py:635
  158.1 19.0 %collective-permute-start.13 = (bf16[512,768]{1,0:T(8,128)(2,1)S(1)}, bf16[512,768]{1,0:T(8,128)(2,1)S(1)}, u32[]{:S(2)}, u32[]{:S(2)}) collective-permute-start(bf16[512,768]{1,0:T(8,128)(2,1)S(1)} %copy-done.8), channel_id=1, source_target_pairs={{0,1},{1,0},{2,3},{3,2},{4,5},{5,4},{6,7},{7,6},{8,9},{9,8},{10,11... | collective-permute-start | bytes 2359304 | tf_op jit(solution)/shard_map/ppermute | solution.py:673
  159.2 22.7 %copy-start.1 = (bf16[512,384]{1,0:T(8,128)(2,1)}, bf16[512,384]{1,0:T(8,128)(2,1)S(1)}, u32[]{:S(2)}) copy-start(bf16[512,384]{1,0:T(8,128)(2,1)S(1)} %pick.3.y_ref) | copy-start | bytes 1179652
  165.2 5.5 %collective-permute-start.11 = (bf16[112,768]{1,0:T(8,128)(2,1)S(1)}, bf16[112,768]{1,0:T(8,128)(2,1)S(1)}, u32[]{:S(2)}, u32[]{:S(2)}) collective-permute-start(bf16[112,768]{1,0:T(8,128)(2,1)S(1)} %add_convert_fusion.7), channel_id=1, source_target_pairs={{0,4},{2,6},{4,0},{6,2},{8,12},{10,14},{12,8},{14,10},{16,20},{18,... | collective-permute-start | bytes 516104 | tf_op jit(solution)/shard_map/ppermute | solution.py:635
  167.1 6.0 %collective-permute-start.9 = (bf16[96,768]{1,0:T(8,128)(2,1)S(1)}, bf16[96,768]{1,0:T(8,128)(2,1)S(1)}, u32[]{:S(2)}, u32[]{:S(2)}) collective-permute-start(bf16[96,768]{1,0:T(8,128)(2,1)S(1)} %add_convert_fusion.11), channel_id=1, source_target_pairs={{0,8},{2,10},{4,12},{6,14},{8,0},{10,2},{12,4},{14,6},{16,24},{18,... | collective-permute-start | bytes 442376 | tf_op jit(solution)/shard_map/ppermute | solution.py:635
  170.8 15.5 %collective-permute-start.12 = (bf16[112,768]{1,0:T(8,128)(2,1)S(1)}, bf16[112,768]{1,0:T(8,128)(2,1)S(1)}, u32[]{:S(2)}, u32[]{:S(2)}) collective-permute-start(bf16[112,768]{1,0:T(8,128)(2,1)S(1)} %add_convert_fusion.6), channel_id=1, source_target_pairs={{0,16},{2,18},{4,20},{6,22},{8,24},{10,26},{12,28},{14,30},{16,0},... | collective-permute-start | bytes 516104 | tf_op jit(solution)/shard_map/ppermute | solution.py:635
  173.2 13.1 %collective-permute-start.10 = (bf16[96,768]{1,0:T(8,128)(2,1)S(1)}, bf16[96,768]{1,0:T(8,128)(2,1)S(1)}, u32[]{:S(2)}, u32[]{:S(2)}) collective-permute-start(bf16[96,768]{1,0:T(8,128)(2,1)S(1)} %add_convert_fusion.10), channel_id=1, source_target_pairs={{0,16},{2,18},{4,20},{6,22},{8,24},{10,26},{12,28},{14,30},{16,0},... | collective-permute-start | bytes 442376 | tf_op jit(solution)/shard_map/ppermute | solution.py:635
  181.9 12.5 %collective-permute-start.19 = (bf16[512,384]{1,0:T(8,128)(2,1)S(1)}, bf16[512,384]{1,0:T(8,128)(2,1)S(1)}, u32[]{:S(2)}, u32[]{:S(2)}) collective-permute-start(bf16[512,384]{1,0:T(8,128)(2,1)S(1)} %pick.3.y_ref), channel_id=1, source_target_pairs={{0,1},{1,0},{2,3},{3,2},{4,5},{5,4},{6,7},{7,6},{8,9},{9,8},{10,11... | collective-permute-start | bytes 1179656 | tf_op jit(solution)/shard_map/ppermute | solution.py:673
  186.3 5.2 %collective-permute-start.14 = (bf16[96,768]{1,0:T(8,128)(2,1)S(1)}, bf16[96,768]{1,0:T(8,128)(2,1)S(1)}, u32[]{:S(2)}, u32[]{:S(2)}) collective-permute-start(bf16[96,768]{1,0:T(8,128)(2,1)S(1)} %add_convert_fusion.9), channel_id=1, source_target_pairs={{0,8},{2,10},{4,12},{6,14},{8,0},{10,2},{12,4},{14,6},{16,24},{18,... | collective-permute-start | bytes 442376 | tf_op jit(solution)/shard_map/ppermute | solution.py:635
  186.7 7.0 %collective-permute-start.16 = (bf16[112,768]{1,0:T(8,128)(2,1)S(1)}, bf16[112,768]{1,0:T(8,128)(2,1)S(1)}, u32[]{:S(2)}, u32[]{:S(2)}) collective-permute-start(bf16[112,768]{1,0:T(8,128)(2,1)S(1)} %add_convert_fusion.5), channel_id=1, source_target_pairs={{0,4},{2,6},{4,0},{6,2},{8,12},{10,14},{12,8},{14,10},{16,20},{18,... | collective-permute-start | bytes 516104 | tf_op jit(solution)/shard_map/ppermute | solution.py:635
  191.6 8.3 %collective-permute-start.15 = (bf16[192,768]{1,0:T(8,128)(2,1)S(1)}, bf16[192,768]{1,0:T(8,128)(2,1)S(1)}, u32[]{:S(2)}, u32[]{:S(2)}) collective-permute-start(bf16[192,768]{1,0:T(8,128)(2,1)S(1)} %pad_maximum_fusion.3), channel_id=1, source_target_pairs={{0,4},{2,6},{4,0},{6,2},{8,12},{10,14},{12,8},{14,10},{16,20},{18,... | collective-permute-start | bytes 884744 | tf_op jit(solution)/shard_map/ppermute | solution.py:635
  193.8 7.7 %collective-permute-start.17 = (bf16[192,768]{1,0:T(8,128)(2,1)S(1)}, bf16[192,768]{1,0:T(8,128)(2,1)S(1)}, u32[]{:S(2)}, u32[]{:S(2)}) collective-permute-start(bf16[192,768]{1,0:T(8,128)(2,1)S(1)} %pad_maximum_fusion.2), channel_id=1, source_target_pairs={{0,8},{2,10},{4,12},{6,14},{8,0},{10,2},{12,4},{14,6},{16,24},{18,... | collective-permute-start | bytes 884744 | tf_op jit(solution)/shard_map/ppermute | solution.py:635
  197.9 4.1 %collective-permute-start.18 = (bf16[32,768]{1,0:T(8,128)(2,1)S(1)}, bf16[32,768]{1,0:T(8,128)(2,1)S(1)}, u32[]{:S(2)}, u32[]{:S(2)}) collective-permute-start(bf16[32,768]{1,0:T(8,128)(2,1)S(1)} %slice.112.small_ref), channel_id=1, source_target_pairs={{0,1},{1,0},{2,3},{3,2},{4,5},{5,4},{6,7},{7,6},{8,9},{9,8},{10,11... | collective-permute-start | bytes 147464 | tf_op jit(solution)/shard_map/ppermute | solution.py:673
  202.0 2.0 collective-permute-start.20
  202.0 2.8 %collective-permute-start.21 = (bf16[384,768]{1,0:T(8,128)(2,1)S(1)}, bf16[384,768]{1,0:T(8,128)(2,1)S(1)}, u32[]{:S(2)}, u32[]{:S(2)}) collective-permute-start(bf16[384,768]{1,0:T(8,128)(2,1)S(1)} %get-tuple-element.116.b_ref), channel_id=1, source_target_pairs={{0,2},{2,0},{4,6},{6,4},{8,10},{10,8},{12,14},{14,12},{16,18},{18,... | collective-permute-start | bytes 1769480 | tf_op jit(solution)/shard_map/ppermute | solution.py:635
  (17 other events, 71.0 us)

commit v4 on v3

--- a/solution.py
+++ b/solution.py
@@ -72,9 +72,10 @@
         ids_ref[...] = ids
 
     normed = n_ref[...]
-    q = dot(normed, wq_ref[...]).astype(bf16)
-    k = dot(normed, wk_ref[...]).astype(bf16)
-    v = dot(normed, wv_ref[...]).astype(bf16)
+    span = 2 * half
+    weight = jnp.concatenate([wq_ref[...], wk_ref[...], wv_ref[...]], axis=1)
+    qkv = dot(normed, weight).astype(bf16)
+    q, k, v = qkv[:, :span], qkv[:, span : 2 * span], qkv[:, 2 * span :]
     q_ref[...] = q
     k_ref[...] = k
     v_ref[...] = v
@@ -214,18 +215,17 @@
     dq_low = (dq * scale).astype(bf16)
     dk_turned = (jnp.concatenate(dk_parts, axis=0) * scale).astype(bf16)
     dv_turned = jnp.concatenate(dv_parts, axis=0).astype(bf16)
-    part = (
-        contract_last(dq_low, wq_ref[...])
-        + contract_last(dk_turned.T, wk_ref[...])
-        + contract_last(dv_turned.T, wv_ref[...])
+    part = contract_last(
+        jnp.concatenate([dq_low, dk_turned.T, dv_turned.T], axis=1),
+        jnp.concatenate([wq_ref[...], wk_ref[...], wv_ref[...]], axis=1),
     )
     normed = n_ref[...]
     here = pl.ds(pl.multiple_of(pair * span, span), span)
-    grad_k = dot(dk_turned, normed).astype(bf16)
-    grad_v = dot(dv_turned, normed).astype(bf16)
+    turned = jnp.concatenate([dk_turned, dv_turned, dq_low.T], axis=0)
+    grads = dot(turned, normed).astype(bf16)
+    grad_k, grad_v, grad_q = grads[:span], grads[span : 2 * span], grads[2 * span :]
     keep_ref[here, :] = jnp.where(even, grad_k, grad_v)
     send_ref[here, :] = jnp.where(even, grad_v, grad_k)
-    grad_q = dot(dq_low.T, normed).astype(bf16)
     grad_o = dot(o_ref[...].T, da_ref[...]).astype(bf16)
     keep = jnp.where(even, grad_q, grad_o)
     send = jnp.where(even, grad_o, grad_q)

time: 209 us -> 208 us (level)
  no operation moved by 1% of the time
where the time goes in v4:
time: 208 us; the launch traced here: 207 us
  waiting for transfers between devices  73.9 us (36%)
  Pallas kernels  59.6 us (29%)
  starting transfers between devices  48 us (23%)
  matrix products  13.8 us (7%)
  local copies, waits for them, and re-layouts  5.65 us (3%)
  other arithmetic  5.33 us (3%)
    all_to_all x4, starting transfers between devices, to_experts(): lax.all_to_all(block, 'dp', split_axis=0, concat_axis=0, tiled=True)  26.3 us
    ppermute x14, waiting for transfers between devices, exchange(): return lax.ppermute(value, 'dp', [(i, i ^ 1 << bit) for i in range(count)])  25.7 us
    all_to_all x4, waiting for transfers between devices, to_experts(): lax.all_to_all(block, 'dp', split_axis=0, concat_axis=0, tiled=True)  24.6 us
    ppermute x8, waiting for transfers between devices, swapped(): return lax.ppermute(value, 'mp', swap)  23.7 us
    ppermute x14, starting transfers between devices, exchange(): return lax.ppermute(value, 'dp', [(i, i ^ 1 << bit) for i in range(count)])  15.4 us
    pallas_call x1, Pallas kernels, attend_back(): pl.pallas_call(functools.partial(attend_back_kernel, buckets), grid=(head...  13.2 us
    pallas_call x1, Pallas kernels, expert(): pl.pallas_call(expert_kernel, grid=(hidden // step,), in_specs=[whole((ro...  12.1 us
    dot_general x3, matrix products, contract_rows(): lax.dot_general(left, right, (((0,), (0,)), ((), ())), preferred_element_...  9.69 us
  transfers between devices with their start and end apart: 26, of which 17 were waited for; matrix products, arithmetic and copies ran while one was open for 9% of the time, Pallas kernels for 20%

profile of v4, /device:TPU:0, one launch (start us, length us, event | category | flops | bytes accessed | tf_op | source)
XLA Modules:
  0.0 207.3 jit_solution(1392136697409032659)
XLA Ops:
  0.7 2.8 %place.1 = bf16[640,768]{1,0:T(8,128)(2,1)} custom-call(s32[1,512]{1,0:T(1,128)} %bitcast.49, s32[1,512]{1,0:T(1,128)} %bitcast.47, bf16[512,768]{1,0:T(8,128)(2,1)} %c_ref.3), custom_call_target="tpu_custom_call" | custom-call | flops 1000000000 | bytes 3000000 | tf_op jit(solution)/shard_map/place/pallas_call | solution.py:324
  3.5 7.4 %all-to-all-start.1 = ((bf16[16,40,768]{2,1,0:T(8,128)(2,1)}), bf16[16,40,768]{2,1,0:T(8,128)(2,1)S(1)}, u32[]{:S(2)}, u32[]{:S(2)}) async-start(bf16[16,40,768]{2,1,0:T(8,128)(2,1)} %bitcast.43), calls=%async_computation.1 | async-start | bytes 1966080 | tf_op jit(solution)/shard_map/all_to_all | solution.py:677
  13.2 9.3 %attend.1 = (bf16[512,384]{1,0:T(8,128)(2,1)}, bf16[512,384]{1,0:T(8,128)(2,1)}, bf16[512,384]{1,0:T(8,128)(2,1)}, bf16[512,384]{1,0:T(8,128)(2,1)}, bf16[6,512,512]{2,1,0:T(8,128)(2,1)}, /*index=5*/s32[8,1024]{1,0:T(8,128)}) custom-call(bf16[512,768]{1,0:T(8,128)(2,1)} %x_ref.7, f32[768]{0:T(1024)} %gain_ref.11, bf16[768,384]{1,0:T(8,128)(2,1)} %wq_ref.3, ...), custom_call_target="tpu_custom_call" | custom-call | flops 8999999488 | bytes 9000000 | tf_op jit(solution)/shard_map/attend/pallas_call | solution.py:116
  24.7 9.3 %collective-permute-done.1.o_other_ref = bf16[512,384]{1,0:T(8,128)(2,1)S(1)} collective-permute-done((bf16[512,384]{1,0:T(8,128)(2,1)}, bf16[512,384]{1,0:T(8,128)(2,1)S(1)}, u32[]{:S(2)}, u32[]{:S(2)}) %collective-permute-start.1) | collective-permute-done | bytes 393248 | tf_op jit(solution)/shard_map/ppermute | solution.py:673
  34.7 4.5 %middle.1 = (f32[512,768]{1,0:T(8,128)}, bf16[640,768]{1,0:T(8,128)(2,1)}) custom-call(s32[5]{0:T(128)} %stack.23.place_ref, bf16[512,384]{1,0:T(8,128)(2,1)} %get-tuple-element.71.o_ref, bf16[512,384]{1,0:T(8,128)(2,1)} %copy-done.17, bf16[384,768]{1,0:T(8,128)(2,1)} %w_ref.5, bf16[192,768]{1,0:T(8,128)(2,1)} %copy-done.18, bf16[192,768]{1,0:T(8,128)(2,1)} %copy-done.19, ...), custom_call_target="tpu_custom_call" | custom-call | flops 2000000000 | bytes 6000000 | tf_op jit(solution)/shard_map/middle/pallas_call | solution.py:372
  39.2 5.7 %all-to-all-start = ((bf16[16,40,768]{2,1,0:T(8,128)(2,1)}), bf16[16,40,768]{2,1,0:T(8,128)(2,1)S(1)}, u32[]{:S(2)}, u32[]{:S(2)}) async-start(bf16[16,40,768]{2,1,0:T(8,128)(2,1)} %bitcast.45), calls=%async_computation | async-start | bytes 1966080 | tf_op jit(solution)/shard_map/all_to_all | solution.py:677
  45.2 21.7 %all-to-all-done = bf16[16,40,768]{2,1,0:T(8,128)(2,1)S(1)} async-done(((bf16[16,40,768]{2,1,0:T(8,128)(2,1)}), bf16[16,40,768]{2,1,0:T(8,128)(2,1)S(1)}, u32[]{:S(2)}, u32[]{:S(2)}) %all-to-all-start) | async-done | bytes 983072 | tf_op jit(solution)/shard_map/all_to_all | solution.py:677
  67.8 12.1 %expert.1 = (bf16[640,768]{1,0:T(8,128)(2,1)}, bf16[640,1536]{1,0:T(8,128)(2,1)}, bf16[640,1536]{1,0:T(8,128)(2,1)}, bf16[640,768]{1,0:T(8,128)(2,1)}, f32[640,1]{1,0:T(8,128)}, /*index=5*/f32[640,16]{1,0:T(8,128)}) custom-call(bf16[640,768]{1,0:T(8,128)(2,1)} %bitcast.39, bf16[640,768]{1,0:T(8,128)(2,1)} %bitcast.42, bf16[768,1536]{1,0:T(8,128)(2,1)} %bitcast.51, ...), custom_call_target="tpu_custom_call" | custom-call | flops 4499999744 | bytes 12000000 | tf_op jit(solution)/shard_map/expert/pallas_call | solution.py:598
  79.8 6.7 %all-to-all-start.2 = ((bf16[16,40,768]{2,1,0:T(8,128)(2,1)}), bf16[16,40,768]{2,1,0:T(8,128)(2,1)S(1)}, u32[]{:S(2)}, u32[]{:S(2)}) async-start(bf16[16,40,768]{2,1,0:T(8,128)(2,1)} %bitcast.44), calls=%async_computation.2 | async-start | bytes 1966080 | tf_op jit(solution)/shard_map/all_to_all | solution.py:677
  86.7 4.1 %multiply_convert_fusion = bf16[640,768]{1,0:T(8,128)(2,1)S(1)} fusion(bf16[640,1536]{1,0:T(8,128)(2,1)} %get-tuple-element.75, f32[640]{0:T(1024)S(1)} %reduce, bf16[1,1536,768]{2,1,0:T(8,128)(2,1)} %param.26), kind=kOutput, calls=%fused_computation.2 | convolution fusion | flops 1510932480 | bytes 5310976 | tf_op jit(solution)/shard_map/dot_general | solution.py:18
  91.5 4.3 %convolution_bitcast_fusion.1 = f32[1,1536,768]{2,1,0:T(8,128)} fusion(bf16[640,1536]{1,0:T(8,128)(2,1)S(1)} %copy-done.21, bf16[640,768]{1,0:T(8,128)(2,1)S(1)} %copy-done.22), kind=kOutput, calls=%fused_computation.1 | convolution fusion | flops 1509949440 | bytes 7667712 | tf_op jit(solution)/shard_map/dot_general | solution.py:26
  97.0 4.2 %convolution_bitcast_fusion = f32[1,768,1536]{2,1,0:T(8,128)} fusion(bf16[640,768]{1,0:T(8,128)(2,1)S(1)} %bitcast.41, bf16[640,1536]{1,0:T(8,128)(2,1)S(1)} %copy-done.20), kind=kOutput, calls=%fused_computation | convolution fusion | flops 1509949440 | bytes 7667712 | tf_op jit(solution)/shard_map/dot_general | solution.py:26
  101.2 3.3 %collective-permute-done.3 = bf16[640,384]{1,0:T(8,128)(2,1)S(1)} collective-permute-done((bf16[640,384]{1,0:T(8,128)(2,1)S(1)}, bf16[640,384]{1,0:T(8,128)(2,1)S(1)}, u32[]{:S(2)}, u32[]{:S(2)}) %collective-permute-start.3) | collective-permute-done | bytes 491552 | tf_op jit(solution)/shard_map/ppermute | solution.py:673
  105.5 2.9 %all-to-all-done.2 = bf16[16,40,768]{2,1,0:T(8,128)(2,1)S(1)} async-done(((bf16[16,40,768]{2,1,0:T(8,128)(2,1)}), bf16[16,40,768]{2,1,0:T(8,128)(2,1)S(1)}, u32[]{:S(2)}, u32[]{:S(2)}) %all-to-all-start.2) | async-done | bytes 983072 | tf_op jit(solution)/shard_map/all_to_all | solution.py:677
  111.4 6.5 %all-to-all-start.3 = ((bf16[16,40,384]{2,1,0:T(8,128)(2,1)}), bf16[16,40,384]{2,1,0:T(8,128)(2,1)S(1)}, u32[]{:S(2)}, u32[]{:S(2)}) async-start(bf16[16,40,384]{2,1,0:T(8,128)(2,1)} %bitcast.22), calls=%async_computation.3 | async-start | bytes 983040 | tf_op jit(solution)/shard_map/all_to_all | solution.py:677
  117.9 7.6 %collective-permute-done.5.got_ref = bf16[384,768]{1,0:T(8,128)(2,1)S(1)} collective-permute-done((bf16[384,768]{1,0:T(8,128)(2,1)S(1)}, bf16[384,768]{1,0:T(8,128)(2,1)S(1)}, u32[]{:S(2)}, u32[]{:S(2)}) %collective-permute-start.5) | collective-permute-done | bytes 589856 | tf_op jit(solution)/shard_map/ppermute | solution.py:673
  126.3 3.9 %middle_back.2 = (f32[512,768]{1,0:T(8,128)}, bf16[512,768]{1,0:T(8,128)(2,1)}, bf16[512,384]{1,0:T(8,128)(2,1)}, f32[1,768]{1,0:T(1,128)}) custom-call(bf16[384,768]{1,0:T(8,128)(2,1)} %copy-done, bf16[384,768]{1,0:T(8,128)(2,1)} %copy-done.10, f32[512,768]{1,0:T(8,128)} %get-tuple-element.84.hmid_ref, bf16[512,768]{1,0:T(8,128)(2,1)} %c_ref.3, ...), custom_call_target="tpu_custom_call" | custom-call | flops 1000000000 | bytes 6000000 | tf_op jit(solution)/shard_map/middle_back/pallas_call | solution.py:418
  130.9 2.5 %middle_back.3 = (f32[512,768]{1,0:T(8,128)}, bf16[512,768]{1,0:T(8,128)(2,1)}, bf16[512,384]{1,0:T(8,128)(2,1)}, f32[1,768]{1,0:T(1,128)}) custom-call(bf16[128,768]{1,0:T(8,128)(2,1)} %copy-done.2, bf16[128,768]{1,0:T(8,128)(2,1)} %copy-done.14, f32[512,768]{1,0:T(8,128)} %get-tuple-element.84.hmid_ref, ...), custom_call_target="tpu_custom_call", output_to_operand_aliasing={{0}: (6, {}), {1}: (7, {}), {2}: (8, {})} | custom-call | flops 1000000000 | bytes 6000000 | tf_op jit(solution)/shard_map/middle_back/pallas_call | solution.py:418
  133.4 13.2 %attend_back.1 = (bf16[512,768]{1,0:T(8,128)(2,1)}, bf16[832,768]{1,0:T(8,128)(2,1)}, bf16[832,768]{1,0:T(8,128)(2,1)}) custom-call(s32[1]{0:T(128)} %bitcast.side_ref, bf16[512,384]{1,0:T(8,128)(2,1)} %get-tuple-element.90.do_ref, bf16[512,384]{1,0:T(8,128)(2,1)} %get-tuple-element.91.q_ref, bf16[512,384]{1,0:T(8,128)(2,1)} %get-tuple-element.92.k_ref, ...), custom_call_target="tpu_custom_call" | custom-call | flops 12000000000 | bytes 9000000 | tf_op jit(solution)/shard_map/attend_back/pallas_call | solution.py:276
  146.7 3.2 %collective-permute-done.6 = bf16[832,768]{1,0:T(8,128)(2,1)S(1)} collective-permute-done((bf16[832,768]{1,0:T(8,128)(2,1)}, bf16[832,768]{1,0:T(8,128)(2,1)S(1)}, u32[]{:S(2)}, u32[]{:S(2)}) %collective-permute-start.6) | collective-permute-done | bytes 1277984 | tf_op jit(solution)/shard_map/ppermute | solution.py:635
  151.3 3.1 %collective-permute-start.8 = (bf16[224,768]{1,0:T(8,128)(2,1)S(1)}, bf16[224,768]{1,0:T(8,128)(2,1)S(1)}, u32[]{:S(2)}, u32[]{:S(2)}) collective-permute-start(bf16[224,768]{1,0:T(8,128)(2,1)S(1)} %get-tuple-element.129), channel_id=1, source_target_pairs={{0,8},{2,10},{4,12},{6,14},{8,0},{10,2},{12,4},{14,6},{16,24},{18,... | collective-permute-start | bytes 1032200 | tf_op jit(solution)/shard_map/ppermute | solution.py:635
  155.6 1.9 collective-permute-start.7
  158.7 5.9 %collective-permute-done.7 = bf16[192,768]{1,0:T(8,128)(2,1)S(1)} collective-permute-done((bf16[192,768]{1,0:T(8,128)(2,1)S(1)}, bf16[192,768]{1,0:T(8,128)(2,1)S(1)}, u32[]{:S(2)}, u32[]{:S(2)}) %collective-permute-start.7) | collective-permute-done | bytes 294944 | tf_op jit(solution)/shard_map/ppermute | solution.py:635
  166.9 3.2 %collective-permute-done.11 = bf16[112,768]{1,0:T(8,128)(2,1)S(1)} collective-permute-done((bf16[112,768]{1,0:T(8,128)(2,1)S(1)}, bf16[112,768]{1,0:T(8,128)(2,1)S(1)}, u32[]{:S(2)}, u32[]{:S(2)}) %collective-permute-start.11) | collective-permute-done | bytes 172064 | tf_op jit(solution)/shard_map/ppermute | solution.py:635
  170.2 2.3 %collective-permute-start.12 = (bf16[112,768]{1,0:T(8,128)(2,1)S(1)}, bf16[112,768]{1,0:T(8,128)(2,1)S(1)}, u32[]{:S(2)}, u32[]{:S(2)}) collective-permute-start(bf16[112,768]{1,0:T(8,128)(2,1)S(1)} %add_convert_fusion.6), channel_id=1, source_target_pairs={{0,16},{2,18},{4,20},{6,22},{8,24},{10,26},{12,28},{14,30},{16,0},... | collective-permute-start | bytes 516104 | tf_op jit(solution)/shard_map/ppermute | solution.py:635
  173.4 3.1 %collective-permute-done.13.got_ref = bf16[512,768]{1,0:T(8,128)(2,1)S(1)} collective-permute-done((bf16[512,768]{1,0:T(8,128)(2,1)S(1)}, bf16[512,768]{1,0:T(8,128)(2,1)S(1)}, u32[]{:S(2)}, u32[]{:S(2)}) %collective-permute-start.13) | collective-permute-done | bytes 786464 | tf_op jit(solution)/shard_map/ppermute | solution.py:673
  177.4 3.9 %input_back.1 = f32[512,768]{1,0:T(8,128)} custom-call(bf16[512,768]{1,0:T(8,128)(2,1)} %get-tuple-element.108.own_ref, bf16[512,768]{1,0:T(8,128)(2,1)} %copy-done.9, bf16[512,768]{1,0:T(8,128)(2,1)} %x_ref.7, f32[512,768]{1,0:T(8,128)} %get-tuple-element.109.dh_ref, f32[768]{0:T(1024)} %gain_ref.11), custom_call_target="tpu_custom_call" | custom-call | flops 100000000 | bytes 6000000 | tf_op jit(solution)/shard_map/input_back/pallas_call | solution.py:453
  181.9 3.8 %collective-permute-done.10 = bf16[96,768]{1,0:T(8,128)(2,1)S(1)} collective-permute-done((bf16[96,768]{1,0:T(8,128)(2,1)S(1)}, bf16[96,768]{1,0:T(8,128)(2,1)S(1)}, u32[]{:S(2)}, u32[]{:S(2)}) %collective-permute-start.10) | collective-permute-done | bytes 147488 | tf_op jit(solution)/shard_map/ppermute | solution.py:635
  187.6 3.4 %collective-permute-done.14 = bf16[96,768]{1,0:T(8,128)(2,1)S(1)} collective-permute-done((bf16[96,768]{1,0:T(8,128)(2,1)S(1)}, bf16[96,768]{1,0:T(8,128)(2,1)S(1)}, u32[]{:S(2)}, u32[]{:S(2)}) %collective-permute-start.14) | collective-permute-done | bytes 147488 | tf_op jit(solution)/shard_map/ppermute | solution.py:635
  191.0 2.2 %collective-permute-start.15 = (bf16[192,768]{1,0:T(8,128)(2,1)S(1)}, bf16[192,768]{1,0:T(8,128)(2,1)S(1)}, u32[]{:S(2)}, u32[]{:S(2)}) collective-permute-start(bf16[192,768]{1,0:T(8,128)(2,1)S(1)} %pad_maximum_fusion.3), channel_id=1, source_target_pairs={{0,4},{2,6},{4,0},{6,2},{8,12},{10,14},{12,8},{14,10},{16,20},{18,... | collective-permute-start | bytes 884744 | tf_op jit(solution)/shard_map/ppermute | solution.py:635
  194.6 2.7 %finish.1 = bf16[512,768]{1,0:T(8,128)(2,1)} custom-call(s32[5]{0:T(128)} %stack.23.place_ref, bf16[512,384]{1,0:T(8,128)(2,1)} %copy-done.1, bf16[512,384]{1,0:T(8,128)(2,1)} %copy-done.11, f32[512,768]{1,0:T(8,128)} %get-tuple-element.84.hmid_ref), custom_call_target="tpu_custom_call" | custom-call | flops 1000000 | bytes 4000000 | tf_op jit(solution)/shard_map/finish/pallas_call | solution.py:470
  204.3 3.1 %unpack.1 = (f32[768,384]{1,0:T(8,128)}, f32[768,384]{1,0:T(8,128)}, f32[768,384]{1,0:T(8,128)}, f32[384,768]{1,0:T(8,128)}, f32[16,768]{1,0:T(8,128)}, /*index=...) custom-call(s32[5]{0:T(128)S(1)} %copy-done.3, bf16[384,768]{1,0:T(8,128)(2,1)S(1)} %get-tuple-element.115.a_ref, ...), custom_call_target="tpu_custom_call" | custom-call | flops 100000000 | bytes 8000000 | tf_op jit(solution)/shard_map/unpack/pallas_call | solution.py:519
  (105 shorter events, 32.6 us)
Async XLA Ops:
  3.5 35.7 %all-to-all-start.1 = ((bf16[16,40,768]{2,1,0:T(8,128)(2,1)}), bf16[16,40,768]{2,1,0:T(8,128)(2,1)S(1)}, u32[]{:S(2)}, u32[]{:S(2)}) async-start(bf16[16,40,768]{2,1,0:T(8,128)(2,1)} %bitcast.43), calls=%async_computation.1 | async-start | bytes 1966080 | tf_op jit(solution)/shard_map/all_to_all | solution.py:677
  11.6 10.9 %collective-permute-start = (bf16[192,768]{1,0:T(8,128)(2,1)}, bf16[192,768]{1,0:T(8,128)(2,1)S(1)}, u32[]{:S(2)}, u32[]{:S(2)}) collective-permute-start(bf16[192,768]{1,0:T(8,128)(2,1)} %slice_select_fusion), channel_id=1, source_target_pairs={{0,1},{1,0},{2,3},{3,2},{4,5},{5,4},{6,7},{7,6},{8,9},{9,8},{10,11... | collective-permute-start | bytes 884744 | tf_op jit(solution)/shard_map/ppermute | solution.py:673
  22.5 11.5 %copy-start.18 = (bf16[192,768]{1,0:T(8,128)(2,1)}, bf16[192,768]{1,0:T(8,128)(2,1)S(1)}, u32[]{:S(2)}) copy-start(bf16[192,768]{1,0:T(8,128)(2,1)S(1)} %collective-permute-done.w_near_ref) | copy-start | bytes 884740
  22.5 11.4 %collective-permute-start.1 = (bf16[512,384]{1,0:T(8,128)(2,1)}, bf16[512,384]{1,0:T(8,128)(2,1)S(1)}, u32[]{:S(2)}, u32[]{:S(2)}) collective-permute-start(bf16[512,384]{1,0:T(8,128)(2,1)} %get-tuple-element.71.o_ref), channel_id=1, source_target_pairs={{0,1},{1,0},{2,3},{3,2},{4,5},{5,4},{6,7},{7,6},{8,9},{9,8},{10,11... | collective-permute-start | bytes 1179656 | tf_op jit(solution)/shard_map/ppermute | solution.py:673
  23.1 1.6 collective-permute-start.2
  39.2 27.6 %copy-start.7 = (bf16[16,40,768]{2,1,0:T(8,128)(2,1)}, bf16[16,40,768]{2,1,0:T(8,128)(2,1)S(1)}, u32[]{:S(2)}) copy-start(bf16[16,40,768]{2,1,0:T(8,128)(2,1)S(1)} %all-to-all-done.1) | copy-start | bytes 2949124
  39.2 27.6 %all-to-all-start = ((bf16[16,40,768]{2,1,0:T(8,128)(2,1)}), bf16[16,40,768]{2,1,0:T(8,128)(2,1)S(1)}, u32[]{:S(2)}, u32[]{:S(2)}) async-start(bf16[16,40,768]{2,1,0:T(8,128)(2,1)} %bitcast.45), calls=%async_computation | async-start | bytes 1966080 | tf_op jit(solution)/shard_map/all_to_all | solution.py:677
  79.8 28.5 %all-to-all-start.2 = ((bf16[16,40,768]{2,1,0:T(8,128)(2,1)}), bf16[16,40,768]{2,1,0:T(8,128)(2,1)S(1)}, u32[]{:S(2)}, u32[]{:S(2)}) async-start(bf16[16,40,768]{2,1,0:T(8,128)(2,1)} %bitcast.44), calls=%async_computation.2 | async-start | bytes 1966080 | tf_op jit(solution)/shard_map/all_to_all | solution.py:677
  90.9 13.6 %collective-permute-start.3 = (bf16[640,384]{1,0:T(8,128)(2,1)S(1)}, bf16[640,384]{1,0:T(8,128)(2,1)S(1)}, u32[]{:S(2)}, u32[]{:S(2)}) collective-permute-start(bf16[640,384]{1,0:T(8,128)(2,1)S(1)} %broadcast_select_fusion), channel_id=1, source_target_pairs={{0,1},{1,0},{2,3},{3,2},{4,5},{5,4},{6,7},{7,6},{8,9},{9,8},{10,11... | collective-permute-start | bytes 1474568 | tf_op jit(solution)/shard_map/ppermute | solution.py:673
  109.2 16.2 %copy-start = (bf16[384,768]{1,0:T(8,128)(2,1)}, bf16[384,768]{1,0:T(8,128)(2,1)S(1)}, u32[]{:S(2)}) copy-start(bf16[384,768]{1,0:T(8,128)(2,1)S(1)} %get-tuple-element.85.own_ref) | copy-start | bytes 1769476
  109.3 21.0 %copy-start.2 = (bf16[128,768]{1,0:T(8,128)(2,1)}, bf16[128,768]{1,0:T(8,128)(2,1)S(1)}, u32[]{:S(2)}) copy-start(bf16[128,768]{1,0:T(8,128)(2,1)S(1)} %get-tuple-element.83.own_ref) | copy-start | bytes 589828
  109.3 16.2 %collective-permute-start.5 = (bf16[384,768]{1,0:T(8,128)(2,1)S(1)}, bf16[384,768]{1,0:T(8,128)(2,1)S(1)}, u32[]{:S(2)}, u32[]{:S(2)}) collective-permute-start(bf16[384,768]{1,0:T(8,128)(2,1)S(1)} %get-tuple-element.85.own_ref), channel_id=1, source_target_pairs={{0,1},{1,0},{2,3},{3,2},{4,5},{5,4},{6,7},{7,6},{8,9},{9,8},{10,11... | collective-permute-start | bytes 1769480 | tf_op jit(solution)/shard_map/ppermute | solution.py:673
  109.8 20.4 %collective-permute-start.4 = (bf16[128,768]{1,0:T(8,128)(2,1)S(1)}, bf16[128,768]{1,0:T(8,128)(2,1)S(1)}, u32[]{:S(2)}, u32[]{:S(2)}) collective-permute-start(bf16[128,768]{1,0:T(8,128)(2,1)S(1)} %get-tuple-element.83.own_ref), channel_id=1, source_target_pairs={{0,1},{1,0},{2,3},{3,2},{4,5},{5,4},{6,7},{7,6},{8,9},{9,8},{10,11... | collective-permute-start | bytes 589832 | tf_op jit(solution)/shard_map/ppermute | solution.py:673
  111.4 35.3 %all-to-all-start.3 = ((bf16[16,40,384]{2,1,0:T(8,128)(2,1)}), bf16[16,40,384]{2,1,0:T(8,128)(2,1)S(1)}, u32[]{:S(2)}, u32[]{:S(2)}) async-start(bf16[16,40,384]{2,1,0:T(8,128)(2,1)} %bitcast.22), calls=%async_computation.3 | async-start | bytes 983040 | tf_op jit(solution)/shard_map/all_to_all | solution.py:677
  146.6 10.9 %copy-start.8 = (bf16[512,768]{1,0:T(8,128)(2,1)S(1)}, bf16[512,768]{1,0:T(8,128)(2,1)}, u32[]{:S(2)}) copy-start(bf16[512,768]{1,0:T(8,128)(2,1)} %get-tuple-element.108.own_ref) | copy-start | bytes 2359300
  146.7 3.3 %collective-permute-start.6 = (bf16[832,768]{1,0:T(8,128)(2,1)}, bf16[832,768]{1,0:T(8,128)(2,1)S(1)}, u32[]{:S(2)}, u32[]{:S(2)}) collective-permute-start(bf16[832,768]{1,0:T(8,128)(2,1)} %get-tuple-element.104), channel_id=1, source_target_pairs={{0,2},{2,0},{4,6},{6,4},{8,10},{10,8},{12,14},{14,12},{16,18},{18,... | collective-permute-start | bytes 3833864 | tf_op jit(solution)/shard_map/ppermute | solution.py:635
  151.3 13.3 %collective-permute-start.8 = (bf16[224,768]{1,0:T(8,128)(2,1)S(1)}, bf16[224,768]{1,0:T(8,128)(2,1)S(1)}, u32[]{:S(2)}, u32[]{:S(2)}) collective-permute-start(bf16[224,768]{1,0:T(8,128)(2,1)S(1)} %get-tuple-element.129), channel_id=1, source_target_pairs={{0,8},{2,10},{4,12},{6,14},{8,0},{10,2},{12,4},{14,6},{16,24},{18,... | collective-permute-start | bytes 1032200 | tf_op jit(solution)/shard_map/ppermute | solution.py:635
  155.6 8.9 %collective-permute-start.7 = (bf16[192,768]{1,0:T(8,128)(2,1)S(1)}, bf16[192,768]{1,0:T(8,128)(2,1)S(1)}, u32[]{:S(2)}, u32[]{:S(2)}) collective-permute-start(bf16[192,768]{1,0:T(8,128)(2,1)S(1)} %get-tuple-element.130), channel_id=1, source_target_pairs={{0,4},{2,6},{4,0},{6,2},{8,12},{10,14},{12,8},{14,10},{16,20},{18,... | collective-permute-start | bytes 884744 | tf_op jit(solution)/shard_map/ppermute | solution.py:635
  157.5 19.0 %collective-permute-start.13 = (bf16[512,768]{1,0:T(8,128)(2,1)S(1)}, bf16[512,768]{1,0:T(8,128)(2,1)S(1)}, u32[]{:S(2)}, u32[]{:S(2)}) collective-permute-start(bf16[512,768]{1,0:T(8,128)(2,1)S(1)} %copy-done.8), channel_id=1, source_target_pairs={{0,1},{1,0},{2,3},{3,2},{4,5},{5,4},{6,7},{7,6},{8,9},{9,8},{10,11... | collective-permute-start | bytes 2359304 | tf_op jit(solution)/shard_map/ppermute | solution.py:673
  158.7 22.7 %copy-start.1 = (bf16[512,384]{1,0:T(8,128)(2,1)}, bf16[512,384]{1,0:T(8,128)(2,1)S(1)}, u32[]{:S(2)}) copy-start(bf16[512,384]{1,0:T(8,128)(2,1)S(1)} %pick.3.y_ref) | copy-start | bytes 1179652
  164.6 5.5 %collective-permute-start.11 = (bf16[112,768]{1,0:T(8,128)(2,1)S(1)}, bf16[112,768]{1,0:T(8,128)(2,1)S(1)}, u32[]{:S(2)}, u32[]{:S(2)}) collective-permute-start(bf16[112,768]{1,0:T(8,128)(2,1)S(1)} %add_convert_fusion.7), channel_id=1, source_target_pairs={{0,4},{2,6},{4,0},{6,2},{8,12},{10,14},{12,8},{14,10},{16,20},{18,... | collective-permute-start | bytes 516104 | tf_op jit(solution)/shard_map/ppermute | solution.py:635
  166.5 6.0 %collective-permute-start.9 = (bf16[96,768]{1,0:T(8,128)(2,1)S(1)}, bf16[96,768]{1,0:T(8,128)(2,1)S(1)}, u32[]{:S(2)}, u32[]{:S(2)}) collective-permute-start(bf16[96,768]{1,0:T(8,128)(2,1)S(1)} %add_convert_fusion.11), channel_id=1, source_target_pairs={{0,8},{2,10},{4,12},{6,14},{8,0},{10,2},{12,4},{14,6},{16,24},{18,... | collective-permute-start | bytes 442376 | tf_op jit(solution)/shard_map/ppermute | solution.py:635
  170.2 15.5 %collective-permute-start.12 = (bf16[112,768]{1,0:T(8,128)(2,1)S(1)}, bf16[112,768]{1,0:T(8,128)(2,1)S(1)}, u32[]{:S(2)}, u32[]{:S(2)}) collective-permute-start(bf16[112,768]{1,0:T(8,128)(2,1)S(1)} %add_convert_fusion.6), channel_id=1, source_target_pairs={{0,16},{2,18},{4,20},{6,22},{8,24},{10,26},{12,28},{14,30},{16,0},... | collective-permute-start | bytes 516104 | tf_op jit(solution)/shard_map/ppermute | solution.py:635
  172.6 13.1 %collective-permute-start.10 = (bf16[96,768]{1,0:T(8,128)(2,1)S(1)}, bf16[96,768]{1,0:T(8,128)(2,1)S(1)}, u32[]{:S(2)}, u32[]{:S(2)}) collective-permute-start(bf16[96,768]{1,0:T(8,128)(2,1)S(1)} %add_convert_fusion.10), channel_id=1, source_target_pairs={{0,16},{2,18},{4,20},{6,22},{8,24},{10,26},{12,28},{14,30},{16,0},... | collective-permute-start | bytes 442376 | tf_op jit(solution)/shard_map/ppermute | solution.py:635
  181.4 12.5 %collective-permute-start.19 = (bf16[512,384]{1,0:T(8,128)(2,1)S(1)}, bf16[512,384]{1,0:T(8,128)(2,1)S(1)}, u32[]{:S(2)}, u32[]{:S(2)}) collective-permute-start(bf16[512,384]{1,0:T(8,128)(2,1)S(1)} %pick.3.y_ref), channel_id=1, source_target_pairs={{0,1},{1,0},{2,3},{3,2},{4,5},{5,4},{6,7},{7,6},{8,9},{9,8},{10,11... | collective-permute-start | bytes 1179656 | tf_op jit(solution)/shard_map/ppermute | solution.py:673
  185.7 5.2 %collective-permute-start.14 = (bf16[96,768]{1,0:T(8,128)(2,1)S(1)}, bf16[96,768]{1,0:T(8,128)(2,1)S(1)}, u32[]{:S(2)}, u32[]{:S(2)}) collective-permute-start(bf16[96,768]{1,0:T(8,128)(2,1)S(1)} %add_convert_fusion.9), channel_id=1, source_target_pairs={{0,8},{2,10},{4,12},{6,14},{8,0},{10,2},{12,4},{14,6},{16,24},{18,... | collective-permute-start | bytes 442376 | tf_op jit(solution)/shard_map/ppermute | solution.py:635
  186.2 7.0 %collective-permute-start.16 = (bf16[112,768]{1,0:T(8,128)(2,1)S(1)}, bf16[112,768]{1,0:T(8,128)(2,1)S(1)}, u32[]{:S(2)}, u32[]{:S(2)}) collective-permute-start(bf16[112,768]{1,0:T(8,128)(2,1)S(1)} %add_convert_fusion.5), channel_id=1, source_target_pairs={{0,4},{2,6},{4,0},{6,2},{8,12},{10,14},{12,8},{14,10},{16,20},{18,... | collective-permute-start | bytes 516104 | tf_op jit(solution)/shard_map/ppermute | solution.py:635
  191.0 8.3 %collective-permute-start.15 = (bf16[192,768]{1,0:T(8,128)(2,1)S(1)}, bf16[192,768]{1,0:T(8,128)(2,1)S(1)}, u32[]{:S(2)}, u32[]{:S(2)}) collective-permute-start(bf16[192,768]{1,0:T(8,128)(2,1)S(1)} %pad_maximum_fusion.3), channel_id=1, source_target_pairs={{0,4},{2,6},{4,0},{6,2},{8,12},{10,14},{12,8},{14,10},{16,20},{18,... | collective-permute-start | bytes 884744 | tf_op jit(solution)/shard_map/ppermute | solution.py:635
  193.2 7.7 %collective-permute-start.17 = (bf16[192,768]{1,0:T(8,128)(2,1)S(1)}, bf16[192,768]{1,0:T(8,128)(2,1)S(1)}, u32[]{:S(2)}, u32[]{:S(2)}) collective-permute-start(bf16[192,768]{1,0:T(8,128)(2,1)S(1)} %pad_maximum_fusion.2), channel_id=1, source_target_pairs={{0,8},{2,10},{4,12},{6,14},{8,0},{10,2},{12,4},{14,6},{16,24},{18,... | collective-permute-start | bytes 884744 | tf_op jit(solution)/shard_map/ppermute | solution.py:635
  197.3 4.1 %collective-permute-start.18 = (bf16[32,768]{1,0:T(8,128)(2,1)S(1)}, bf16[32,768]{1,0:T(8,128)(2,1)S(1)}, u32[]{:S(2)}, u32[]{:S(2)}) collective-permute-start(bf16[32,768]{1,0:T(8,128)(2,1)S(1)} %slice.112.small_ref), channel_id=1, source_target_pairs={{0,1},{1,0},{2,3},{3,2},{4,5},{5,4},{6,7},{7,6},{8,9},{9,8},{10,11... | collective-permute-start | bytes 147464 | tf_op jit(solution)/shard_map/ppermute | solution.py:673
  201.4 2.0 collective-permute-start.20
  201.4 2.8 %collective-permute-start.21 = (bf16[384,768]{1,0:T(8,128)(2,1)S(1)}, bf16[384,768]{1,0:T(8,128)(2,1)S(1)}, u32[]{:S(2)}, u32[]{:S(2)}) collective-permute-start(bf16[384,768]{1,0:T(8,128)(2,1)S(1)} %get-tuple-element.116.b_ref), channel_id=1, source_target_pairs={{0,2},{2,0},{4,6},{6,4},{8,10},{10,8},{12,14},{14,12},{16,18},{18,... | collective-permute-start | bytes 1769480 | tf_op jit(solution)/shard_map/ppermute | solution.py:635
  (17 other events, 71.0 us)
